TPU v7x, 256 devices: a whole 4x4x8 slice. The times are simulated.
256 devices in a mesh: chol: 32 (over x, z_hi, y), walk: 8 (over z_lo, core).
Axes of the slice: x: 4, y: 4, z: 8 (z_hi: 2, z_lo: 4; z = z_hi * 4 + z_lo), core: 2. Of those that a mesh axis runs over, the one named last changes fastest.
Arguments:
- green: bfloat16 [32, 120, 320], P('walk'), may hold values from -6 to 6
- walkers: bfloat16 [32, 320, 120], P('walk', 'chol'), may hold values from -6 to 6
- chol_rot: bfloat16 [3840, 120, 320], P(('chol', 'walk')), may hold values from -0.0625 to 0.0625
- chol_full: bfloat16 [3840, 320, 320], P(('chol', 'walk')), may hold values from -0.0625 to 0.0625
- fields: float32 [3840, 32], P(('chol', 'walk')), may hold values from -6 to 6
- one_body_rot: bfloat16 [120, 320], replicated, may hold values from -0.03125 to 0.03125
Outputs:
- new_walkers: bfloat16 [32, 320, 120], P('walk', 'chol')
- energy: float32 [32], replicated
- log_weight: float32 [32], replicated
All inputs are finite; a program needn't handle non-finite values.
Results may differ from a plain program's by a relative error of at most 0.024.
Values may be sent and summed in bfloat16 or wider, within the bound.
No kernel may reach another device: no remote copies, remote signals or barrier semaphores. Data moves between devices by JAX's collectives and lax.ppermute only.
A program may use at most 192 MiB of HBM per device.

v0:
```python
import jax
import jax.numpy as jnp
from jax import lax
from jax.sharding import PartitionSpec as P

ORDER = 4


step_root = 0.1


def on_device(green, walkers, chol_rot, chol_full, fields, one_body_rot):
    chol_count = lax.axis_size("chol")
    group_count = lax.axis_size("walk")
    vectors_here = chol_rot.shape[0]
    electrons = chol_rot.shape[1]
    orbitals = chol_rot.shape[2]
    group_size = green.shape[0]
    row_count = orbitals // chol_count
    vector_total = vectors_here * chol_count * group_count
    rot_flat = chol_rot.reshape(vectors_here, electrons * orbitals)
    gain_flat = one_body_rot.reshape(electrons * orbitals)
    piece = lax.all_gather(green, "walk", axis=0, tiled=True)
    flat_piece = piece.reshape(piece.shape[0], electrons * orbitals)
    partial_bias = lax.dot_general(
        rot_flat, flat_piece, (((1,), (1,)), ((), ())), preferred_element_type=jnp.float32
    )
    pairs = jnp.einsum("gin,wjn->gwij", chol_rot, piece, preferred_element_type=jnp.float32)
    exchange_terms = -jnp.einsum("gwij,gwji->w", pairs, pairs)
    one_terms = 2.0 * jnp.dot(flat_piece, gain_flat, preferred_element_type=jnp.float32)
    bias = 2.0 * step_root * partial_bias
    weight_part = jnp.sum(fields * bias - 0.5 * bias * bias, axis=0) / vector_total**0.5
    energy_part = (
        jnp.sum(2.0 * partial_bias * partial_bias, axis=0) + exchange_terms
    ) / vector_total
    log_weight = lax.psum(weight_part, ("chol", "walk"))
    shifted = (fields - bias).astype(jnp.bfloat16)
    shifted_groups = shifted.reshape(vectors_here, group_count, group_size)
    chol_rows = chol_full.reshape(vectors_here, chol_count, row_count, orbitals)
    partial_field = step_root * jnp.einsum(
        "gcrq,gvk->cvkrq", chol_rows, shifted_groups, preferred_element_type=jnp.float32
    )
    partial_field = partial_field.reshape(chol_count * group_count, group_size, row_count, orbitals)
    field_rows = lax.psum_scatter(partial_field, ("chol", "walk"), scatter_dimension=0, tiled=True)[
        0
    ]
    field_half = field_rows.astype(jnp.bfloat16)
    current = walkers
    accumulated = walkers.astype(jnp.float32)
    for order in range(1, ORDER + 1):
        product = jnp.einsum(
            "wrq,wqe->wre",
            field_half,
            lax.all_gather(current, "chol", axis=1, tiled=True),
            preferred_element_type=jnp.float32,
        )
        update = product / order
        accumulated = accumulated + update
        current = update.astype(jnp.bfloat16)
    energy = one_terms + lax.psum(energy_part, ("chol", "walk"))
    return (accumulated.astype(jnp.bfloat16), energy, log_weight)


def solution(mesh):
    in_specs = (
        P("walk", None, None),
        P("walk", "chol", None),
        P(("chol", "walk"), None, None),
        P(("chol", "walk"), None, None),
        P(("chol", "walk"), None),
        P(),
    )
    out_specs = (P("walk", "chol", None), P(), P())
    return jax.shard_map(
        on_device, mesh=mesh, in_specs=in_specs, out_specs=out_specs, check_vma=False
    )
```

profile of v0, /device:TPU:8, one launch (start us, length us, event | category | flops | bytes accessed | tf_op | source)
XLA Modules:
  0.0 763.4 jit_solution(10945414160896299727)
XLA Ops:
  7.2 0.0 copy-start
  7.2 0.0 all-gather.2.cloned.1.call-start
  7.2 0.7 all-gather.2.cloned.1.call-update
  7.9 6.2 copy.44
  14.1 111.8 %all_gather.16 = bf16[4,320,120]{2,0,1:T(4,128)(2,1)S(1)} all-gather(bf16[4,10,120]{2,0,1:T(4,128)(2,1)S(1)} %copy-done.4), channel_id=1, replica_groups=mesh['chol'=32,'walk'=8] {'chol'}, dimensions={1}, use_global_device_ids=true | all-gather | bytes 316800 | tf_op jit(solution)/shard_map/all_gather | solution.py:54
  125.9 15.7 %fusion.1 = f32[32,120,15,120]{3,1,2,0:T(8,128)} fusion(bf16[32,120,320]{1,2,0:T(8,128)(2,1)} %all-gather.2.cloned.1.call-done, bf16[15,120,320]{1,2,0:T(8,128)(2,1)S(1)} %copy-done.2), kind=kOutput, calls=%fused_computation.4 | convolution fusion | flops 4423680000 | bytes 31257600 | tf_op jit(solution)/shard_map/gin,wjn->gwij/dot_general | solution.py:28
  141.6 29.5 %copy.68 = f32[32,15,120,120]{3,2,1,0:T(8,128)} copy(f32[32,15,120,120]{2,3,1,0:T(8,128)} %bitcast.40) | data formatting | bytes 55296000
  171.1 19.8 %fusion = f32[32]{0:T(128)S(1)} fusion(f32[32,15,120,120]{3,2,1,0:T(8,128)} %copy.68, f32[32,120,15,120]{3,1,2,0:T(8,128)} %fusion.1), kind=kLoop, calls=%fused_computation.1 | loop fusion | flops 13823968 | bytes 55296128 | tf_op jit(solution)/shard_map/gwij,gwji->w/dot_general | solution.py:29
  190.9 2.1 subtract_reduce_fusion
  193.0 0.1 copy.43
  193.1 9.8 %multiply_bitcast_fusion = f32[32,8,4,10,320]{4,1,3,0,2:T(8,128)} fusion(bf16[15,32,10,320,1]{3,0,2,1,4:T(8,128)(2,1)} %bitcast.42, bf16[15,8,4,1,1]{0,2,1,4,3:T(4,128)(2,1)S(1)} %bitcast.43), kind=kOutput, calls=%fused_computation.3 | convolution fusion | flops 101580800 | bytes 16180160 | tf_op jit(solution)/shard_map/gcrq,gvk->cvkrq/dot_general | solution.py:40
  202.9 13.0 %copy.125 = f32[32,8,4,10,320]{4,1,0,3,2:T(8,128)} copy(f32[32,8,4,10,320]{4,1,3,0,2:T(8,128)} %multiply_bitcast_fusion) | data formatting | bytes 26214400 | tf_op jit(solution)/shard_map/mul | solution.py:40
  216.0 19.9 %copy.47 = f32[256,4,10,320]{3,1,2,0:T(4,128)} copy(f32[256,4,10,320]{3,0,2,1:T(8,128)} %bitcast.41) | data formatting | bytes 26214400 | tf_op jit(solution)/shard_map/reshape | solution.py:43
  235.9 185.3 %all-reduce.3 = (bf16[256,4,10,320]{3,1,2,0:T(4,128)(2,1)}, f32[32]{0:T(128)S(1)}, f32[32]{0:T(128)}) all-reduce(f32[256,4,10,320]{3,1,2,0:T(4,128)} %copy.47, f32[32]{0:T(128)S(1)} %get-tuple-element.27, f32[32]{0:T(128)S(1)} %get-tuple-element.28), channel_id=2, replica_groups=mesh['chol'=32,'walk'=8] {'chol','walk'}, use_global_device_ids=true, to_apply=%region_0.0.clone | all-reduce | flops 3276864 | bytes 19661312
  421.2 0.8 fusion.35
  422.0 0.2 fusion.39
  422.2 110.1 %all_gather.17 = bf16[4,320,120]{2,0,1:T(4,128)(2,1)S(1)} all-gather(bf16[4,10,120]{2,0,1:T(4,128)(2,1)S(1)} %copy.50), channel_id=1, replica_groups=mesh['chol'=32,'walk'=8] {'chol'}, dimensions={1}, use_global_device_ids=true | all-gather | bytes 316800 | tf_op jit(solution)/shard_map/all_gather | solution.py:54
  532.2 0.2 fusion.40
  532.4 112.9 %all_gather.18 = bf16[4,320,120]{2,0,1:T(4,128)(2,1)S(1)} all-gather(bf16[4,10,120]{2,0,1:T(4,128)(2,1)S(1)} %copy.53), channel_id=1, replica_groups=mesh['chol'=32,'walk'=8] {'chol'}, dimensions={1}, use_global_device_ids=true | all-gather | bytes 316800 | tf_op jit(solution)/shard_map/all_gather | solution.py:54
  645.3 0.2 fusion.41
  645.4 108.3 %all_gather.19 = bf16[4,320,120]{2,0,1:T(4,128)(2,1)S(1)} all-gather(bf16[4,10,120]{2,0,1:T(4,128)(2,1)S(1)} %copy.56), channel_id=1, replica_groups=mesh['chol'=32,'walk'=8] {'chol'}, dimensions={1}, use_global_device_ids=true | all-gather | bytes 316800 | tf_op jit(solution)/shard_map/all_gather | solution.py:54
  753.7 0.2 fusion.10
  753.9 0.6 copy.59
  754.5 2.0 fusion.22
  (16 shorter events, 0.1 us)
Async XLA Ops:
  7.2 747.4 %copy-start = (bf16[120,320]{0,1:T(8,128)(2,1)S(1)}, bf16[120,320]{0,1:T(8,128)(2,1)}, u32[]{:S(2)}) copy-start(bf16[120,320]{0,1:T(8,128)(2,1)} %param.11) | copy-start | bytes 230404
  7.2 118.7 %all-gather.2.cloned.1.call-start = ((), (), s32[]{:S(2)}) async-start(), calls=%async_computation | async-start | bytes 2949120 | tf_op jit(solution)/shard_map/all_gather | solution.py:23
  7.9 6.2 copy-start.4
  7.9 118.0 %copy-start.2 = (bf16[15,120,320]{1,2,0:T(8,128)(2,1)S(1)}, bf16[15,120,320]{1,2,0:T(8,128)(2,1)}, u32[]{:S(2)}) copy-start(bf16[15,120,320]{1,2,0:T(8,128)(2,1)} %param.8) | copy-start | bytes 3456004
  171.1 19.8 %copy-start.1 = (bf16[32,120,320]{1,2,0:T(8,128)(2,1)S(1)}, bf16[32,120,320]{1,2,0:T(8,128)(2,1)}, u32[]{:S(2)}) copy-start(bf16[32,120,320]{1,2,0:T(8,128)(2,1)} %all-gather.2.cloned.1.call-done) | copy-start | bytes 7372804
  171.1 19.8 %copy-start.3 = (bf16[15,120,320]{1,2,0:T(8,128)(2,1)S(1)}, bf16[15,120,320]{1,2,0:T(8,128)(2,1)}, u32[]{:S(2)}) copy-start(bf16[15,120,320]{1,2,0:T(8,128)(2,1)} %param.8) | copy-start | bytes 3456004
  171.1 19.8 %copy-start.5 = (f32[15,32]{1,0:T(8,128)S(1)}, f32[15,32]{1,0:T(8,128)}, u32[]{:S(2)}) copy-start(f32[15,32]{1,0:T(8,128)} %param.10) | copy-start | bytes 5764
Sparse Core Ops, SparseCore 0:
  9.8 43.6 all-gather.1
where the time goes:
time: 765 us; the launch traced here: 763 us
  blocking collectives  628 us (82%)
  local copies, waits for them, and re-layouts  70.1 us (9%)
  matrix products  30.3 us (4%)
  other arithmetic  19.8 us (3%)
  between operations  14.1 us (2%)
    all_gather x4, blocking collectives, on_device(): lax.all_gather(current, 'chol', axis=1, tiled=True)  443 us
    unnamed x1, blocking collectives  185 us
    unnamed x15, local copies, waits for them, and re-layouts  36.3 us
    reshape x1, local copies, waits for them, and re-layouts, on_device(): partial_field.reshape(chol_count * group_count, group_size, row_count, or...  19.9 us
    dot_general x1, other arithmetic, on_device(): exchange_terms = -jnp.einsum('gwij,gwji->w', pairs, pairs)  19.8 us
    dot_general x1, matrix products, on_device(): jnp.einsum('gin,wjn->gwij', chol_rot, piece, preferred_element_type=jnp.f...  15.7 us
  transfers between devices with their start and end apart: 1, of which 0 were waited for; matrix products, arithmetic and copies ran while one was open for 1% of the time, Pallas kernels for 0%

commit v1 on v0

v1 whole, which is shorter than its diff:
```python
import functools

import jax
import jax.numpy as jnp
from jax import lax
from jax.experimental import pallas as pl
from jax.experimental.pallas import tpu as pltpu
from jax.sharding import Mesh, PartitionSpec as P

ORDER = 4
step_root = 0.1

AXES = ("x", "zh", "y", "zl", "core")
SIZES = (4, 2, 4, 4, 2)
Z = ("zh", "zl")
HIGH = ("x", "zh", "y")
LOW = ("zl", "core")

ROW = 128
WIDE = 384
TILE = 16
f32 = jnp.float32
bf16 = jnp.bfloat16
CONTRACT_LAST = (((1,), (1,)), ((), ()))


def ring(count, shift):
    return [(i, (i + shift) % count) for i in range(count)]


def parts_of(value):
    high = value.astype(bf16).astype(f32)
    rest = value - high
    middle = rest.astype(bf16).astype(f32)
    low = (rest - middle).astype(bf16).astype(f32)
    row = lax.broadcasted_iota(jnp.int32, (TILE, value.shape[1]), 0)
    zero = jnp.zeros((TILE, value.shape[1]), f32)
    return jnp.where(
        row == 0, high, jnp.where(row == 1, middle, jnp.where(row == 2, low, zero))
    )


def pair_kernel(vectors, *refs):
    rot_ref, greens, (trace_ref, square_ref) = refs[0], refs[1:-2], refs[-2:]
    orbitals = rot_ref.shape[2]
    eye = (
        lax.broadcasted_iota(jnp.int32, (ROW, ROW), 0)
        == lax.broadcasted_iota(jnp.int32, (ROW, ROW), 1)
    ).astype(f32)
    base = 0
    for green_ref in greens:
        count = green_ref.shape[0] // 2

        def two_walkers(i, carry, green_ref=green_ref, base=base):
            green = green_ref[pl.ds(2 * i, 2)].reshape(2 * ROW, orbitals)
            rot = rot_ref[...].reshape(vectors * ROW, orbitals)
            pairs = lax.dot_general(rot, green, CONTRACT_LAST, preferred_element_type=f32)
            for w in range(2):
                total = jnp.zeros((8, ROW), f32)
                for g in range(vectors):
                    block = pairs[g * ROW : (g + 1) * ROW, w * ROW : (w + 1) * ROW]
                    total = total + jnp.sum((block * block.T).reshape(ROW // 8, 8, ROW), axis=0)
                    trace_ref[base + 2 * i + w, pl.ds(g, 1), :] = jnp.sum(
                        block * eye, axis=0, keepdims=True
                    )
                square_ref[base + 2 * i + w] = total
            return carry

        if count == 1:
            two_walkers(0, 0)
        else:
            lax.fori_loop(0, count, two_walkers, 0)
        base += 2 * count


def pair_sums(rot, greens):
    vectors = rot.shape[0]
    walkers = sum(g.shape[0] for g in greens)
    return pl.pallas_call(
        functools.partial(pair_kernel, vectors),
        out_shape=(
            jax.ShapeDtypeStruct((walkers, vectors, ROW), f32),
            jax.ShapeDtypeStruct((walkers, 8, ROW), f32),
        ),
        compiler_params=pltpu.CompilerParams(vmem_limit_bytes=40 * 2**20),
        cost_estimate=pl.CostEstimate(
            flops=4 * walkers * vectors * ROW * ROW * 512, bytes_accessed=3 * 2**20, transcendentals=0
        ),
        name="pairs",
    )(rot, *greens)


def field_kernel(vectors, order_ref, message_ref, *refs):
    blocks, out_ref = refs[:-1], refs[-1]
    rows, orbitals = blocks[0].shape[1:]
    depth = vectors * TILE
    spread = (
        lax.broadcasted_iota(jnp.int32, (ROW, depth), 0)
        == lax.shift_right_logical(lax.broadcasted_iota(jnp.int32, (ROW, depth), 1), 4)
    ).astype(bf16)
    same = (
        jnp.bitwise_and(lax.broadcasted_iota(jnp.int32, (TILE * TILE, depth), 0), TILE - 1)
        == jnp.bitwise_and(lax.broadcasted_iota(jnp.int32, (TILE * TILE, depth), 1), TILE - 1)
    )
    weights = []
    for b in range(len(blocks)):
        shifted = message_ref[order_ref[b], 0:TILE, :].astype(bf16)
        wide = jnp.dot(shifted, spread, preferred_element_type=f32)
        wide = jnp.broadcast_to(wide[:, None, :], (TILE, TILE, depth)).reshape(TILE * TILE, depth)
        weights.append(jnp.where(same, wide, 0.0).astype(bf16))
    out_ref[:, :, :, 256:WIDE] = jnp.zeros((4, 4, rows, WIDE - 256), bf16)
    for t in range(rows // TILE):
        total = jnp.zeros((TILE * TILE, orbitals), f32)
        for b, block_ref in enumerate(blocks):
            block = block_ref[:, t * TILE : (t + 1) * TILE, :].reshape(depth, orbitals)
            total = total + jnp.dot(weights[b], block, preferred_element_type=f32)
        total = (step_root * total).astype(bf16).reshape(TILE, TILE, orbitals)
        for w in range(TILE):
            out_ref[w % 4, w // 4, t * TILE : (t + 1) * TILE, 0:orbitals] = total[w]
    scalars = message_ref[0, TILE : TILE + 1, :]
    for s in range(1, len(blocks)):
        scalars = scalars + message_ref[s, TILE : TILE + 1, :]
    scalars = parts_of(scalars).astype(bf16)
    upper = lax.broadcasted_iota(jnp.int32, (TILE, 128), 1) >= 64
    for w in range(4):
        held = out_ref[w, 0, 0:TILE, 256:WIDE]
        out_ref[w, 0, 0:TILE, 256:WIDE] = jnp.where(upper, scalars, held)


def field_rows(order, message, blocks):
    vectors, rows, orbitals = blocks[0].shape
    return pl.pallas_call(
        functools.partial(field_kernel, vectors),
        out_shape=jax.ShapeDtypeStruct((4, 4, rows, WIDE), bf16),
        in_specs=[pl.BlockSpec(memory_space=pltpu.SMEM)]
        + [pl.BlockSpec(memory_space=pltpu.VMEM)] * (1 + len(blocks)),
        compiler_params=pltpu.CompilerParams(vmem_limit_bytes=40 * 2**20),
        cost_estimate=pl.CostEstimate(
            flops=2 * 256 * 256 * 384 * 40, bytes_accessed=5 * 2**20, transcendentals=0
        ),
        name="field_rows",
    )(order, message, *blocks)


def sum_kernel(copies, in_ref, out_ref):
    upper = lax.broadcasted_iota(jnp.int32, (TILE, 128), 1) >= 64
    sources, groups = in_ref.shape[:2]
    for g in range(groups):
        total = in_ref[0, g].astype(f32)
        for s in range(1, sources):
            total = total + in_ref[s, g].astype(f32)
        if g == 0:
            first = total[0:TILE, 256:WIDE]
            scalars = parts_of(jnp.sum(first, axis=0, keepdims=True))
        rounded = total.astype(bf16)
        corner = jnp.where(upper, scalars, total[0:TILE, 256:WIDE]).astype(bf16)
        for k in range(g, copies, groups):
            out_ref[k] = rounded
            out_ref[k, 0:TILE, 256:WIDE] = corner


def sum_over_y(received):
    _, _, rows, wide = received.shape
    return pl.pallas_call(
        functools.partial(sum_kernel, 8),
        out_shape=jax.ShapeDtypeStruct((8, rows, wide), bf16),
        compiler_params=pltpu.CompilerParams(vmem_limit_bytes=24 * 2**20),
        name="sum_y",
    )(received)


def last_kernel(in_ref, walker_ref, out_ref, scalars_ref):
    total = in_ref[0].astype(f32)
    for s in range(1, in_ref.shape[0]):
        total = total + in_ref[s].astype(f32)
    rounded = total.astype(bf16)
    scalars_ref[...] = jnp.sum(total[0:TILE, 256:WIDE], axis=0, keepdims=True)
    for k in range(4):
        out_ref[k, :, 0:WIDE] = rounded
        out_ref[k, :, WIDE : WIDE + 128] = walker_ref[...]


def sum_over_z(received, walker_rows):
    _, rows, wide = received.shape
    return pl.pallas_call(
        last_kernel,
        out_shape=(
            jax.ShapeDtypeStruct((4, rows, wide + 128), bf16),
            jax.ShapeDtypeStruct((1, 128), f32),
        ),
        compiler_params=pltpu.CompilerParams(vmem_limit_bytes=24 * 2**20),
        name="sum_z",
    )(received, walker_rows)


def taylor_kernel(orbitals, in_ref, out_ref):
    whole = in_ref[...].reshape(orbitals, in_ref.shape[2])
    field = whole[:, 0:orbitals]
    current = whole[:, WIDE : WIDE + 128]
    total = current.astype(f32)
    for order in range(1, ORDER + 1):
        update = jnp.dot(field, current, preferred_element_type=f32) / order
        total = total + update
        current = update.astype(bf16)
    out_ref[...] = total.astype(bf16)


def taylor(gathered):
    orbitals = gathered.shape[0] * gathered.shape[1]
    return pl.pallas_call(
        functools.partial(taylor_kernel, orbitals),
        out_shape=jax.ShapeDtypeStruct((orbitals, 128), bf16),
        compiler_params=pltpu.CompilerParams(vmem_limit_bytes=24 * 2**20),
        name="taylor",
    )(gathered)


def by_source(relative, index):
    turned = jnp.concatenate([relative[0:1], relative[3:4], relative[2:3], relative[1:2]])
    twice = jnp.concatenate([turned, turned])
    return lax.dynamic_slice_in_dim(twice, lax.rem(4 - index, 4), 4, axis=0)


def on_device(green, walkers, chol_rot, chol_full, fields, one_body_rot):
    x, zh, y, zl, core = (lax.axis_index(a) for a in AXES)
    vectors, electrons, orbitals = chol_rot.shape
    vector_total = vectors * 256
    rows = orbitals // 4
    group = green.shape[0]

    def swap(a):
        return lax.ppermute(a, "core", ring(2, 1))

    padded = jnp.pad(green, ((0, 0), (0, ROW - electrons), (0, 0)))
    rot = jnp.pad(chol_rot, ((0, 0), (0, ROW - electrons), (0, 0)))
    before = lax.ppermute(padded, Z, ring(8, 1))
    after = lax.ppermute(padded, Z, ring(8, -1))
    far_a = lax.ppermute(padded[:2], Z, ring(8, 2))
    far_b = lax.ppermute(padded[2:], Z, ring(8, -2))

    def rows_of(position):
        return lax.dynamic_slice_in_dim(chol_full, lax.rem(position, 4) * rows, rows, axis=1)

    mine = [rows_of(x)]
    for k in (1, 2, 3):
        mine.append(lax.ppermute(rows_of(x + k), "x", ring(4, k)))
    blocks, order = [], []
    for k in range(4):
        source = 2 * lax.rem(x + 4 - k, 4)
        blocks += [mine[k], swap(mine[k])]
        order += [source + core, source + 1 - core]

    held = [lax.dynamic_slice_in_dim(walkers, y, 1, axis=0)]
    for k in (1, 2, 3):
        piece = lax.dynamic_slice_in_dim(walkers, lax.rem(y + k, 4), 1, axis=0)
        held.append(lax.ppermute(piece, "y", ring(4, k)))
    held = by_source(jnp.concatenate(held), y).reshape(rows // 2, electrons)
    other = lax.ppermute(held, "zh", ring(2, 1))
    walker_rows = jnp.where(
        zh == 0, jnp.concatenate([held, other]), jnp.concatenate([other, held])
    )
    walker_rows = jnp.pad(walker_rows, ((0, 0), (0, 128 - electrons)))

    shards = [
        [padded, swap(padded)],
        [before, swap(before)],
        [far_a, far_b, swap(far_a), swap(far_b)],
        [after, swap(after)],
    ]
    sums = [pair_sums(rot, shards[d]) for d in (0, 1, 3, 2)]
    sums = [sums[0], sums[1], sums[3], sums[2]]
    traces = jnp.stack([jnp.sum(s[0], axis=-1) for s in sums]).reshape(4, 2, group, vectors)
    squares = jnp.stack([jnp.sum(s[1], axis=(1, 2)) for s in sums]).reshape(4, 2, group)
    single = 2.0 * jnp.sum(green.astype(f32) * one_body_rot.astype(f32), axis=(1, 2))
    squares = squares.at[0, 0].add(single * (-vector_total / 32.0))

    def by_group(a):
        a = jnp.where(core == 0, a, a[:, ::-1])
        return by_source(a, zl)

    intersection = by_group(traces).reshape(8 * group, vectors)
    exchange = by_group(squares).reshape(8 * group)
    bias = 2.0 * step_root * intersection
    noise = fields.T
    weight_part = jnp.sum(noise * bias - 0.5 * bias * bias, axis=1) / vector_total**0.5
    energy_part = (
        jnp.sum(2.0 * intersection * intersection, axis=1) - exchange
    ) / vector_total
    shifted = (noise - bias).astype(bf16).astype(f32)
    shifted = shifted.reshape(4, 2, group, vectors).transpose(1, 0, 2, 3).reshape(2, 4 * group, vectors)
    scalars = jnp.concatenate([energy_part, weight_part])
    message = jnp.concatenate(
        [
            jnp.pad(shifted, ((0, 0), (0, 0), (0, 128 - vectors))),
            jnp.broadcast_to(jnp.pad(scalars, (64, 0))[None, None], (2, 1, 128)),
            jnp.zeros((2, 7, 128), f32),
        ],
        axis=1,
    )
    message = jnp.broadcast_to(message[None], (4, 2, 24, 128)).reshape(8, 24, 128)
    message = lax.all_to_all(message, ("x", "core"), 0, 0)

    field = field_rows(jnp.stack(order).astype(jnp.int32), message, blocks)
    field = lax.all_to_all(field, "y", 0, 0)
    field = sum_over_y(field)
    field = lax.all_to_all(field, Z, 0, 0)
    field, scalars = sum_over_z(field, walker_rows)
    field = lax.all_to_all(field, "x", 0, 0)
    whole = taylor(field)[:, :electrons]
    new = lax.dynamic_slice_in_dim(whole, rows * x + (rows // 2) * zh, rows // 2, axis=0)
    new = lax.all_to_all(new.reshape(4, rows // 8, electrons), "y", 0, 0)
    return new, scalars[0, 64:96], scalars[0, 96:128]


def solution(mesh):
    split = Mesh(mesh.devices.reshape(SIZES), AXES)
    in_specs = (
        P(LOW, None, None),
        P(LOW, HIGH, None),
        P(HIGH + LOW, None, None),
        P(HIGH + LOW, None, None),
        P(HIGH + LOW, None),
        P(),
    )
    out_specs = (P(LOW, HIGH, None), P(), P())
    return jax.shard_map(
        on_device, mesh=split, in_specs=in_specs, out_specs=out_specs, check_vma=False
    )
```

time: 765 us -> 156 us (0.20)
  blocking collectives: 628 us -> 17.5 us
  local copies, waits for them, and re-layouts: 70.1 us -> 13.5 us
  starting transfers between devices: 0.04 us -> 47.4 us
  waiting for transfers between devices: 0.68 us -> 48 us
  matrix products: 30.3 us -> 0 us
  Pallas kernels: 0 us -> 25.1 us
  other arithmetic: 19.8 us -> 1.55 us
  between operations: 14.1 us -> 0.99 us
    all_gather x4 -> x0, blocking collectives: 443 us -> none  [on_device(): lax.all_gather(current, 'chol', axis=1, tiled=True)]
    unnamed x1 -> x0, blocking collectives: 185 us -> none
    unnamed x15 -> x28, local copies, waits for them, and re-layouts: 36.3 us -> 3.83 us
    ppermute x0 -> x20, waiting for transfers between devices: none -> 32 us  [the longest x3 23.8 us: on_device(): mine.append(lax.ppermute(rows_of(x + k), 'x', ring(4, k)))]
    dot_general x8 -> x0, matrix products: 30.3 us -> none  [the longest x1 15.7 us: on_device(): jnp.einsum('gin,wjn->gwij', chol_rot, piece, preferred_element_type=jnp.f...]
    ppermute x0 -> x20, starting transfers between devices: none -> 27.8 us  [the longest x1 6.01 us: on_device(): other = lax.ppermute(held, 'zh', ring(2, 1))]
    pallas_call x0 -> x8, Pallas kernels: none -> 25.1 us  [the longest x4 17.2 us: pair_sums(): pl.pallas_call(functools.partial(pair_kernel, vectors), out_shape=(jax.Sh...]
    dot_general x1 -> x0, other arithmetic: 19.8 us -> none  [on_device(): exchange_terms = -jnp.einsum('gwij,gwji->w', pairs, pairs)]
  transfers between devices with their start and end apart: 1 -> 24, of which waited for: 0 -> 8; matrix products, arithmetic and copies ran while one was open for 1% -> 8% of each run, Pallas kernels for 0% -> 11%
where the time goes in v1:
time: 156 us; the launch traced here: 154 us
  waiting for transfers between devices  48 us (31%)
  starting transfers between devices  47.4 us (30%)
  Pallas kernels  25.1 us (16%)
  blocking collectives  17.5 us (11%)
  local copies, waits for them, and re-layouts  13.5 us (9%)
    ppermute x3, waiting for transfers between devices, on_device(): mine.append(lax.ppermute(rows_of(x + k), 'x', ring(4, k)))  23.8 us
    all_to_all x1, blocking collectives, on_device(): field = lax.all_to_all(field, 'y', 0, 0)  17.5 us
    pallas_call x4, Pallas kernels, pair_sums(): pl.pallas_call(functools.partial(pair_kernel, vectors), out_shape=(jax.Sh...  17.2 us
    all_to_all x1, starting transfers between devices, on_device(): field = lax.all_to_all(field, Z, 0, 0)  7.39 us
    all_to_all x1, waiting for transfers between devices, on_device(): field = lax.all_to_all(field, 'x', 0, 0)  6.99 us
    ppermute x1, starting transfers between devices, on_device(): other = lax.ppermute(held, 'zh', ring(2, 1))  6.01 us
    ppermute x3, starting transfers between devices, on_device(): mine.append(lax.ppermute(rows_of(x + k), 'x', ring(4, k)))  5.74 us
    all_to_all x1, waiting for transfers between devices, on_device(): message = lax.all_to_all(message, ('x', 'core'), 0, 0)  5.71 us
  transfers between devices with their start and end apart: 24, of which 8 were waited for; matrix products, arithmetic and copies ran while one was open for 8% of the time, Pallas kernels for 11%

profile of v1, /device:TPU:8, one launch (start us, length us, event | category | flops | bytes accessed | tf_op | source)
XLA Modules:
  0.0 154.0 jit_solution(14277455431191005906)
XLA Ops:
  4.6 3.9 %collective-permute-start.7 = (bf16[4,128,320]{2,1,0:T(8,128)(2,1)}, bf16[4,128,320]{2,1,0:T(8,128)(2,1)}, u32[]{:S(2)}, u32[]{:S(2)}) collective-permute-start(bf16[4,128,320]{2,1,0:T(8,128)(2,1)} %pad.27.refs_1_), channel_id=1, source_target_pairs={{0,38},{2,0},{4,2},{6,4},{32,6},{34,32},{36,34},{38,36},{1,39},{3,... | collective-permute-start | bytes 983048 | tf_op jit(solution)/shard_map/ppermute | solution.py:237
  9.2 4.1 %collective-permute-start.4 = (bf16[2,128,320]{2,1,0:T(8,128)(2,1)S(1)}, bf16[2,128,320]{2,1,0:T(8,128)(2,1)}, u32[]{:S(2)}, u32[]{:S(2)}) collective-permute-start(bf16[2,128,320]{2,1,0:T(8,128)(2,1)S(1)} %get-tuple-element.42), channel_id=1, source_target_pairs={{0,36},{2,38},{4,0},{6,2},{32,4},{34,6},{36,32},{38,34},{1,37},{3,... | collective-permute-start | bytes 491528 | tf_op jit(solution)/shard_map/ppermute | solution.py:239
  13.4 3.8 %constant_dynamic-slice_fusion.6 = (bf16[15,80,320]{2,1,0:T(8,128)(2,1)}, bf16[15,80,320]{2,1,0:T(8,128)(2,1)}, bf16[15,80,320]{2,1,0:T(8,128)(2,1)S(1)}, bf16[15,80,320]{2,1,0:T(8,128)(2,1)}) fusion(bf16[15,320,320]{2,1,0:T(8,128)(2,1)} %param.11, s32[]{:T(128)S(6)} %select_n.66, s32[]{:T(128)S(6)} %select_n.64, s32[]{:T(128)S(6)} %select_n.63, s32[]{:T(128)S(6)} %select_n.65), kind=kLoop, calls=%fused_computation.40 | loop fusion | bytes 6144016 | tf_op jit(solution)/shard_map/dynamic_slice | solution.py:242
  21.0 3.2 %collective-permute-done.3.refs_1_ = bf16[2,128,320]{2,1,0:T(8,128)(2,1)} collective-permute-done((bf16[2,128,320]{2,1,0:T(8,128)(2,1)}, bf16[2,128,320]{2,1,0:T(8,128)(2,1)}, u32[]{:S(2)}, u32[]{:S(2)}) %collective-permute-start.3) | collective-permute-done | bytes 163872 | tf_op jit(solution)/shard_map/ppermute | solution.py:238
  26.2 4.4 %pairs.4 = (f32[8,15,128]{2,1,0:T(8,128)S(1)}, f32[8,8,128]{2,1,0:T(8,128)S(1)}) custom-call(bf16[15,128,320]{2,1,0:T(8,128)(2,1)S(1)} %pad.26.refs_0_, bf16[4,128,320]{2,1,0:T(8,128)(2,1)} %pad.27.refs_1_, bf16[4,128,320]{2,1,0:T(8,128)(2,1)} %collective-permute-done.refs_2_), custom_call_target="tpu_custom_call" | custom-call | flops 4026531840 | bytes 3145728 | tf_op jit(solution)/shard_map/pairs/pallas_call | solution.py:79
  30.7 2.9 %collective-permute-start.12 = (bf16[15,80,320]{2,1,0:T(8,128)(2,1)}, bf16[15,80,320]{2,1,0:T(8,128)(2,1)}, u32[]{:S(2)}, u32[]{:S(2)}) collective-permute-start(bf16[15,80,320]{2,1,0:T(8,128)(2,1)} %get-tuple-element.41), channel_id=1, source_target_pairs={{0,128},{64,192},{128,0},{192,64},{1,129},{65,193},{129,1},{193,65... | collective-permute-start | bytes 2304008 | tf_op jit(solution)/shard_map/ppermute | solution.py:246
  34.9 4.0 %pairs.6 = (f32[8,15,128]{2,1,0:T(8,128)S(1)}, f32[8,8,128]{2,1,0:T(8,128)S(1)}) custom-call(bf16[15,128,320]{2,1,0:T(8,128)(2,1)S(1)} %pad.26.refs_0_, bf16[2,128,320]{2,1,0:T(8,128)(2,1)} %collective-permute-done.3.refs_1_, bf16[2,128,320]{2,1,0:T(8,128)(2,1)} %collective-permute-done.4.refs_2_, bf16[2,128,320]{2,1,0:T(8,128)(2,1)S(1)} %collective-permute-done.5.refs_3_, ...), custom_call_target="tpu_custom_call" | custom-call | flops 4026531840 | bytes 3145728 | tf_op jit(solution)/shard_map/pairs/pallas_call | solution.py:79
  40.3 4.4 %pairs.5 = (f32[8,15,128]{2,1,0:T(8,128)S(1)}, f32[8,8,128]{2,1,0:T(8,128)S(1)}) custom-call(bf16[15,128,320]{2,1,0:T(8,128)(2,1)S(1)} %pad.26.refs_0_, bf16[4,128,320]{2,1,0:T(8,128)(2,1)} %collective-permute-done.1.refs_1_, bf16[4,128,320]{2,1,0:T(8,128)(2,1)} %collective-permute-done.2.refs_2_), custom_call_target="tpu_custom_call" | custom-call | flops 4026531840 | bytes 3145728 | tf_op jit(solution)/shard_map/pairs/pallas_call | solution.py:79
  45.0 4.4 %pairs.7 = (f32[8,15,128]{2,1,0:T(8,128)S(1)}, f32[8,8,128]{2,1,0:T(8,128)S(1)}) custom-call(bf16[15,128,320]{2,1,0:T(8,128)(2,1)S(1)} %pad.26.refs_0_, bf16[4,128,320]{2,1,0:T(8,128)(2,1)} %collective-permute-done.7.refs_1_, bf16[4,128,320]{2,1,0:T(8,128)(2,1)} %collective-permute-done.8.refs_2_), custom_call_target="tpu_custom_call" | custom-call | flops 4026531840 | bytes 3145728 | tf_op jit(solution)/shard_map/pairs/pallas_call | solution.py:79
  50.8 16.9 %collective-permute-done.12.refs_4_ = bf16[15,80,320]{2,1,0:T(8,128)(2,1)} collective-permute-done((bf16[15,80,320]{2,1,0:T(8,128)(2,1)}, bf16[15,80,320]{2,1,0:T(8,128)(2,1)}, u32[]{:S(2)}, u32[]{:S(2)}) %collective-permute-start.12) | collective-permute-done | bytes 768032 | tf_op jit(solution)/shard_map/ppermute | solution.py:246
  67.7 6.9 %collective-permute-done.14.refs_6_ = bf16[15,80,320]{2,1,0:T(8,128)(2,1)} collective-permute-done((bf16[15,80,320]{2,1,0:T(8,128)(2,1)}, bf16[15,80,320]{2,1,0:T(8,128)(2,1)}, u32[]{:S(2)}, u32[]{:S(2)}) %collective-permute-start.14) | collective-permute-done | bytes 768032 | tf_op jit(solution)/shard_map/ppermute | solution.py:246
  75.5 4.0 %all-to-all-start = ((f32[8,24,128]{2,1,0:T(8,128)}), f32[8,24,128]{2,1,0:T(8,128)S(1)}, u32[]{:S(2)}, u32[]{:S(2)}) async-start(f32[8,24,128]{2,1,0:T(8,128)} %bitcast.19), calls=%async_computation | async-start | bytes 196608 | tf_op jit(solution)/shard_map/all_to_all | solution.py:301
  79.6 5.7 %all-to-all-done.message_ref = f32[8,24,128]{2,1,0:T(8,128)S(1)} async-done(((f32[8,24,128]{2,1,0:T(8,128)}), f32[8,24,128]{2,1,0:T(8,128)S(1)}, u32[]{:S(2)}, u32[]{:S(2)}) %all-to-all-start) | async-done | bytes 98336 | tf_op jit(solution)/shard_map/all_to_all | solution.py:301
  85.3 5.4 %field_rows.1 = bf16[4,4,80,384]{3,2,1,0:T(8,128)(2,1)S(1)} custom-call(s32[8]{0:T(128)S(1)} %stack.65.order_ref, f32[8,24,128]{2,1,0:T(8,128)S(1)} %all-to-all-done.message_ref, bf16[15,80,320]{2,1,0:T(8,128)(2,1)S(1)} %get-tuple-element.40.refs_0_, bf16[15,80,320]{2,1,0:T(8,128)(2,1)} %collective-permute-done.9.refs_1_, ...), custom_call_target="tpu_custom_call" | custom-call | flops 2013265920 | bytes 5242880 | tf_op jit(solution)/shard_map/field_rows/pallas_call | solution.py:132
  90.7 17.5 %all_to_all.25.in_ref = bf16[4,4,80,384]{3,2,1,0:T(8,128)(2,1)S(1)} all-to-all(bf16[4,4,80,384]{3,2,1,0:T(8,128)(2,1)S(1)} %field_rows.1), channel_id=1, replica_groups=mesh['x'=4,'zh'=2,'y'=4,'zl'=4,'core'=2] {'y'}, dimensions={0} | all-to-all | bytes 1966080 | tf_op jit(solution)/shard_map/all_to_all | solution.py:304
  109.1 7.4 %all-to-all-start.2 = ((bf16[8,80,384]{2,1,0:T(8,128)(2,1)}), bf16[8,80,384]{2,1,0:T(8,128)(2,1)S(1)}, u32[]{:S(2)}, u32[]{:S(2)}) async-start(bf16[8,80,384]{2,1,0:T(8,128)(2,1)} %sum_y.1), calls=%async_computation.2 | async-start | bytes 983040 | tf_op jit(solution)/shard_map/all_to_all | solution.py:306
  118.7 2.2 %collective-permute-start.18 = (bf16[1,10,120]{2,0,1:T(2,128)(2,1)S(1)}, bf16[1,10,120]{2,0,1:T(2,128)(2,1)S(1)}, u32[]{:S(2)}, u32[]{:S(2)}) collective-permute-start(bf16[1,10,120]{2,0,1:T(2,128)(2,1)S(1)} %get-tuple-element.49), channel_id=1, source_target_pairs={{0,8},{8,16},{16,24},{24,0},{1,9},{9,17},{17,25},{25,1},{2,10},{10... | collective-permute-start | bytes 7208 | tf_op jit(solution)/shard_map/ppermute | solution.py:256
  120.9 2.5 %collective-permute-done.17 = bf16[1,10,120]{2,0,1:T(2,128)(2,1)S(1)} collective-permute-done((bf16[1,10,120]{2,0,1:T(2,128)(2,1)S(1)}, bf16[1,10,120]{2,0,1:T(2,128)(2,1)S(1)}, u32[]{:S(2)}, u32[]{:S(2)}) %collective-permute-start.17) | collective-permute-done | bytes 2432 | tf_op jit(solution)/shard_map/ppermute | solution.py:256
  123.6 6.0 %collective-permute-start.19 = (bf16[40,120]{1,0:T(8,128)(2,1)S(1)}, bf16[40,120]{1,0:T(8,128)(2,1)S(1)}, u32[]{:S(2)}, u32[]{:S(2)}) collective-permute-start(bf16[40,120]{1,0:T(8,128)(2,1)S(1)} %reshape.96), channel_id=1, source_target_pairs={{0,32},{32,0},{1,33},{33,1},{2,34},{34,2},{3,35},{35,3},{4,36},{36... | collective-permute-start | bytes 28808 | tf_op jit(solution)/shard_map/ppermute | solution.py:258
  129.6 2.5 %collective-permute-done.19 = bf16[40,120]{1,0:T(8,128)(2,1)S(1)} collective-permute-done((bf16[40,120]{1,0:T(8,128)(2,1)S(1)}, bf16[40,120]{1,0:T(8,128)(2,1)S(1)}, u32[]{:S(2)}, u32[]{:S(2)}) %collective-permute-start.19) | collective-permute-done | bytes 9632 | tf_op jit(solution)/shard_map/ppermute | solution.py:258
  132.9 3.5 %all-to-all-start.3 = ((bf16[4,80,512]{2,1,0:T(8,128)(2,1)}), bf16[4,80,512]{2,1,0:T(8,128)(2,1)S(1)}, u32[]{:S(2)}, u32[]{:S(2)}) async-start(bf16[4,80,512]{2,1,0:T(8,128)(2,1)} %get-tuple-element.33), calls=%async_computation.3 | async-start | bytes 655360 | tf_op jit(solution)/shard_map/all_to_all | solution.py:308
  136.4 7.0 %all-to-all-done.3.in_ref = bf16[4,80,512]{2,1,0:T(8,128)(2,1)S(1)} async-done(((bf16[4,80,512]{2,1,0:T(8,128)(2,1)}), bf16[4,80,512]{2,1,0:T(8,128)(2,1)S(1)}, u32[]{:S(2)}, u32[]{:S(2)}) %all-to-all-start.3) | async-done | bytes 327712 | tf_op jit(solution)/shard_map/all_to_all | solution.py:308
  144.8 4.7 %all-to-all-start.4 = ((bf16[4,10,120]{2,1,0:T(8,128)(2,1)}), bf16[4,10,120]{2,1,0:T(8,128)(2,1)S(1)}, u32[]{:S(2)}, u32[]{:S(2)}) async-start(bf16[4,10,120]{2,1,0:T(8,128)(2,1)} %reshape.97), calls=%async_computation.4 | async-start | bytes 32768 | tf_op jit(solution)/shard_map/all_to_all | solution.py:311
  150.1 3.3 %all-to-all-done.4 = bf16[4,10,120]{2,1,0:T(8,128)(2,1)S(1)} async-done(((bf16[4,10,120]{2,1,0:T(8,128)(2,1)}), bf16[4,10,120]{2,1,0:T(8,128)(2,1)S(1)}, u32[]{:S(2)}, u32[]{:S(2)}) %all-to-all-start.4) | async-done | bytes 9632 | tf_op jit(solution)/shard_map/all_to_all | solution.py:311
  (112 shorter events, 22.4 us)
Async XLA Ops:
  2.6 32.3 %collective-permute-start.1 = (bf16[4,128,320]{2,1,0:T(8,128)(2,1)}, bf16[4,128,320]{2,1,0:T(8,128)(2,1)}, u32[]{:S(2)}, u32[]{:S(2)}) collective-permute-start(bf16[4,128,320]{2,1,0:T(8,128)(2,1)} %pad.27.refs_1_), channel_id=1, source_target_pairs={{0,2},{2,4},{4,6},{6,32},{32,34},{34,36},{36,38},{38,0},{1,3},{3,5... | collective-permute-start | bytes 983048 | tf_op jit(solution)/shard_map/ppermute | solution.py:236
  4.6 35.0 %collective-permute-start.7 = (bf16[4,128,320]{2,1,0:T(8,128)(2,1)}, bf16[4,128,320]{2,1,0:T(8,128)(2,1)}, u32[]{:S(2)}, u32[]{:S(2)}) collective-permute-start(bf16[4,128,320]{2,1,0:T(8,128)(2,1)} %pad.27.refs_1_), channel_id=1, source_target_pairs={{0,38},{2,0},{4,2},{6,4},{32,6},{34,32},{36,34},{38,36},{1,39},{3,... | collective-permute-start | bytes 983048 | tf_op jit(solution)/shard_map/ppermute | solution.py:237
  8.5 17.2 %collective-permute-start = (bf16[4,128,320]{2,1,0:T(8,128)(2,1)}, bf16[4,128,320]{2,1,0:T(8,128)(2,1)}, u32[]{:S(2)}, u32[]{:S(2)}) collective-permute-start(bf16[4,128,320]{2,1,0:T(8,128)(2,1)} %pad.27.refs_1_), channel_id=1, source_target_pairs={{0,1},{1,0},{2,3},{3,2},{4,5},{5,4},{6,7},{7,6},{8,9},{9,8},{10,11... | collective-permute-start | bytes 983048 | tf_op jit(solution)/shard_map/ppermute | solution.py:232
  9.2 15.0 %collective-permute-start.3 = (bf16[2,128,320]{2,1,0:T(8,128)(2,1)}, bf16[2,128,320]{2,1,0:T(8,128)(2,1)}, u32[]{:S(2)}, u32[]{:S(2)}) collective-permute-start(bf16[2,128,320]{2,1,0:T(8,128)(2,1)} %get-tuple-element.43), channel_id=1, source_target_pairs={{0,4},{2,6},{4,32},{6,34},{32,36},{34,38},{36,0},{38,2},{1,5},{3,7... | collective-permute-start | bytes 491528 | tf_op jit(solution)/shard_map/ppermute | solution.py:238
  9.2 16.5 %collective-permute-start.4 = (bf16[2,128,320]{2,1,0:T(8,128)(2,1)S(1)}, bf16[2,128,320]{2,1,0:T(8,128)(2,1)}, u32[]{:S(2)}, u32[]{:S(2)}) collective-permute-start(bf16[2,128,320]{2,1,0:T(8,128)(2,1)S(1)} %get-tuple-element.42), channel_id=1, source_target_pairs={{0,36},{2,38},{4,0},{6,2},{32,4},{34,6},{36,32},{38,34},{1,37},{3,... | collective-permute-start | bytes 491528 | tf_op jit(solution)/shard_map/ppermute | solution.py:239
  24.2 26.1 %collective-permute-start.10 = (bf16[15,80,320]{2,1,0:T(8,128)(2,1)}, bf16[15,80,320]{2,1,0:T(8,128)(2,1)S(1)}, u32[]{:S(2)}, u32[]{:S(2)}) collective-permute-start(bf16[15,80,320]{2,1,0:T(8,128)(2,1)} %get-tuple-element.39), channel_id=1, source_target_pairs={{0,64},{64,128},{128,192},{192,0},{1,65},{65,129},{129,193},{193,1... | collective-permute-start | bytes 2304008 | tf_op jit(solution)/shard_map/ppermute | solution.py:246
  25.7 4.9 %collective-permute-start.5 = (bf16[2,128,320]{2,1,0:T(8,128)(2,1)}, bf16[2,128,320]{2,1,0:T(8,128)(2,1)S(1)}, u32[]{:S(2)}, u32[]{:S(2)}) collective-permute-start(bf16[2,128,320]{2,1,0:T(8,128)(2,1)} %collective-permute-done.3.refs_1_), channel_id=1, source_target_pairs={{0,1},{1,0},{2,3},{3,2},{4,5},{5,4},{6,7},{7,6},{8,9},{9,8},{10,11... | collective-permute-start | bytes 491528 | tf_op jit(solution)/shard_map/ppermute | solution.py:232
  25.7 7.8 %collective-permute-start.6 = (bf16[2,128,320]{2,1,0:T(8,128)(2,1)}, bf16[2,128,320]{2,1,0:T(8,128)(2,1)S(1)}, u32[]{:S(2)}, u32[]{:S(2)}) collective-permute-start(bf16[2,128,320]{2,1,0:T(8,128)(2,1)} %collective-permute-done.4.refs_2_), channel_id=1, source_target_pairs={{0,1},{1,0},{2,3},{3,2},{4,5},{5,4},{6,7},{7,6},{8,9},{9,8},{10,11... | collective-permute-start | bytes 491528 | tf_op jit(solution)/shard_map/ppermute | solution.py:232
  30.7 37.1 %collective-permute-start.12 = (bf16[15,80,320]{2,1,0:T(8,128)(2,1)}, bf16[15,80,320]{2,1,0:T(8,128)(2,1)}, u32[]{:S(2)}, u32[]{:S(2)}) collective-permute-start(bf16[15,80,320]{2,1,0:T(8,128)(2,1)} %get-tuple-element.41), channel_id=1, source_target_pairs={{0,128},{64,192},{128,0},{192,64},{1,129},{65,193},{129,1},{193,65... | collective-permute-start | bytes 2304008 | tf_op jit(solution)/shard_map/ppermute | solution.py:246
  33.6 41.0 %collective-permute-start.14 = (bf16[15,80,320]{2,1,0:T(8,128)(2,1)}, bf16[15,80,320]{2,1,0:T(8,128)(2,1)}, u32[]{:S(2)}, u32[]{:S(2)}) collective-permute-start(bf16[15,80,320]{2,1,0:T(8,128)(2,1)} %get-tuple-element.38), channel_id=1, source_target_pairs={{0,192},{64,0},{128,64},{192,128},{1,193},{65,1},{129,65},{193,129... | collective-permute-start | bytes 2304008 | tf_op jit(solution)/shard_map/ppermute | solution.py:246
  34.9 5.3 %collective-permute-start.2 = (bf16[4,128,320]{2,1,0:T(8,128)(2,1)}, bf16[4,128,320]{2,1,0:T(8,128)(2,1)}, u32[]{:S(2)}, u32[]{:S(2)}) collective-permute-start(bf16[4,128,320]{2,1,0:T(8,128)(2,1)} %collective-permute-done.1.refs_1_), channel_id=1, source_target_pairs={{0,1},{1,0},{2,3},{3,2},{4,5},{5,4},{6,7},{7,6},{8,9},{9,8},{10,11... | collective-permute-start | bytes 983048 | tf_op jit(solution)/shard_map/ppermute | solution.py:232
  39.6 45.7 %collective-permute-start.9 = (bf16[15,80,320]{2,1,0:T(8,128)(2,1)S(1)}, bf16[15,80,320]{2,1,0:T(8,128)(2,1)}, u32[]{:S(2)}, u32[]{:S(2)}) collective-permute-start(bf16[15,80,320]{2,1,0:T(8,128)(2,1)S(1)} %get-tuple-element.40.refs_0_), channel_id=1, source_target_pairs={{0,1},{1,0},{2,3},{3,2},{4,5},{5,4},{6,7},{7,6},{8,9},{9,8},{10,11... | collective-permute-start | bytes 2304008 | tf_op jit(solution)/shard_map/ppermute | solution.py:232
  40.2 4.8 %collective-permute-start.8 = (bf16[4,128,320]{2,1,0:T(8,128)(2,1)}, bf16[4,128,320]{2,1,0:T(8,128)(2,1)}, u32[]{:S(2)}, u32[]{:S(2)}) collective-permute-start(bf16[4,128,320]{2,1,0:T(8,128)(2,1)} %collective-permute-done.7.refs_1_), channel_id=1, source_target_pairs={{0,1},{1,0},{2,3},{3,2},{4,5},{5,4},{6,7},{7,6},{8,9},{9,8},{10,11... | collective-permute-start | bytes 983048 | tf_op jit(solution)/shard_map/ppermute | solution.py:232
  50.3 35.0 %collective-permute-start.11 = (bf16[15,80,320]{2,1,0:T(8,128)(2,1)S(1)}, bf16[15,80,320]{2,1,0:T(8,128)(2,1)S(1)}, u32[]{:S(2)}, u32[]{:S(2)}) collective-permute-start(bf16[15,80,320]{2,1,0:T(8,128)(2,1)S(1)} %collective-permute-done.10.refs_2_), channel_id=1, source_target_pairs={{0,1},{1,0},{2,3},{3,2},{4,5},{5,4},{6,7},{7,6},{8,9},{9,8},{10,11... | collective-permute-start | bytes 2304008 | tf_op jit(solution)/shard_map/ppermute | solution.py:232
  67.7 17.6 %collective-permute-start.13 = (bf16[15,80,320]{2,1,0:T(8,128)(2,1)}, bf16[15,80,320]{2,1,0:T(8,128)(2,1)}, u32[]{:S(2)}, u32[]{:S(2)}) collective-permute-start(bf16[15,80,320]{2,1,0:T(8,128)(2,1)} %collective-permute-done.12.refs_4_), channel_id=1, source_target_pairs={{0,1},{1,0},{2,3},{3,2},{4,5},{5,4},{6,7},{7,6},{8,9},{9,8},{10,11... | collective-permute-start | bytes 2304008 | tf_op jit(solution)/shard_map/ppermute | solution.py:232
  74.6 10.8 %collective-permute-start.15 = (bf16[15,80,320]{2,1,0:T(8,128)(2,1)}, bf16[15,80,320]{2,1,0:T(8,128)(2,1)}, u32[]{:S(2)}, u32[]{:S(2)}) collective-permute-start(bf16[15,80,320]{2,1,0:T(8,128)(2,1)} %collective-permute-done.14.refs_6_), channel_id=1, source_target_pairs={{0,1},{1,0},{2,3},{3,2},{4,5},{5,4},{6,7},{7,6},{8,9},{9,8},{10,11... | collective-permute-start | bytes 2304008 | tf_op jit(solution)/shard_map/ppermute | solution.py:232
  75.5 9.8 %all-to-all-start = ((f32[8,24,128]{2,1,0:T(8,128)}), f32[8,24,128]{2,1,0:T(8,128)S(1)}, u32[]{:S(2)}, u32[]{:S(2)}) async-start(f32[8,24,128]{2,1,0:T(8,128)} %bitcast.19), calls=%async_computation | async-start | bytes 196608 | tf_op jit(solution)/shard_map/all_to_all | solution.py:301
  109.1 23.0 %all-to-all-start.2 = ((bf16[8,80,384]{2,1,0:T(8,128)(2,1)}), bf16[8,80,384]{2,1,0:T(8,128)(2,1)S(1)}, u32[]{:S(2)}, u32[]{:S(2)}) async-start(bf16[8,80,384]{2,1,0:T(8,128)(2,1)} %sum_y.1), calls=%async_computation.2 | async-start | bytes 983040 | tf_op jit(solution)/shard_map/all_to_all | solution.py:306
  116.5 4.4 %collective-permute-start.16 = (bf16[1,10,120]{2,0,1:T(2,128)(2,1)S(1)}, bf16[1,10,120]{2,0,1:T(2,128)(2,1)S(1)}, u32[]{:S(2)}, u32[]{:S(2)}) collective-permute-start(bf16[1,10,120]{2,0,1:T(2,128)(2,1)S(1)} %get-tuple-element.50), channel_id=1, source_target_pairs={{0,24},{8,0},{16,8},{24,16},{1,25},{9,1},{17,9},{25,17},{2,26},{10... | collective-permute-start | bytes 7208 | tf_op jit(solution)/shard_map/ppermute | solution.py:256
  118.3 5.1 %collective-permute-start.17 = (bf16[1,10,120]{2,0,1:T(2,128)(2,1)S(1)}, bf16[1,10,120]{2,0,1:T(2,128)(2,1)S(1)}, u32[]{:S(2)}, u32[]{:S(2)}) collective-permute-start(bf16[1,10,120]{2,0,1:T(2,128)(2,1)S(1)} %get-tuple-element.52), channel_id=1, source_target_pairs={{0,16},{8,24},{16,0},{24,8},{1,17},{9,25},{17,1},{25,9},{2,18},{10... | collective-permute-start | bytes 7208 | tf_op jit(solution)/shard_map/ppermute | solution.py:256
  118.7 4.7 %collective-permute-start.18 = (bf16[1,10,120]{2,0,1:T(2,128)(2,1)S(1)}, bf16[1,10,120]{2,0,1:T(2,128)(2,1)S(1)}, u32[]{:S(2)}, u32[]{:S(2)}) collective-permute-start(bf16[1,10,120]{2,0,1:T(2,128)(2,1)S(1)} %get-tuple-element.49), channel_id=1, source_target_pairs={{0,8},{8,16},{16,24},{24,0},{1,9},{9,17},{17,25},{25,1},{2,10},{10... | collective-permute-start | bytes 7208 | tf_op jit(solution)/shard_map/ppermute | solution.py:256
  123.6 8.5 %collective-permute-start.19 = (bf16[40,120]{1,0:T(8,128)(2,1)S(1)}, bf16[40,120]{1,0:T(8,128)(2,1)S(1)}, u32[]{:S(2)}, u32[]{:S(2)}) collective-permute-start(bf16[40,120]{1,0:T(8,128)(2,1)S(1)} %reshape.96), channel_id=1, source_target_pairs={{0,32},{32,0},{1,33},{33,1},{2,34},{34,2},{3,35},{35,3},{4,36},{36... | collective-permute-start | bytes 28808 | tf_op jit(solution)/shard_map/ppermute | solution.py:258
  132.9 10.5 %all-to-all-start.3 = ((bf16[4,80,512]{2,1,0:T(8,128)(2,1)}), bf16[4,80,512]{2,1,0:T(8,128)(2,1)S(1)}, u32[]{:S(2)}, u32[]{:S(2)}) async-start(bf16[4,80,512]{2,1,0:T(8,128)(2,1)} %get-tuple-element.33), calls=%async_computation.3 | async-start | bytes 655360 | tf_op jit(solution)/shard_map/all_to_all | solution.py:308
  144.8 8.6 %all-to-all-start.4 = ((bf16[4,10,120]{2,1,0:T(8,128)(2,1)}), bf16[4,10,120]{2,1,0:T(8,128)(2,1)S(1)}, u32[]{:S(2)}, u32[]{:S(2)}) async-start(bf16[4,10,120]{2,1,0:T(8,128)(2,1)} %reshape.97), calls=%async_computation.4 | async-start | bytes 32768 | tf_op jit(solution)/shard_map/all_to_all | solution.py:311
  (5 other events, 17.3 us)

commit v2 on v1

v2 whole, which is shorter than its diff:
```python
import functools

import jax
import jax.numpy as jnp
from jax import lax
from jax.experimental import pallas as pl
from jax.experimental.pallas import tpu as pltpu
from jax.sharding import Mesh, PartitionSpec as P

ORDER = 4
step_root = 0.1

AXES = ("x", "zh", "y", "zl", "core")
SIZES = (4, 2, 4, 4, 2)
Z = ("zh", "zl")
HIGH = ("x", "zh", "y")
LOW = ("zl", "core")

ROW = 128
WIDE = 384
TILE = 16
f32 = jnp.float32
bf16 = jnp.bfloat16
CONTRACT_LAST = (((1,), (1,)), ((), ()))


def ring(count, shift):
    return [(i, (i + shift) % count) for i in range(count)]


def parts_of(value):
    high = value.astype(bf16).astype(f32)
    rest = value - high
    middle = rest.astype(bf16).astype(f32)
    low = (rest - middle).astype(bf16).astype(f32)
    row = lax.broadcasted_iota(jnp.int32, (TILE, value.shape[1]), 0)
    zero = jnp.zeros((TILE, value.shape[1]), f32)
    return jnp.where(
        row == 0, high, jnp.where(row == 1, middle, jnp.where(row == 2, low, zero))
    )


def pair_kernel(vectors, turned, walkers, *refs):
    rot_ref, greens = refs[0], refs[1 : 1 + walkers]
    trace_ref, square_ref = refs[1 + walkers : 3 + walkers]
    if not turned:
        raw_ref, rot_ref = rot_ref, refs[3 + walkers]
        for g in range(vectors):
            rot_ref[g] = widen(raw_ref[g]).T
    orbitals = rot_ref.shape[2]
    eye = (
        lax.broadcasted_iota(jnp.int32, (ROW, ROW), 0)
        == lax.broadcasted_iota(jnp.int32, (ROW, ROW), 1)
    ).astype(f32)
    base = 0
    for green_ref in greens:
        count = green_ref.shape[0] // 2

        def two_walkers(i, carry, green_ref=green_ref, base=base):
            green = jnp.concatenate([widen(green_ref[2 * i]), widen(green_ref[2 * i + 1])], axis=1)
            rot = rot_ref[...].reshape(vectors * ROW, orbitals)
            pairs = jnp.dot(rot, green, preferred_element_type=f32)
            for w in range(2):
                total = jnp.zeros((8, ROW), f32)
                for g in range(vectors):
                    block = pairs[g * ROW : (g + 1) * ROW, w * ROW : (w + 1) * ROW]
                    total = total + jnp.sum((block * block.T).reshape(ROW // 8, 8, ROW), axis=0)
                    trace_ref[base + 2 * i + w, pl.ds(g, 1), :] = jnp.sum(
                        block * eye, axis=0, keepdims=True
                    )
                square_ref[base + 2 * i + w] = total
            return carry

        if count == 1:
            two_walkers(0, 0)
        else:
            lax.fori_loop(0, count, two_walkers, 0)
        base += 2 * count


def widen(a):
    return jnp.concatenate([a, jnp.zeros((a.shape[0], ROW - a.shape[1]), a.dtype)], axis=1)


def pair_sums(rot, greens, turned):
    vectors = rot.shape[0]
    walkers = sum(g.shape[0] for g in greens)
    out_shape = [
        jax.ShapeDtypeStruct((walkers, vectors, ROW), f32),
        jax.ShapeDtypeStruct((walkers, 8, ROW), f32),
    ]
    if not turned:
        out_shape.append(jax.ShapeDtypeStruct((vectors, ROW, rot.shape[1]), bf16))
    return pl.pallas_call(
        functools.partial(pair_kernel, vectors, turned, len(greens)),
        out_shape=out_shape,
        compiler_params=pltpu.CompilerParams(vmem_limit_bytes=40 * 2**20),
        cost_estimate=pl.CostEstimate(
            flops=4 * walkers * vectors * ROW * ROW * 512, bytes_accessed=3 * 2**20, transcendentals=0
        ),
        name="pairs",
    )(rot, *greens)


def field_kernel(vectors, carries, order_ref, message_ref, *refs):
    blocks, out_ref = refs[:-1], refs[-1]
    rows, orbitals = blocks[0].shape[1:]
    depth = vectors * TILE
    spread = (
        lax.broadcasted_iota(jnp.int32, (ROW, depth), 0)
        == lax.shift_right_logical(lax.broadcasted_iota(jnp.int32, (ROW, depth), 1), 4)
    ).astype(bf16)
    same = (
        jnp.bitwise_and(lax.broadcasted_iota(jnp.int32, (TILE * TILE, depth), 0), TILE - 1)
        == jnp.bitwise_and(lax.broadcasted_iota(jnp.int32, (TILE * TILE, depth), 1), TILE - 1)
    )
    weights = []
    for b in range(len(blocks)):
        shifted = message_ref[order_ref[b], 0:TILE, :].astype(bf16)
        wide = jnp.dot(shifted, spread, preferred_element_type=f32)
        wide = jnp.broadcast_to(wide[:, None, :], (TILE, TILE, depth)).reshape(TILE * TILE, depth)
        weights.append(jnp.where(same, wide, 0.0).astype(bf16))
    out_ref[:, :, :, 256:WIDE] = jnp.zeros((4, 4, rows, WIDE - 256), bf16)
    for t in range(rows // TILE):
        total = jnp.zeros((TILE * TILE, orbitals), f32)
        for b, block_ref in enumerate(blocks):
            block = block_ref[:, t * TILE : (t + 1) * TILE, :].reshape(depth, orbitals)
            total = total + jnp.dot(weights[b], block, preferred_element_type=f32)
        total = (step_root * total).astype(bf16).reshape(TILE, TILE, orbitals)
        for w in range(TILE):
            out_ref[w % 4, w // 4, t * TILE : (t + 1) * TILE, 0:orbitals] = total[w]
    if not carries:
        return
    scalars = message_ref[0, TILE : TILE + 1, :]
    for s in range(1, len(blocks)):
        scalars = scalars + message_ref[s, TILE : TILE + 1, :]
    scalars = parts_of(scalars).astype(bf16)
    upper = lax.broadcasted_iota(jnp.int32, (TILE, 128), 1) >= 64
    for w in range(4):
        held = out_ref[w, 0, 0:TILE, 256:WIDE]
        out_ref[w, 0, 0:TILE, 256:WIDE] = jnp.where(upper, scalars, held)


def field_rows(order, message, blocks, carries):
    vectors, rows, orbitals = blocks[0].shape
    return pl.pallas_call(
        functools.partial(field_kernel, vectors, carries),
        out_shape=jax.ShapeDtypeStruct((4, 4, rows, WIDE), bf16),
        in_specs=[pl.BlockSpec(memory_space=pltpu.SMEM)]
        + [pl.BlockSpec(memory_space=pltpu.VMEM)] * (1 + len(blocks)),
        compiler_params=pltpu.CompilerParams(vmem_limit_bytes=40 * 2**20),
        cost_estimate=pl.CostEstimate(
            flops=rows * 256 * 384 * 256, bytes_accessed=rows * 60000, transcendentals=0
        ),
        name="field_rows",
    )(order, message, *blocks)


def sum_kernel(copies, first_ref, second_ref, out_ref):
    upper = lax.broadcasted_iota(jnp.int32, (TILE, 128), 1) >= 64
    sources, groups, rows = first_ref.shape[:3]
    for g in range(groups):
        total = first_ref[0, g].astype(f32)
        below = second_ref[0, g].astype(f32)
        for s in range(1, sources):
            total = total + first_ref[s, g].astype(f32)
            below = below + second_ref[s, g].astype(f32)
        if g == 0:
            scalars = parts_of(jnp.sum(total[0:TILE, 256:WIDE], axis=0, keepdims=True))
        corner = jnp.where(upper, scalars, total[0:TILE, 256:WIDE]).astype(bf16)
        total, below = total.astype(bf16), below.astype(bf16)
        for k in range(g, copies, groups):
            out_ref[k, 0:rows] = total
            out_ref[k, rows:] = below
            out_ref[k, 0:TILE, 256:WIDE] = corner


def sum_second_axis(first, second):
    rows, wide = first.shape[2] + second.shape[2], first.shape[3]
    return pl.pallas_call(
        functools.partial(sum_kernel, 8),
        out_shape=jax.ShapeDtypeStruct((8, rows, wide), bf16),
        compiler_params=pltpu.CompilerParams(vmem_limit_bytes=24 * 2**20),
        name="sum_plane",
    )(first, second)


def last_kernel(in_ref, out_ref, scalars_ref):
    total = in_ref[0].astype(f32)
    for s in range(1, in_ref.shape[0]):
        total = total + in_ref[s].astype(f32)
    rounded = total.astype(bf16)
    scalars_ref[...] = jnp.sum(total[0:TILE, 256:WIDE], axis=0, keepdims=True)
    for k in range(out_ref.shape[0]):
        out_ref[k] = rounded


def sum_over_z(received):
    _, rows, wide = received.shape
    return pl.pallas_call(
        last_kernel,
        out_shape=(
            jax.ShapeDtypeStruct((16, rows, wide), bf16),
            jax.ShapeDtypeStruct((1, 128), f32),
        ),
        compiler_params=pltpu.CompilerParams(vmem_limit_bytes=24 * 2**20),
        name="sum_z",
    )(received)


def taylor_kernel(first_rows, in_ref, walkers_ref, out_ref):
    orbitals = walkers_ref.shape[1]
    for w in range(4):
        field = jnp.concatenate(
            [in_ref[4 * k + w, 0:first_rows] for k in range(4)]
            + [in_ref[4 * w + k, first_rows:] for k in range(4)]
        )[:, 0:orbitals]
        current = walkers_ref[w]
        total = current.astype(f32)
        for order in range(1, ORDER + 1):
            update = jnp.dot(field, current, preferred_element_type=f32) / order
            total = total + update
            current = update.astype(bf16)
        out_ref[w] = total.astype(bf16)


def taylor(gathered, walkers, first_rows):
    return pl.pallas_call(
        functools.partial(taylor_kernel, first_rows),
        out_shape=jax.ShapeDtypeStruct(walkers.shape, bf16),
        compiler_params=pltpu.CompilerParams(vmem_limit_bytes=24 * 2**20),
        name="taylor",
    )(gathered, walkers)


def by_source(relative, index):
    turned = jnp.concatenate([relative[0:1], relative[3:4], relative[2:3], relative[1:2]])
    twice = jnp.concatenate([turned, turned])
    return lax.dynamic_slice_in_dim(twice, lax.rem(4 - index, 4), 4, axis=0)


def on_device(green, walkers, chol_rot, chol_full, fields, one_body_rot):
    x, zh, y, zl, core = (lax.axis_index(a) for a in AXES)
    vectors, electrons, orbitals = chol_rot.shape
    vector_total = vectors * 256
    group = green.shape[0]
    tiles = orbitals // TILE
    first_rows = TILE * ((tiles // 4 + 1) // 2)
    second_rows = orbitals // 4 - first_rows

    def swap(a):
        return lax.ppermute(a, "core", ring(2, 1))

    turned = green.swapaxes(1, 2)
    before = lax.ppermute(turned, Z, ring(8, 1))
    after = lax.ppermute(turned, Z, ring(8, -1))
    far_a = lax.ppermute(turned[:2], Z, ring(8, 2))
    far_b = lax.ppermute(turned[2:], Z, ring(8, -2))

    def rows_of_vectors(axis, position, start, rows):
        def rows_of(k):
            first = start + lax.rem(position + k, 4) * rows
            return lax.dynamic_slice_in_dim(chol_full, first, rows, axis=1)

        mine = [rows_of(0)]
        for k in (1, 2, 3):
            mine.append(lax.ppermute(rows_of(k), axis, ring(4, k)))
        blocks, order = [], []
        for k in range(4):
            source = 2 * lax.rem(position + 4 - k, 4)
            blocks += [mine[k], swap(mine[k])]
            order += [source + core, source + 1 - core]
        return blocks, jnp.stack(order).astype(jnp.int32)

    first_blocks, first_order = rows_of_vectors("x", x, 0, first_rows)
    second_blocks, second_order = rows_of_vectors("y", y, 4 * first_rows, second_rows)

    whole = jnp.broadcast_to(walkers[None], (32,) + walkers.shape)
    whole = lax.all_to_all(whole, HIGH, 0, 0)
    whole = whole.transpose(1, 0, 2, 3).reshape(group, orbitals, electrons)

    shards = [
        [turned, swap(turned)],
        [before, swap(before)],
        [far_a, far_b, swap(far_a), swap(far_b)],
        [after, swap(after)],
    ]
    own = pair_sums(chol_rot.swapaxes(1, 2), shards[0], False)
    sums = [own] + [pair_sums(own[2], shards[d], True) for d in (1, 2, 3)]
    traces = jnp.stack([jnp.sum(s[0], axis=-1) for s in sums]).reshape(4, 2, group, vectors)
    squares = jnp.stack([jnp.sum(s[1], axis=(1, 2)) for s in sums]).reshape(4, 2, group)
    single = 2.0 * jnp.sum(green.astype(f32) * one_body_rot.astype(f32), axis=(1, 2))
    squares = squares.at[0, 0].add(single * (-vector_total / 32.0))

    def by_group(a):
        a = jnp.where(core == 0, a, a[:, ::-1])
        return by_source(a, zl)

    intersection = by_group(traces).reshape(8 * group, vectors)
    exchange = by_group(squares).reshape(8 * group)
    bias = 2.0 * step_root * intersection
    noise = fields.T
    weight_part = jnp.sum(noise * bias - 0.5 * bias * bias, axis=1) / vector_total**0.5
    energy_part = (
        jnp.sum(2.0 * intersection * intersection, axis=1) - exchange
    ) / vector_total
    shifted = (noise - bias).astype(bf16).astype(f32)
    shifted = shifted.reshape(4, 2, group, vectors).transpose(1, 0, 2, 3).reshape(2, 4 * group, vectors)
    scalars = jnp.concatenate([energy_part, weight_part])
    message = jnp.concatenate(
        [
            jnp.pad(shifted, ((0, 0), (0, 0), (0, 128 - vectors))),
            jnp.broadcast_to(jnp.pad(scalars, (64, 0))[None, None], (2, 1, 128)),
            jnp.zeros((2, 7, 128), f32),
        ],
        axis=1,
    )
    message = jnp.broadcast_to(message[None], (4, 2, 24, 128)).reshape(8, 24, 128)
    first = lax.all_to_all(message, ("x", "core"), 0, 0)
    second = lax.all_to_all(message, ("y", "core"), 0, 0)

    first = field_rows(first_order, first, first_blocks, True)
    first = lax.all_to_all(first, "y", 0, 0)
    second = field_rows(second_order, second, second_blocks, False)
    second = lax.all_to_all(second, "x", 0, 0)
    field = sum_second_axis(first, second)
    field = lax.all_to_all(field, Z, 0, 0)
    field, scalars = sum_over_z(field)
    field = lax.all_to_all(field, ("x", "y"), 0, 0)
    new = taylor(field, whole, first_rows)
    share = orbitals // 32
    new = lax.dynamic_slice_in_dim(new, share * (8 * x + 4 * zh + y), share, axis=1)
    return new, scalars[0, 64:96], scalars[0, 96:128]


def solution(mesh):
    split = Mesh(mesh.devices.reshape(SIZES), AXES)
    in_specs = (
        P(LOW, None, None),
        P(LOW, HIGH, None),
        P(HIGH + LOW, None, None),
        P(HIGH + LOW, None, None),
        P(HIGH + LOW, None),
        P(),
    )
    out_specs = (P(LOW, HIGH, None), P(), P())
    return jax.shard_map(
        on_device, mesh=split, in_specs=in_specs, out_specs=out_specs, check_vma=False
    )
```

time: 156 us -> 181 us (1.16)
  blocking collectives: 17.5 us -> 39.5 us
  waiting for transfers between devices: 48 us -> 56.8 us
  starting transfers between devices: 47.4 us -> 40.8 us
  Pallas kernels: 25.1 us -> 27.6 us
    all_to_all x1 -> x3, blocking collectives: 17.5 us -> 39.5 us  [the longest x1 19.1 us: on_device(): field = lax.all_to_all(field, Z, 0, 0)]
    all_to_all x4, waiting for transfers between devices: 16 us -> 29.1 us  [the longest x1 12 us: on_device(): whole = lax.all_to_all(whole, HIGH, 0, 0)]
    ppermute x11 -> x10, starting transfers between devices: 26.1 us -> 21 us  [the longest x6 10.9 us: rows_of_vectors(): mine.append(lax.ppermute(rows_of(k), axis, ring(4, k)))]
    ppermute x11 -> x10, waiting for transfers between devices: 31.9 us -> 27.6 us  [the longest x6 22.2 us: rows_of_vectors(): mine.append(lax.ppermute(rows_of(k), axis, ring(4, k)))]
    pallas_call x8 -> x9, Pallas kernels: 25.1 us -> 27.6 us  [the longest x4 16.5 us: pair_sums(): pl.pallas_call(functools.partial(pair_kernel, vectors, turned, len(greens...]
    pad x3 -> x0, local copies, waits for them, and re-layouts: 2.44 us -> none  [the longest x1 1.61 us: on_device(): rot = jnp.pad(chol_rot, ((0, 0), (0, ROW - electrons), (0, 0)))]
    all_to_all x4, starting transfers between devices: 19.6 us -> 17.5 us  [the longest x1 4.98 us: on_device(): whole = lax.all_to_all(whole, HIGH, 0, 0)]
    dynamic_slice x5 -> x3, local copies, waits for them, and re-layouts: 3.86 us -> 5.34 us  [the longest x2 5.32 us: rows_of(): return lax.dynamic_slice_in_dim(chol_full, first, rows, axis=1)]
  transfers between devices with their start and end apart: 24 -> 27, of which waited for: 8 -> 8; matrix products, arithmetic and copies ran while one was open for 8% -> 6% of each run, Pallas kernels for 11% -> 14%
where the time goes in v2:
time: 181 us; the launch traced here: 180 us
  waiting for transfers between devices  56.8 us (31%)
  starting transfers between devices  40.8 us (23%)
  blocking collectives  39.5 us (22%)
  Pallas kernels  27.6 us (15%)
  local copies, waits for them, and re-layouts  12.8 us (7%)
    ppermute x6, waiting for transfers between devices, rows_of_vectors(): mine.append(lax.ppermute(rows_of(k), axis, ring(4, k)))  22.2 us
    all_to_all x1, blocking collectives, on_device(): field = lax.all_to_all(field, Z, 0, 0)  19.1 us
    pallas_call x4, Pallas kernels, pair_sums(): pl.pallas_call(functools.partial(pair_kernel, vectors, turned, len(greens...  16.5 us
    all_to_all x1, waiting for transfers between devices, on_device(): whole = lax.all_to_all(whole, HIGH, 0, 0)  12 us
    all_to_all x1, blocking collectives, on_device(): first = lax.all_to_all(first, 'y', 0, 0)  11.5 us
    ppermute x6, starting transfers between devices, rows_of_vectors(): mine.append(lax.ppermute(rows_of(k), axis, ring(4, k)))  10.9 us
    all_to_all x1, waiting for transfers between devices, on_device(): field = lax.all_to_all(field, ('x', 'y'), 0, 0)  10.6 us
    all_to_all x1, blocking collectives, on_device(): second = lax.all_to_all(message, ('y', 'core'), 0, 0)  8.95 us
  transfers between devices with their start and end apart: 27, of which 8 were waited for; matrix products, arithmetic and copies ran while one was open for 6% of the time, Pallas kernels for 14%

profile of v2, /device:TPU:8, one launch (start us, length us, event | category | flops | bytes accessed | tf_op | source)
XLA Modules:
  0.0 180.0 jit_solution(15889380562886805892)
XLA Ops:
  0.8 5.9 %collective-permute-start.7 = (bf16[4,320,120]{2,1,0:T(8,128)(2,1)}, bf16[4,320,120]{2,1,0:T(8,128)(2,1)}, u32[]{:S(2)}, u32[]{:S(2)}) collective-permute-start(bf16[4,320,120]{2,1,0:T(8,128)(2,1)} %bitcast.51), channel_id=1, source_target_pairs={{0,38},{2,0},{4,2},{6,4},{32,6},{34,32},{36,34},{38,36},{1,39},{3,... | collective-permute-start | bytes 921608 | tf_op jit(solution)/shard_map/ppermute | solution.py:256
  7.8 4.1 %collective-permute-start.4 = (bf16[2,320,120]{2,1,0:T(8,128)(2,1)S(1)}, bf16[2,320,120]{2,1,0:T(8,128)(2,1)}, u32[]{:S(2)}, u32[]{:S(2)}) collective-permute-start(bf16[2,320,120]{2,1,0:T(8,128)(2,1)S(1)} %get-tuple-element.51), channel_id=1, source_target_pairs={{0,36},{2,38},{4,0},{6,2},{32,4},{34,6},{36,32},{38,34},{1,37},{3,... | collective-permute-start | bytes 460808 | tf_op jit(solution)/shard_map/ppermute | solution.py:258
  12.0 2.9 %constant_dynamic-slice_fusion.5 = (bf16[15,48,320]{2,1,0:T(8,128)(2,1)}, bf16[15,48,320]{2,1,0:T(8,128)(2,1)}, bf16[15,48,320]{2,1,0:T(8,128)(2,1)}, bf16[15,48,320]{2,1,0:T(8,128)(2,1)S(1)}) fusion(bf16[15,320,320]{2,1,0:T(8,128)(2,1)} %param.11, s32[]{:T(128)S(6)} %select_n.55, s32[]{:T(128)S(6)} %select_n.54, s32[]{:T(128)S(6)} %select_n.53, s32[]{:T(128)S(6)} %select_n.52), kind=kLoop, calls=%fused_computation.38 | loop fusion | bytes 3686416 | tf_op jit(solution)/shard_map/dynamic_slice | solution.py:263
  17.7 5.4 %collective-permute-done.3.refs_1_ = bf16[2,320,120]{2,1,0:T(8,128)(2,1)S(1)} collective-permute-done((bf16[2,320,120]{2,1,0:T(8,128)(2,1)S(1)}, bf16[2,320,120]{2,1,0:T(8,128)(2,1)S(1)}, u32[]{:S(2)}, u32[]{:S(2)}) %collective-permute-start.3) | collective-permute-done | bytes 153632 | tf_op jit(solution)/shard_map/ppermute | solution.py:257
  25.0 4.5 %pairs.4 = (f32[8,15,128]{2,1,0:T(8,128)S(1)}, f32[8,8,128]{2,1,0:T(8,128)S(1)}, bf16[15,128,320]{2,1,0:T(8,128)(2,1)S(1)}) custom-call(bf16[15,320,120]{2,1,0:T(8,128)(2,1)S(1)} %bitcast.55, bf16[4,320,120]{2,1,0:T(8,128)(2,1)S(1)} %bitcast.54, bf16[4,320,120]{2,1,0:T(8,128)(2,1)} %collective-permute-done.refs_2_), custom_call_target="tpu_custom_call" | custom-call | flops 4026531840 | bytes 3145728 | tf_op jit(solution)/shard_map/pairs/pallas_call | solution.py:94
  31.5 3.8 %pairs.6 = (f32[8,15,128]{2,1,0:T(8,128)S(1)}, f32[8,8,128]{2,1,0:T(8,128)S(1)}) custom-call(bf16[15,128,320]{2,1,0:T(8,128)(2,1)S(1)} %get-tuple-element.27.refs_0_, bf16[2,320,120]{2,1,0:T(8,128)(2,1)S(1)} %collective-permute-done.3.refs_1_, bf16[2,320,120]{2,1,0:T(8,128)(2,1)} %collective-permute-done.4.refs_2_, ...), custom_call_target="tpu_custom_call" | custom-call | flops 4026531840 | bytes 3145728 | tf_op jit(solution)/shard_map/pairs/pallas_call | solution.py:94
  38.7 4.1 %pairs.7 = (f32[8,15,128]{2,1,0:T(8,128)S(1)}, f32[8,8,128]{2,1,0:T(8,128)S(1)}) custom-call(bf16[15,128,320]{2,1,0:T(8,128)(2,1)S(1)} %copy-done.3, bf16[4,320,120]{2,1,0:T(8,128)(2,1)} %collective-permute-done.7.refs_1_, bf16[4,320,120]{2,1,0:T(8,128)(2,1)S(1)} %collective-permute-done.8.refs_2_), custom_call_target="tpu_custom_call" | custom-call | flops 4026531840 | bytes 3145728 | tf_op jit(solution)/shard_map/pairs/pallas_call | solution.py:94
  46.5 4.1 %pairs.5 = (f32[8,15,128]{2,1,0:T(8,128)S(1)}, f32[8,8,128]{2,1,0:T(8,128)S(1)}) custom-call(bf16[15,128,320]{2,1,0:T(8,128)(2,1)S(1)} %copy-done.4, bf16[4,320,120]{2,1,0:T(8,128)(2,1)} %collective-permute-done.1.refs_1_, bf16[4,320,120]{2,1,0:T(8,128)(2,1)S(1)} %collective-permute-done.2.refs_2_), custom_call_target="tpu_custom_call" | custom-call | flops 4026531840 | bytes 3145728 | tf_op jit(solution)/shard_map/pairs/pallas_call | solution.py:94
  51.7 2.8 %collective-permute-start.12 = (bf16[15,48,320]{2,1,0:T(8,128)(2,1)}, bf16[15,48,320]{2,1,0:T(8,128)(2,1)S(1)}, u32[]{:S(2)}, u32[]{:S(2)}) collective-permute-start(bf16[15,48,320]{2,1,0:T(8,128)(2,1)} %get-tuple-element.48), channel_id=1, source_target_pairs={{0,128},{64,192},{128,0},{192,64},{1,129},{65,193},{129,1},{193,65... | collective-permute-start | bytes 1382408 | tf_op jit(solution)/shard_map/ppermute | solution.py:267
  57.4 10.7 %collective-permute-done.12.refs_4_ = bf16[15,48,320]{2,1,0:T(8,128)(2,1)S(1)} collective-permute-done((bf16[15,48,320]{2,1,0:T(8,128)(2,1)}, bf16[15,48,320]{2,1,0:T(8,128)(2,1)S(1)}, u32[]{:S(2)}, u32[]{:S(2)}) %collective-permute-start.12) | collective-permute-done | bytes 460832 | tf_op jit(solution)/shard_map/ppermute | solution.py:267
  68.1 11.0 %collective-permute-done.14.refs_6_ = bf16[15,48,320]{2,1,0:T(8,128)(2,1)S(1)} collective-permute-done((bf16[15,48,320]{2,1,0:T(8,128)(2,1)}, bf16[15,48,320]{2,1,0:T(8,128)(2,1)S(1)}, u32[]{:S(2)}, u32[]{:S(2)}) %collective-permute-start.14) | collective-permute-done | bytes 460832 | tf_op jit(solution)/shard_map/ppermute | solution.py:267
  80.4 9.0 %all_to_all.35.message_ref = f32[8,24,128]{2,1,0:T(8,128)S(1)} all-to-all(f32[8,24,128]{2,1,0:T(8,128)} %bitcast.21), channel_id=1, replica_groups=mesh['x'=4,'zh'=2,'y'=4,'zl'=4,'core'=2] {'y','core'}, dimensions={0} | all-to-all | bytes 196608 | tf_op jit(solution)/shard_map/all_to_all | solution.py:320
  89.4 4.3 %all-to-all-start = ((f32[8,24,128]{2,1,0:T(8,128)}), f32[8,24,128]{2,1,0:T(8,128)S(1)}, u32[]{:S(2)}, u32[]{:S(2)}) async-start(f32[8,24,128]{2,1,0:T(8,128)} %bitcast.21), calls=%async_computation | async-start | bytes 196608 | tf_op jit(solution)/shard_map/all_to_all | solution.py:319
  93.7 3.7 %field_rows.3 = bf16[4,4,32,384]{3,2,1,0:T(8,128)(2,1)} custom-call(s32[8]{0:T(128)S(1)} %stack.111.order_ref, f32[8,24,128]{2,1,0:T(8,128)S(1)} %all_to_all.35.message_ref, bf16[15,32,320]{2,1,0:T(8,128)(2,1)S(1)} %get-tuple-element.45.refs_0_, bf16[15,32,320]{2,1,0:T(8,128)(2,1)S(1)} %collective-permute-done.16.refs_1_, ...), custom_call_target="tpu_custom_call" | custom-call | flops 805306368 | bytes 1920000 | tf_op jit(solution)/shard_map/field_rows/pallas_call | solution.py:146
  99.5 3.5 %all-to-all-start.3 = ((bf16[4,4,32,384]{3,2,1,0:T(8,128)(2,1)}), bf16[4,4,32,384]{3,2,1,0:T(8,128)(2,1)S(1)}, u32[]{:S(2)}, u32[]{:S(2)}) async-start(bf16[4,4,32,384]{3,2,1,0:T(8,128)(2,1)} %field_rows.3), calls=%async_computation.3 | async-start | bytes 786432 | tf_op jit(solution)/shard_map/all_to_all | solution.py:325
  103.1 3.5 %field_rows.2 = bf16[4,4,48,384]{3,2,1,0:T(8,128)(2,1)S(1)} custom-call(s32[8]{0:T(128)S(1)} %stack.92.order_ref, f32[8,24,128]{2,1,0:T(8,128)S(1)} %all-to-all-done.message_ref, bf16[15,48,320]{2,1,0:T(8,128)(2,1)S(1)} %get-tuple-element.50.refs_0_, bf16[15,48,320]{2,1,0:T(8,128)(2,1)} %collective-permute-done.9.refs_1_, ...), custom_call_target="tpu_custom_call" | custom-call | flops 1207959552 | bytes 2880000 | tf_op jit(solution)/shard_map/field_rows/pallas_call | solution.py:146
  106.6 4.5 %all-to-all-done.3.second_ref = bf16[4,4,32,384]{3,2,1,0:T(8,128)(2,1)S(1)} async-done(((bf16[4,4,32,384]{3,2,1,0:T(8,128)(2,1)}), bf16[4,4,32,384]{3,2,1,0:T(8,128)(2,1)S(1)}, u32[]{:S(2)}, u32[]{:S(2)}) %all-to-all-start.3) | async-done | bytes 393248 | tf_op jit(solution)/shard_map/all_to_all | solution.py:325
  111.1 11.5 %all_to_all.36.first_ref = bf16[4,4,48,384]{3,2,1,0:T(8,128)(2,1)S(1)} all-to-all(bf16[4,4,48,384]{3,2,1,0:T(8,128)(2,1)S(1)} %field_rows.2), channel_id=1, replica_groups=mesh['x'=4,'zh'=2,'y'=4,'zl'=4,'core'=2] {'y'}, dimensions={0} | all-to-all | bytes 1179648 | tf_op jit(solution)/shard_map/all_to_all | solution.py:323
  122.7 19.1 %all_to_all.37.in_ref = bf16[8,80,384]{2,1,0:T(8,128)(2,1)S(1)} all-to-all(bf16[8,80,384]{2,1,0:T(8,128)(2,1)S(1)} %sum_plane.1), channel_id=1, replica_groups=mesh['x'=4,'zh'=2,'y'=4,'zl'=4,'core'=2] {'zh','zl'}, dimensions={0} | all-to-all | bytes 983040 | tf_op jit(solution)/shard_map/all_to_all | solution.py:327
  142.6 5.0 %all-to-all-start.6 = ((bf16[32,4,10,120]{3,1,2,0:T(4,128)(2,1)}), bf16[32,4,10,120]{3,1,2,0:T(4,128)(2,1)S(1)}, u32[]{:S(2)}, u32[]{:S(2)}) async-start(bf16[32,4,10,120]{3,1,2,0:T(4,128)(2,1)} %broadcast_in_dim.11), calls=%async_computation.6 | async-start | bytes 655360 | tf_op jit(solution)/shard_map/all_to_all | solution.py:279
  148.7 12.0 %all-to-all-done.6 = bf16[32,4,10,120]{3,1,2,0:T(4,128)(2,1)S(1)} async-done(((bf16[32,4,10,120]{3,1,2,0:T(4,128)(2,1)}), bf16[32,4,10,120]{3,1,2,0:T(4,128)(2,1)S(1)}, u32[]{:S(2)}, u32[]{:S(2)}) %all-to-all-start.6) | async-done | bytes 307232 | tf_op jit(solution)/shard_map/all_to_all | solution.py:279
  160.7 4.8 %all-to-all-start.5 = ((bf16[16,80,384]{2,1,0:T(8,128)(2,1)}), bf16[16,80,384]{2,1,0:T(8,128)(2,1)S(1)}, u32[]{:S(2)}, u32[]{:S(2)}) async-start(bf16[16,80,384]{2,1,0:T(8,128)(2,1)} %get-tuple-element.35), calls=%async_computation.5 | async-start | bytes 1966080 | tf_op jit(solution)/shard_map/all_to_all | solution.py:329
  166.1 10.6 %all-to-all-done.5.in_ref = bf16[16,80,384]{2,1,0:T(8,128)(2,1)S(1)} async-done(((bf16[16,80,384]{2,1,0:T(8,128)(2,1)}), bf16[16,80,384]{2,1,0:T(8,128)(2,1)S(1)}, u32[]{:S(2)}, u32[]{:S(2)}) %all-to-all-start.5) | async-done | bytes 983072 | tf_op jit(solution)/shard_map/all_to_all | solution.py:329
  176.7 2.7 %taylor.1 = bf16[4,320,120]{2,1,0:T(8,128)(2,1)S(1)} custom-call(bf16[16,80,384]{2,1,0:T(8,128)(2,1)S(1)} %all-to-all-done.5.in_ref, bf16[4,320,120]{2,1,0:T(8,128)(2,1)S(1)} %copy.17.walkers_ref), custom_call_target="tpu_custom_call" | custom-call | tf_op jit(solution)/shard_map/taylor/pallas_call | solution.py:228
  (119 shorter events, 25.7 us)
Async XLA Ops:
  0.7 23.9 %collective-permute-start = (bf16[4,320,120]{2,1,0:T(8,128)(2,1)}, bf16[4,320,120]{2,1,0:T(8,128)(2,1)}, u32[]{:S(2)}, u32[]{:S(2)}) collective-permute-start(bf16[4,320,120]{2,1,0:T(8,128)(2,1)} %bitcast.50), channel_id=1, source_target_pairs={{0,1},{1,0},{2,3},{3,2},{4,5},{5,4},{6,7},{7,6},{8,9},{9,8},{10,11... | collective-permute-start | bytes 921608 | tf_op jit(solution)/shard_map/ppermute | solution.py:252
  0.8 28.8 %collective-permute-start.7 = (bf16[4,320,120]{2,1,0:T(8,128)(2,1)}, bf16[4,320,120]{2,1,0:T(8,128)(2,1)}, u32[]{:S(2)}, u32[]{:S(2)}) collective-permute-start(bf16[4,320,120]{2,1,0:T(8,128)(2,1)} %bitcast.51), channel_id=1, source_target_pairs={{0,38},{2,0},{4,2},{6,4},{32,6},{34,32},{36,34},{38,36},{1,39},{3,... | collective-permute-start | bytes 921608 | tf_op jit(solution)/shard_map/ppermute | solution.py:256
  6.7 29.3 %collective-permute-start.1 = (bf16[4,320,120]{2,1,0:T(8,128)(2,1)}, bf16[4,320,120]{2,1,0:T(8,128)(2,1)}, u32[]{:S(2)}, u32[]{:S(2)}) collective-permute-start(bf16[4,320,120]{2,1,0:T(8,128)(2,1)} %bitcast.52), channel_id=1, source_target_pairs={{0,2},{2,4},{4,6},{6,32},{32,34},{34,36},{36,38},{38,0},{1,3},{3,5... | collective-permute-start | bytes 921608 | tf_op jit(solution)/shard_map/ppermute | solution.py:255
  7.7 15.3 %collective-permute-start.3 = (bf16[2,320,120]{2,1,0:T(8,128)(2,1)S(1)}, bf16[2,320,120]{2,1,0:T(8,128)(2,1)S(1)}, u32[]{:S(2)}, u32[]{:S(2)}) collective-permute-start(bf16[2,320,120]{2,1,0:T(8,128)(2,1)S(1)} %get-tuple-element.52), channel_id=1, source_target_pairs={{0,4},{2,6},{4,32},{6,34},{32,36},{34,38},{36,0},{38,2},{1,5},{3,7... | collective-permute-start | bytes 460808 | tf_op jit(solution)/shard_map/ppermute | solution.py:257
  7.8 16.7 %collective-permute-start.4 = (bf16[2,320,120]{2,1,0:T(8,128)(2,1)S(1)}, bf16[2,320,120]{2,1,0:T(8,128)(2,1)}, u32[]{:S(2)}, u32[]{:S(2)}) collective-permute-start(bf16[2,320,120]{2,1,0:T(8,128)(2,1)S(1)} %get-tuple-element.51), channel_id=1, source_target_pairs={{0,36},{2,38},{4,0},{6,2},{32,4},{34,6},{36,32},{38,34},{1,37},{3,... | collective-permute-start | bytes 460808 | tf_op jit(solution)/shard_map/ppermute | solution.py:258
  23.0 33.9 %collective-permute-start.10 = (bf16[15,48,320]{2,1,0:T(8,128)(2,1)}, bf16[15,48,320]{2,1,0:T(8,128)(2,1)S(1)}, u32[]{:S(2)}, u32[]{:S(2)}) collective-permute-start(bf16[15,48,320]{2,1,0:T(8,128)(2,1)} %get-tuple-element.49), channel_id=1, source_target_pairs={{0,64},{64,128},{128,192},{192,0},{1,65},{65,129},{129,193},{193,1... | collective-permute-start | bytes 1382408 | tf_op jit(solution)/shard_map/ppermute | solution.py:267
  24.5 6.8 %collective-permute-start.6 = (bf16[2,320,120]{2,1,0:T(8,128)(2,1)}, bf16[2,320,120]{2,1,0:T(8,128)(2,1)S(1)}, u32[]{:S(2)}, u32[]{:S(2)}) collective-permute-start(bf16[2,320,120]{2,1,0:T(8,128)(2,1)} %collective-permute-done.4.refs_2_), channel_id=1, source_target_pairs={{0,1},{1,0},{2,3},{3,2},{4,5},{5,4},{6,7},{7,6},{8,9},{9,8},{10,11... | collective-permute-start | bytes 460808 | tf_op jit(solution)/shard_map/ppermute | solution.py:252
  29.6 22.1 %collective-permute-start.16 = (bf16[15,32,320]{2,1,0:T(8,128)(2,1)S(1)}, bf16[15,32,320]{2,1,0:T(8,128)(2,1)S(1)}, u32[]{:S(2)}, u32[]{:S(2)}) collective-permute-start(bf16[15,32,320]{2,1,0:T(8,128)(2,1)S(1)} %get-tuple-element.45.refs_0_), channel_id=1, source_target_pairs={{0,1},{1,0},{2,3},{3,2},{4,5},{5,4},{6,7},{7,6},{8,9},{9,8},{10,11... | collective-permute-start | bytes 921608 | tf_op jit(solution)/shard_map/ppermute | solution.py:252
  29.8 24.7 %collective-permute-start.17 = (bf16[15,32,320]{2,1,0:T(8,128)(2,1)}, bf16[15,32,320]{2,1,0:T(8,128)(2,1)}, u32[]{:S(2)}, u32[]{:S(2)}) collective-permute-start(bf16[15,32,320]{2,1,0:T(8,128)(2,1)} %get-tuple-element.44), channel_id=1, source_target_pairs={{0,8},{8,16},{16,24},{24,0},{1,9},{9,17},{17,25},{25,1},{2,10},{10... | collective-permute-start | bytes 921608 | tf_op jit(solution)/shard_map/ppermute | solution.py:267
  36.0 20.0 %collective-permute-start.19 = (bf16[15,32,320]{2,1,0:T(8,128)(2,1)}, bf16[15,32,320]{2,1,0:T(8,128)(2,1)}, u32[]{:S(2)}, u32[]{:S(2)}) collective-permute-start(bf16[15,32,320]{2,1,0:T(8,128)(2,1)} %get-tuple-element.46), channel_id=1, source_target_pairs={{0,16},{8,24},{16,0},{24,8},{1,17},{9,25},{17,1},{25,9},{2,18},{10... | collective-permute-start | bytes 921608 | tf_op jit(solution)/shard_map/ppermute | solution.py:267
  42.9 13.7 %collective-permute-start.21 = (bf16[15,32,320]{2,1,0:T(8,128)(2,1)}, bf16[15,32,320]{2,1,0:T(8,128)(2,1)}, u32[]{:S(2)}, u32[]{:S(2)}) collective-permute-start(bf16[15,32,320]{2,1,0:T(8,128)(2,1)} %get-tuple-element.43), channel_id=1, source_target_pairs={{0,24},{8,0},{16,8},{24,16},{1,25},{9,1},{17,9},{25,17},{2,26},{10... | collective-permute-start | bytes 921608 | tf_op jit(solution)/shard_map/ppermute | solution.py:267
  51.7 16.4 %collective-permute-start.12 = (bf16[15,48,320]{2,1,0:T(8,128)(2,1)}, bf16[15,48,320]{2,1,0:T(8,128)(2,1)S(1)}, u32[]{:S(2)}, u32[]{:S(2)}) collective-permute-start(bf16[15,48,320]{2,1,0:T(8,128)(2,1)} %get-tuple-element.48), channel_id=1, source_target_pairs={{0,128},{64,192},{128,0},{192,64},{1,129},{65,193},{129,1},{193,65... | collective-permute-start | bytes 1382408 | tf_op jit(solution)/shard_map/ppermute | solution.py:267
  54.5 24.6 %collective-permute-start.14 = (bf16[15,48,320]{2,1,0:T(8,128)(2,1)}, bf16[15,48,320]{2,1,0:T(8,128)(2,1)S(1)}, u32[]{:S(2)}, u32[]{:S(2)}) collective-permute-start(bf16[15,48,320]{2,1,0:T(8,128)(2,1)} %get-tuple-element.47), channel_id=1, source_target_pairs={{0,192},{64,0},{128,64},{192,128},{1,193},{65,1},{129,65},{193,129... | collective-permute-start | bytes 1382408 | tf_op jit(solution)/shard_map/ppermute | solution.py:267
  55.9 23.1 %collective-permute-start.18 = (bf16[15,32,320]{2,1,0:T(8,128)(2,1)}, bf16[15,32,320]{2,1,0:T(8,128)(2,1)}, u32[]{:S(2)}, u32[]{:S(2)}) collective-permute-start(bf16[15,32,320]{2,1,0:T(8,128)(2,1)} %collective-permute-done.17.refs_2_), channel_id=1, source_target_pairs={{0,1},{1,0},{2,3},{3,2},{4,5},{5,4},{6,7},{7,6},{8,9},{9,8},{10,11... | collective-permute-start | bytes 921608 | tf_op jit(solution)/shard_map/ppermute | solution.py:252
  56.6 22.9 %collective-permute-start.20 = (bf16[15,32,320]{2,1,0:T(8,128)(2,1)}, bf16[15,32,320]{2,1,0:T(8,128)(2,1)}, u32[]{:S(2)}, u32[]{:S(2)}) collective-permute-start(bf16[15,32,320]{2,1,0:T(8,128)(2,1)} %collective-permute-done.19.refs_4_), channel_id=1, source_target_pairs={{0,1},{1,0},{2,3},{3,2},{4,5},{5,4},{6,7},{7,6},{8,9},{9,8},{10,11... | collective-permute-start | bytes 921608 | tf_op jit(solution)/shard_map/ppermute | solution.py:252
  56.9 46.2 %collective-permute-start.9 = (bf16[15,48,320]{2,1,0:T(8,128)(2,1)S(1)}, bf16[15,48,320]{2,1,0:T(8,128)(2,1)}, u32[]{:S(2)}, u32[]{:S(2)}) collective-permute-start(bf16[15,48,320]{2,1,0:T(8,128)(2,1)S(1)} %get-tuple-element.50.refs_0_), channel_id=1, source_target_pairs={{0,1},{1,0},{2,3},{3,2},{4,5},{5,4},{6,7},{7,6},{8,9},{9,8},{10,11... | collective-permute-start | bytes 1382408 | tf_op jit(solution)/shard_map/ppermute | solution.py:252
  68.1 25.7 %collective-permute-start.22 = (bf16[15,32,320]{2,1,0:T(8,128)(2,1)}, bf16[15,32,320]{2,1,0:T(8,128)(2,1)}, u32[]{:S(2)}, u32[]{:S(2)}) collective-permute-start(bf16[15,32,320]{2,1,0:T(8,128)(2,1)} %collective-permute-done.21.refs_6_), channel_id=1, source_target_pairs={{0,1},{1,0},{2,3},{3,2},{4,5},{5,4},{6,7},{7,6},{8,9},{9,8},{10,11... | collective-permute-start | bytes 921608 | tf_op jit(solution)/shard_map/ppermute | solution.py:252
  79.1 24.0 %collective-permute-start.11 = (bf16[15,48,320]{2,1,0:T(8,128)(2,1)S(1)}, bf16[15,48,320]{2,1,0:T(8,128)(2,1)}, u32[]{:S(2)}, u32[]{:S(2)}) collective-permute-start(bf16[15,48,320]{2,1,0:T(8,128)(2,1)S(1)} %collective-permute-done.10.refs_2_), channel_id=1, source_target_pairs={{0,1},{1,0},{2,3},{3,2},{4,5},{5,4},{6,7},{7,6},{8,9},{9,8},{10,11... | collective-permute-start | bytes 1382408 | tf_op jit(solution)/shard_map/ppermute | solution.py:252
  79.1 24.0 %collective-permute-start.13 = (bf16[15,48,320]{2,1,0:T(8,128)(2,1)S(1)}, bf16[15,48,320]{2,1,0:T(8,128)(2,1)}, u32[]{:S(2)}, u32[]{:S(2)}) collective-permute-start(bf16[15,48,320]{2,1,0:T(8,128)(2,1)S(1)} %collective-permute-done.12.refs_4_), channel_id=1, source_target_pairs={{0,1},{1,0},{2,3},{3,2},{4,5},{5,4},{6,7},{7,6},{8,9},{9,8},{10,11... | collective-permute-start | bytes 1382408 | tf_op jit(solution)/shard_map/ppermute | solution.py:252
  79.6 23.5 %collective-permute-start.15 = (bf16[15,48,320]{2,1,0:T(8,128)(2,1)S(1)}, bf16[15,48,320]{2,1,0:T(8,128)(2,1)}, u32[]{:S(2)}, u32[]{:S(2)}) collective-permute-start(bf16[15,48,320]{2,1,0:T(8,128)(2,1)S(1)} %collective-permute-done.14.refs_6_), channel_id=1, source_target_pairs={{0,1},{1,0},{2,3},{3,2},{4,5},{5,4},{6,7},{7,6},{8,9},{9,8},{10,11... | collective-permute-start | bytes 1382408 | tf_op jit(solution)/shard_map/ppermute | solution.py:252
  89.4 10.1 %all-to-all-start = ((f32[8,24,128]{2,1,0:T(8,128)}), f32[8,24,128]{2,1,0:T(8,128)S(1)}, u32[]{:S(2)}, u32[]{:S(2)}) async-start(f32[8,24,128]{2,1,0:T(8,128)} %bitcast.21), calls=%async_computation | async-start | bytes 196608 | tf_op jit(solution)/shard_map/all_to_all | solution.py:319
  99.5 11.6 %all-to-all-start.3 = ((bf16[4,4,32,384]{3,2,1,0:T(8,128)(2,1)}), bf16[4,4,32,384]{3,2,1,0:T(8,128)(2,1)S(1)}, u32[]{:S(2)}, u32[]{:S(2)}) async-start(bf16[4,4,32,384]{3,2,1,0:T(8,128)(2,1)} %field_rows.3), calls=%async_computation.3 | async-start | bytes 786432 | tf_op jit(solution)/shard_map/all_to_all | solution.py:325
  142.6 18.1 %all-to-all-start.6 = ((bf16[32,4,10,120]{3,1,2,0:T(4,128)(2,1)}), bf16[32,4,10,120]{3,1,2,0:T(4,128)(2,1)S(1)}, u32[]{:S(2)}, u32[]{:S(2)}) async-start(bf16[32,4,10,120]{3,1,2,0:T(4,128)(2,1)} %broadcast_in_dim.11), calls=%async_computation.6 | async-start | bytes 655360 | tf_op jit(solution)/shard_map/all_to_all | solution.py:279
  160.7 16.0 %all-to-all-start.5 = ((bf16[16,80,384]{2,1,0:T(8,128)(2,1)}), bf16[16,80,384]{2,1,0:T(8,128)(2,1)S(1)}, u32[]{:S(2)}, u32[]{:S(2)}) async-start(bf16[16,80,384]{2,1,0:T(8,128)(2,1)} %get-tuple-element.35), calls=%async_computation.5 | async-start | bytes 1966080 | tf_op jit(solution)/shard_map/all_to_all | solution.py:329
  (11 other events, 120.0 us)

commit v3 on v2

v3 whole, which is shorter than its diff:
```python
import functools

import jax
import jax.numpy as jnp
from jax import lax
from jax.experimental import pallas as pl
from jax.experimental.pallas import tpu as pltpu
from jax.sharding import Mesh, PartitionSpec as P

ORDER = 4
step_root = 0.1

AXES = ("x", "zh", "y", "zl", "core")
SIZES = (4, 2, 4, 4, 2)
Z = ("zh", "zl")
HIGH = ("x", "zh", "y")
LOW = ("zl", "core")

ROW = 128
WIDE = 384
TILE = 16
f32 = jnp.float32
bf16 = jnp.bfloat16
CONTRACT_LAST = (((1,), (1,)), ((), ()))


def after(value, *others):
    return lax.optimization_barrier((value, *others))[0]


def ring(count, shift):
    return [(i, (i + shift) % count) for i in range(count)]


def parts_of(value):
    high = value.astype(bf16).astype(f32)
    rest = value - high
    middle = rest.astype(bf16).astype(f32)
    low = (rest - middle).astype(bf16).astype(f32)
    row = lax.broadcasted_iota(jnp.int32, (TILE, value.shape[1]), 0)
    zero = jnp.zeros((TILE, value.shape[1]), f32)
    return jnp.where(
        row == 0, high, jnp.where(row == 1, middle, jnp.where(row == 2, low, zero))
    )


def pair_kernel(vectors, turned, walkers, *refs):
    rot_ref, greens = refs[0], refs[1 : 1 + walkers]
    trace_ref, square_ref = refs[1 + walkers : 3 + walkers]
    if not turned:
        raw_ref, rot_ref = rot_ref, refs[3 + walkers]
        for g in range(vectors):
            rot_ref[g] = widen(raw_ref[g]).T
    orbitals = rot_ref.shape[2]
    eye = (
        lax.broadcasted_iota(jnp.int32, (ROW, ROW), 0)
        == lax.broadcasted_iota(jnp.int32, (ROW, ROW), 1)
    ).astype(f32)
    base = 0
    for green_ref in greens:
        count = green_ref.shape[0] // 2

        def two_walkers(i, carry, green_ref=green_ref, base=base):
            green = jnp.concatenate([widen(green_ref[2 * i]), widen(green_ref[2 * i + 1])], axis=1)
            rot = rot_ref[...].reshape(vectors * ROW, orbitals)
            pairs = jnp.dot(rot, green, preferred_element_type=f32)
            for w in range(2):
                total = jnp.zeros((8, ROW), f32)
                for g in range(vectors):
                    block = pairs[g * ROW : (g + 1) * ROW, w * ROW : (w + 1) * ROW]
                    total = total + jnp.sum((block * block.T).reshape(ROW // 8, 8, ROW), axis=0)
                    trace_ref[base + 2 * i + w, pl.ds(g, 1), :] = jnp.sum(
                        block * eye, axis=0, keepdims=True
                    )
                square_ref[base + 2 * i + w] = total
            return carry

        if count == 1:
            two_walkers(0, 0)
        else:
            lax.fori_loop(0, count, two_walkers, 0)
        base += 2 * count


def widen(a):
    return jnp.concatenate([a, jnp.zeros((a.shape[0], ROW - a.shape[1]), a.dtype)], axis=1)


def pair_sums(rot, greens, turned):
    vectors = rot.shape[0]
    walkers = sum(g.shape[0] for g in greens)
    out_shape = [
        jax.ShapeDtypeStruct((walkers, vectors, ROW), f32),
        jax.ShapeDtypeStruct((walkers, 8, ROW), f32),
    ]
    if not turned:
        out_shape.append(jax.ShapeDtypeStruct((vectors, ROW, rot.shape[1]), bf16))
    return pl.pallas_call(
        functools.partial(pair_kernel, vectors, turned, len(greens)),
        out_shape=out_shape,
        compiler_params=pltpu.CompilerParams(vmem_limit_bytes=40 * 2**20),
        cost_estimate=pl.CostEstimate(flops=1, bytes_accessed=1, transcendentals=0),
        name="pairs",
    )(rot, *greens)


def message_kernel(vector_total, place_ref, *refs):
    traces, squares = refs[0:4], refs[4:8]
    fields_ref, green_ref, one_body_ref, walkers_ref, out_ref = refs[8:]
    zl, core = place_ref[0], place_ref[1]
    vectors = fields_ref.shape[0]
    lanes = lax.broadcasted_iota(jnp.int32, (vectors, 128), 1)
    lane = lax.broadcasted_iota(jnp.int32, (1, 128), 1)
    intersection = jnp.zeros((vectors, 128), f32)
    exchange = jnp.zeros((1, 128), f32)
    single = jnp.zeros((1, 128), f32)
    one_body = one_body_ref[...].astype(f32)
    for d in range(4):
        for w in range(8):
            owner = core if w < 4 else 1 - core
            index = owner * 16 + (w % 4) * 4 + lax.rem(zl + 4 - d, 4)
            trace = jnp.sum(traces[d][w], axis=1, keepdims=True)
            intersection = jnp.where(lanes == index, trace, intersection)
            exchange = jnp.where(lane == index, jnp.sum(squares[d][w], keepdims=True), exchange)
            if d == 0 and w < 4:
                own = jnp.sum(green_ref[w].astype(f32) * one_body, keepdims=True)
                single = jnp.where(lane == index, own * (2.0 / 32.0), single)
    bias = 2.0 * step_root * intersection
    noise = fields_ref[...]
    weight = jnp.sum(noise * bias - 0.5 * bias * bias, axis=0, keepdims=True) / vector_total**0.5
    energy = jnp.sum(2.0 * intersection * intersection, axis=0, keepdims=True) - exchange
    energy = energy / vector_total + single
    shifted = jnp.concatenate([noise - bias, jnp.zeros((128 - vectors, 128), f32)]).T
    scalars = parts_of(pltpu.roll(energy, 64, 1) + pltpu.roll(weight, 96, 1))
    top = (shifted[0:TILE] + scalars).astype(bf16)
    low = shifted[TILE : 2 * TILE].astype(bf16)
    for k in range(out_ref.shape[0]):
        out_ref[k, 0:TILE] = top
        out_ref[k, TILE : 2 * TILE] = low
        out_ref[k, 2 * TILE :] = walkers_ref[...]


def messages(place, sums, fields, green, one_body, walkers):
    vectors = fields.shape[0]
    return pl.pallas_call(
        functools.partial(message_kernel, vectors * 256),
        out_shape=jax.ShapeDtypeStruct((16, 2 * TILE + walkers.shape[0], 128), bf16),
        in_specs=[pl.BlockSpec(memory_space=pltpu.SMEM)]
        + [pl.BlockSpec(memory_space=pltpu.VMEM)] * 12,
        compiler_params=pltpu.CompilerParams(vmem_limit_bytes=24 * 2**20),
        name="message",
    )(place, *[p[0] for p in sums], *[p[1] for p in sums], fields, green, one_body, walkers)


def field_kernel(vectors, count, adds, place_ref, message_ref, *refs):
    blocks, refs = refs[:count], refs[count:]
    if count == 1:
        blocks = [blocks[0].at[k] for k in range(4)]
    outs = refs[adds:]
    rows, orbitals = blocks[0].shape[1:]
    depth = vectors * TILE
    spread = (
        lax.broadcasted_iota(jnp.int32, (ROW, depth), 0)
        == lax.shift_right_logical(lax.broadcasted_iota(jnp.int32, (ROW, depth), 1), 4)
    ).astype(bf16)
    same = (
        jnp.bitwise_and(lax.broadcasted_iota(jnp.int32, (TILE * TILE, depth), 0), TILE - 1)
        == jnp.bitwise_and(lax.broadcasted_iota(jnp.int32, (TILE * TILE, depth), 1), TILE - 1)
    )
    start = pl.multiple_of(place_ref[4] * TILE, TILE)
    weights = []
    for b in range(len(blocks)):
        shifted = message_ref[place_ref[b], pl.ds(start, TILE), :].astype(f32)
        shifted = pltpu.roll(shifted, place_ref[5], 0).astype(bf16)
        wide = jnp.dot(shifted, spread, preferred_element_type=f32)
        wide = jnp.broadcast_to(wide[:, None, :], (TILE, TILE, depth)).reshape(TILE * TILE, depth)
        weights.append(jnp.where(same, wide, 0.0).astype(bf16))
    outs = [out.at[i] for out in outs for i in range(out.shape[0])]
    for out_ref in outs:
        out_ref[:, :, 256:WIDE] = jnp.zeros((4, rows, WIDE - 256), bf16)
    for t in range(rows // TILE):
        here = slice(t * TILE, (t + 1) * TILE)
        total = jnp.zeros((TILE * TILE, orbitals), f32)
        for b, block_ref in enumerate(blocks):
            block = block_ref[:, here, :].reshape(depth, orbitals)
            total = total + jnp.dot(weights[b], block, preferred_element_type=f32)
        total = (step_root * total).reshape(TILE, TILE, orbitals)
        for w in range(TILE):
            part = total[w]
            if adds:
                part = part + refs[0][w // 4, w % 4, here, 0:orbitals].astype(f32)
            outs[w // 4][w % 4, here, 0:orbitals] = part.astype(bf16)


def field_rows(place, message, blocks, other=None, pieces=1):
    vectors, rows, _ = blocks[0].shape[-3:]
    added = [] if other is None else [other]
    return pl.pallas_call(
        functools.partial(field_kernel, vectors, len(blocks), other is not None),
        out_shape=[jax.ShapeDtypeStruct((4 // pieces, 4, rows, WIDE), bf16)] * pieces,
        in_specs=[pl.BlockSpec(memory_space=pltpu.SMEM)]
        + [pl.BlockSpec(memory_space=pltpu.VMEM)] * (1 + len(blocks) + len(added)),
        compiler_params=pltpu.CompilerParams(vmem_limit_bytes=40 * 2**20),
        cost_estimate=pl.CostEstimate(
            flops=rows * 256 * 384 * 128, bytes_accessed=rows * 40000, transcendentals=0
        ),
        name="field_rows",
    )(place, message, *blocks, *added)


def sum_kernel(copies, message_ref, *refs):
    upper = lax.broadcasted_iota(jnp.int32, (TILE, 128), 1) >= 64
    scalars = message_ref[0, 0:TILE].astype(f32)
    for s in range(1, message_ref.shape[0]):
        scalars = scalars + message_ref[s, 0:TILE].astype(f32)
    scalars = parts_of(jnp.sum(scalars, axis=0, keepdims=True))
    out_ref = refs[-1]
    pieces = [ref.at[i] for ref in refs[:-1] for i in range(ref.shape[0])]
    firsts, seconds = pieces[:4], pieces[4:]
    groups, rows = firsts[0].shape[:2]
    for g in range(groups):
        total = firsts[0][g].astype(f32)
        below = seconds[0][g].astype(f32)
        for s in range(1, 4):
            total = total + firsts[s][g].astype(f32)
            below = below + seconds[s][g].astype(f32)
        corner = jnp.where(upper, scalars, total[0:TILE, 256:WIDE]).astype(bf16)
        total, below = total.astype(bf16), below.astype(bf16)
        for k in range(g, copies, groups):
            out_ref[k, 0:rows] = total
            out_ref[k, rows:] = below
            out_ref[k, 0:TILE, 256:WIDE] = corner


def sum_second_axis(message, first, second):
    rows, wide = first[0].shape[2] + second[0].shape[2], first[0].shape[3]
    return pl.pallas_call(
        functools.partial(sum_kernel, 8),
        out_shape=jax.ShapeDtypeStruct((8, rows, wide), bf16),
        compiler_params=pltpu.CompilerParams(vmem_limit_bytes=24 * 2**20),
        name="sum_plane",
    )(message, *first, *second)


def last_kernel(in_ref, out_ref, scalars_ref):
    total = in_ref[0].astype(f32)
    for s in range(1, in_ref.shape[0]):
        total = total + in_ref[s].astype(f32)
    rounded = total.astype(bf16)
    scalars_ref[...] = jnp.sum(total[0:TILE, 256:WIDE], axis=0, keepdims=True)
    for k in range(out_ref.shape[0]):
        out_ref[k] = rounded


def sum_over_z(received):
    _, rows, wide = received.shape
    return pl.pallas_call(
        last_kernel,
        out_shape=(
            jax.ShapeDtypeStruct((16, rows, wide), bf16),
            jax.ShapeDtypeStruct((1, 128), f32),
        ),
        compiler_params=pltpu.CompilerParams(vmem_limit_bytes=24 * 2**20),
        name="sum_z",
    )(received)


def taylor_kernel(first_rows, in_ref, walkers_ref, out_ref):
    orbitals = walkers_ref.shape[1]
    for w in range(4):
        field = jnp.concatenate(
            [in_ref[4 * k + w, 0:first_rows] for k in range(4)]
            + [in_ref[4 * w + k, first_rows:] for k in range(4)]
        )[:, 0:orbitals]
        current = walkers_ref[w]
        total = current.astype(f32)
        for order in range(1, ORDER + 1):
            update = jnp.dot(field, current, preferred_element_type=f32) / order
            total = total + update
            current = update.astype(bf16)
        out_ref[w] = total.astype(bf16)


def taylor(gathered, walkers, first_rows):
    return pl.pallas_call(
        functools.partial(taylor_kernel, first_rows),
        out_shape=jax.ShapeDtypeStruct(walkers.shape, bf16),
        compiler_params=pltpu.CompilerParams(vmem_limit_bytes=24 * 2**20),
        name="taylor",
    )(gathered, walkers)


def on_device(green, walkers, chol_rot, chol_full, fields, one_body_rot):
    x, zh, y, zl, core = (lax.axis_index(a) for a in AXES)
    vectors, electrons, orbitals = chol_rot.shape
    vector_total = vectors * 256
    group = green.shape[0]
    tiles = orbitals // TILE
    first_rows = TILE * ((tiles // 4 + 1) // 2)
    second_rows = orbitals // 4 - first_rows

    def swap(a):
        return lax.ppermute(a, "core", ring(2, 1))

    turned = green.swapaxes(1, 2)
    before = lax.ppermute(turned, Z, ring(8, 1))
    behind = lax.ppermute(turned, Z, ring(8, -1))
    opposite = [(2 * i + c, 2 * ((i + 2 - 4 * c) % 8) + c) for i in range(8) for c in range(2)]
    far = lax.ppermute(turned, Z + ("core",), opposite)

    first_pieces = [
        lax.dynamic_slice_in_dim(chol_full, lax.rem(x + k, 4) * first_rows, first_rows, axis=1)
        for k in range(4)
    ]
    first_blocks = first_pieces[:1] + [
        lax.ppermute(first_pieces[k], "x", ring(4, k)) for k in (1, 2, 3)
    ]
    second_piece = chol_full[:, 4 * first_rows :].reshape(vectors, 4, second_rows, orbitals)
    second_piece = second_piece.transpose(1, 0, 2, 3)
    second_block = lax.all_to_all(second_piece, "y", 0, 0)

    rot = after(chol_rot.swapaxes(1, 2), *first_pieces, second_piece)
    own = pair_sums(rot, [turned, swap(turned)], False)
    before, behind, far = (after(a, own[0]) for a in (before, behind, far))
    sums = [own] + [pair_sums(own[2], [a, swap(a)], True) for a in (before, far, behind)]

    noise = fields.reshape(vectors, 4, 2, group).transpose(0, 2, 3, 1).reshape(vectors, 8 * group)
    noise = jnp.pad(noise, ((0, 0), (0, 128 - 8 * group)))
    share = walkers.shape[1]
    near = walkers.transpose(1, 0, 2).reshape(share * group, electrons)
    near = jnp.pad(near, ((0, -share * group % TILE), (0, 128 - electrons)))
    message = messages(
        jnp.stack([zl, core]).astype(jnp.int32), sums, noise, turned, one_body_rot.T, near
    )
    message = after(message, *first_blocks, second_block)
    message = lax.all_to_all(message, ("x", "y"), 0, 0)

    def place(positions, half, shift):
        return jnp.stack([*positions, half, shift]).astype(jnp.int32)

    along_x = [4 * lax.rem(x + 4 - k, 4) + y for k in range(4)]
    along_y = [4 * x + k for k in range(4)]
    turn = lax.rem(16 - 4 * x, 16)
    (second,) = field_rows(place(along_y, 1 - core, turn), message, [second_block])
    second = swap(second)
    (first,) = field_rows(place(along_x, 1 - core, 0), message, first_blocks)
    first = swap(first)
    second = field_rows(place(along_y, core, turn), message, [second_block], second, 4)
    second = [second[0]] + [lax.ppermute(second[k], "x", ring(4, k)) for k in (1, 2, 3)]
    (first,) = field_rows(place(along_x, core, 0), message, first_blocks, first)
    first = lax.all_to_all(first, "y", 0, 0)
    near = after(message[:, 2 * TILE : 2 * TILE + share * group, :electrons], second[0])
    other = lax.ppermute(near, "zh", ring(2, 1))
    whole = jnp.where(zh == 0, jnp.stack([near, other], 1), jnp.stack([other, near], 1))
    whole = whole.reshape(4, 4, 2, share, group, electrons).transpose(4, 0, 2, 1, 3, 5)
    whole = whole.reshape(group, orbitals, electrons)
    field = sum_second_axis(message, [first], second)
    field = lax.all_to_all(field, Z, 0, 0)
    field, scalars = sum_over_z(field)
    scalars = scalars + swap(scalars)
    field = lax.all_to_all(field, ("x", "y"), 0, 0)
    new = taylor(field, whole, first_rows)
    new = lax.dynamic_slice_in_dim(new, share * (8 * x + 4 * zh + y), share, axis=1)

    def in_order(a):
        return a.reshape(2, group, 4).transpose(2, 0, 1).reshape(8 * group)

    return new, in_order(scalars[0, 64:96]), in_order(scalars[0, 96:128])


def solution(mesh):
    split = Mesh(mesh.devices.reshape(SIZES), AXES)
    in_specs = (
        P(LOW, None, None),
        P(LOW, HIGH, None),
        P(HIGH + LOW, None, None),
        P(HIGH + LOW, None, None),
        P(HIGH + LOW, None),
        P(),
    )
    out_specs = (P(LOW, HIGH, None), P(), P())
    return jax.shard_map(
        on_device, mesh=split, in_specs=in_specs, out_specs=out_specs, check_vma=False
    )
```

time: 181 us -> 138 us (0.76)
  waiting for transfers between devices: 56.8 us -> 27.1 us
  blocking collectives: 39.5 us -> 21.1 us
  starting transfers between devices: 40.8 us -> 45 us
  Pallas kernels: 27.6 us -> 31.4 us
    all_to_all x2 -> x0, blocking collectives: 20.4 us -> none  [the longest x1 11.5 us: on_device(): first = lax.all_to_all(first, 'y', 0, 0)]
    all_to_all x3, waiting for transfers between devices: 18.6 us -> 7.36 us  [the longest x1 7.36 us: on_device(): message = lax.all_to_all(message, ('x', 'y'), 0, 0)]
    all_to_all x1, waiting for transfers between devices: 10.6 us -> 0.75 us  [on_device(): field = lax.all_to_all(field, ('x', 'y'), 0, 0)]
    ppermute x9, waiting for transfers between devices: 27.6 us -> 18.7 us  [the longest x1 9.01 us: on_device(): other = lax.ppermute(near, 'zh', ring(2, 1))]
    pallas_call x2 -> x5, Pallas kernels: 7.19 us -> 11.5 us  [the longest x4 9.82 us: field_rows(): pl.pallas_call(functools.partial(field_kernel, vectors, len(blocks), othe...]
    all_to_all x3, starting transfers between devices: 12.8 us -> 17 us  [the longest x1 6.91 us: on_device(): message = lax.all_to_all(message, ('x', 'y'), 0, 0)]
    ppermute x9, starting transfers between devices: 21 us -> 17.4 us  [the longest x3 6.64 us: on_device(): lax.ppermute(first_pieces[k], 'x', ring(4, k))]
    all_to_all x1, starting transfers between devices: 4.77 us -> 7.76 us  [on_device(): field = lax.all_to_all(field, ('x', 'y'), 0, 0)]
  transfers between devices with their start and end apart: 27 -> 21, of which waited for: 8 -> 7; matrix products, arithmetic and copies ran while one was open for 6% -> 5% of each run, Pallas kernels for 14% -> 18%
where the time goes in v3:
time: 138 us
  starting transfers between devices  45 us (33%)
  Pallas kernels  31.4 us (23%)
  waiting for transfers between devices  27.1 us (20%)
  blocking collectives  21.1 us (15%)
  local copies, waits for them, and re-layouts  11.7 us (8%)
    all_to_all x1, blocking collectives, on_device(): field = lax.all_to_all(field, Z, 0, 0)  21.1 us
    pallas_call x4, Pallas kernels, pair_sums(): pl.pallas_call(functools.partial(pair_kernel, vectors, turned, len(greens...  16 us
    pallas_call x4, Pallas kernels, field_rows(): pl.pallas_call(functools.partial(field_kernel, vectors, len(blocks), othe...  9.82 us
    ppermute x1, waiting for transfers between devices, on_device(): other = lax.ppermute(near, 'zh', ring(2, 1))  9.01 us
    all_to_all x1, starting transfers between devices, on_device(): field = lax.all_to_all(field, ('x', 'y'), 0, 0)  7.76 us
    all_to_all x1, waiting for transfers between devices, on_device(): message = lax.all_to_all(message, ('x', 'y'), 0, 0)  7.36 us
    all_to_all x1, starting transfers between devices, on_device(): message = lax.all_to_all(message, ('x', 'y'), 0, 0)  6.91 us
    ppermute x3, starting transfers between devices, on_device(): lax.ppermute(first_pieces[k], 'x', ring(4, k))  6.64 us
  transfers between devices with their start and end apart: 21, of which 7 were waited for; matrix products, arithmetic and copies ran while one was open for 5% of the time, Pallas kernels for 18%

profile of v3, /device:TPU:8, one launch (start us, length us, event | category | flops | bytes accessed | tf_op | source)
XLA Modules:
  0.0 137.5 jit_solution(13024827988218227454)
XLA Ops:
  0.7 5.9 %collective-permute-start.5 = (bf16[4,320,120]{2,1,0:T(8,128)(2,1)}, bf16[4,320,120]{2,1,0:T(8,128)(2,1)}, u32[]{:S(2)}, u32[]{:S(2)}) collective-permute-start(bf16[4,320,120]{2,1,0:T(8,128)(2,1)} %bitcast.38), channel_id=1, source_target_pairs={{0,38},{2,0},{4,2},{6,4},{32,6},{34,32},{36,34},{38,36},{1,39},{3,... | collective-permute-start | bytes 921608 | tf_op jit(solution)/shard_map/ppermute | solution.py:307
  8.0 5.0 %all-to-all-start = ((bf16[4,15,32,320]{3,2,1,0:T(8,128)(2,1)}), bf16[4,15,32,320]{3,2,1,0:T(8,128)(2,1)S(1)}, u32[]{:S(2)}, u32[]{:S(2)}) async-start(bf16[4,15,32,320]{3,2,1,0:T(8,128)(2,1)} %bitcast.45), calls=%async_computation | async-start | bytes 2949120 | tf_op jit(solution)/shard_map/all_to_all | solution.py:320
  13.5 3.0 %constant_dynamic-slice_fusion.1 = (bf16[15,48,320]{2,1,0:T(8,128)(2,1)}, bf16[15,48,320]{2,1,0:T(8,128)(2,1)}, bf16[15,48,320]{2,1,0:T(8,128)(2,1)}, bf16[15,48,320]{2,1,0:T(8,128)(2,1)}) fusion(bf16[15,320,320]{2,1,0:T(8,128)(2,1)} %param.9, s32[]{:T(128)S(6)} %select_n.27, s32[]{:T(128)S(6)} %select_n.26, s32[]{:T(128)S(6)} %select_n.25, s32[]{:T(128)S(6)} %select_n.24), kind=kLoop, calls=%fused_computation.3 | loop fusion | bytes 3686416 | tf_op jit(solution)/shard_map/dynamic_slice | solution.py:312
  18.3 3.6 %pairs.4 = (f32[8,15,128]{2,1,0:T(8,128)S(1)}, f32[8,8,128]{2,1,0:T(8,128)S(1)}, bf16[15,128,320]{2,1,0:T(8,128)(2,1)S(1)}) custom-call(bf16[15,320,120]{2,1,0:T(8,128)(2,1)S(1)} %bitcast.43, bf16[4,320,120]{2,1,0:T(8,128)(2,1)S(1)} %bitcast.41, bf16[4,320,120]{2,1,0:T(8,128)(2,1)S(1)} %copy-done.5), custom_call_target="tpu_custom_call" | custom-call | flops 1 | bytes 1 | tf_op jit(solution)/shard_map/pairs/pallas_call | solution.py:98
  24.4 2.7 %collective-permute-start.8 = (bf16[15,48,320]{2,1,0:T(8,128)(2,1)}, bf16[15,48,320]{2,1,0:T(8,128)(2,1)}, u32[]{:S(2)}, u32[]{:S(2)}) collective-permute-start(bf16[15,48,320]{2,1,0:T(8,128)(2,1)} %get-tuple-element.54), channel_id=1, source_target_pairs={{0,128},{64,192},{128,0},{192,64},{1,129},{65,193},{129,1},{193,65... | collective-permute-start | bytes 1382408 | tf_op jit(solution)/shard_map/ppermute | solution.py:316
  27.2 2.4 %collective-permute-start.9 = (bf16[15,48,320]{2,1,0:T(8,128)(2,1)}, bf16[15,48,320]{2,1,0:T(8,128)(2,1)}, u32[]{:S(2)}, u32[]{:S(2)}) collective-permute-start(bf16[15,48,320]{2,1,0:T(8,128)(2,1)} %get-tuple-element.53), channel_id=1, source_target_pairs={{0,192},{64,0},{128,64},{192,128},{1,193},{65,1},{129,65},{193,129... | collective-permute-start | bytes 1382408 | tf_op jit(solution)/shard_map/ppermute | solution.py:316
  32.4 4.1 %pairs.7 = (f32[8,15,128]{2,1,0:T(8,128)S(1)}, f32[8,8,128]{2,1,0:T(8,128)S(1)}) custom-call(bf16[15,128,320]{2,1,0:T(8,128)(2,1)S(1)} %get-tuple-element.26.refs_0_, bf16[4,320,120]{2,1,0:T(8,128)(2,1)} %collective-permute-done.5.refs_1_, bf16[4,320,120]{2,1,0:T(8,128)(2,1)S(1)} %copy-done.7), custom_call_target="tpu_custom_call" | custom-call | flops 1 | bytes 1 | tf_op jit(solution)/shard_map/pairs/pallas_call | solution.py:98
  36.5 4.2 %pairs.6 = (f32[8,15,128]{2,1,0:T(8,128)S(1)}, f32[8,8,128]{2,1,0:T(8,128)S(1)}) custom-call(bf16[15,128,320]{2,1,0:T(8,128)(2,1)S(1)} %get-tuple-element.26.refs_0_, bf16[4,320,120]{2,1,0:T(8,128)(2,1)} %collective-permute-done.3.refs_1_, bf16[4,320,120]{2,1,0:T(8,128)(2,1)} %collective-permute-done.4.refs_2_), custom_call_target="tpu_custom_call" | custom-call | flops 1 | bytes 1 | tf_op jit(solution)/shard_map/pairs/pallas_call | solution.py:98
  40.7 4.2 %pairs.5 = (f32[8,15,128]{2,1,0:T(8,128)S(1)}, f32[8,8,128]{2,1,0:T(8,128)S(1)}) custom-call(bf16[15,128,320]{2,1,0:T(8,128)(2,1)S(1)} %get-tuple-element.26.refs_0_, bf16[4,320,120]{2,1,0:T(8,128)(2,1)} %collective-permute-done.1.refs_1_, bf16[4,320,120]{2,1,0:T(8,128)(2,1)} %collective-permute-done.2.refs_2_), custom_call_target="tpu_custom_call" | custom-call | flops 1 | bytes 1 | tf_op jit(solution)/shard_map/pairs/pallas_call | solution.py:98
  44.9 1.7 %message.1 = bf16[16,80,128]{2,1,0:T(8,128)(2,1)} custom-call(s32[2]{0:T(128)S(1)} %pad_add_fusion.place_ref, f32[8,15,128]{2,1,0:T(8,128)S(1)} %get-tuple-element.25.refs_0_, f32[8,15,128]{2,1,0:T(8,128)S(1)} %get-tuple-element.28.refs_1_, f32[8,15,128]{2,1,0:T(8,128)S(1)} %get-tuple-element.30.refs_2_, f32[8,15,128]{2,1,0:T(8,128)S(1)} %get-tuple-element.32.refs_3_, ...), custom_call_target="tpu_custom_call" | custom-call | tf_op jit(solution)/shard_map/message/pallas_call | solution.py:145
  46.6 5.2 %collective-permute-done.8.refs_2_ = bf16[15,48,320]{2,1,0:T(8,128)(2,1)} collective-permute-done((bf16[15,48,320]{2,1,0:T(8,128)(2,1)}, bf16[15,48,320]{2,1,0:T(8,128)(2,1)}, u32[]{:S(2)}, u32[]{:S(2)}) %collective-permute-start.8) | collective-permute-done | bytes 460832 | tf_op jit(solution)/shard_map/ppermute | solution.py:316
  51.9 6.9 %all-to-all-start.1 = ((bf16[16,80,128]{2,1,0:T(8,128)(2,1)}), bf16[16,80,128]{2,1,0:T(8,128)(2,1)S(1)}, u32[]{:S(2)}, u32[]{:S(2)}) async-start(bf16[16,80,128]{2,1,0:T(8,128)(2,1)} %message.1), calls=%async_computation.1 | async-start | bytes 655360 | tf_op jit(solution)/shard_map/all_to_all | solution.py:336
  58.8 7.4 %all-to-all-done.1.message_ref = bf16[16,80,128]{2,1,0:T(8,128)(2,1)S(1)} async-done(((bf16[16,80,128]{2,1,0:T(8,128)(2,1)}), bf16[16,80,128]{2,1,0:T(8,128)(2,1)S(1)}, u32[]{:S(2)}, u32[]{:S(2)}) %all-to-all-start.1) | async-done | bytes 327712 | tf_op jit(solution)/shard_map/all_to_all | solution.py:336
  67.3 2.5 %field_rows.4 = bf16[4,4,48,384]{3,2,1,0:T(8,128)(2,1)S(1)} custom-call(s32[6]{0:T(128)S(1)} %stack.86.place_ref, bf16[16,80,128]{2,1,0:T(8,128)(2,1)S(1)} %all-to-all-done.1.message_ref, bf16[15,48,320]{2,1,0:T(8,128)(2,1)S(1)} %copy-done, bf16[15,48,320]{2,1,0:T(8,128)(2,1)} %collective-permute-done.7.refs_1_, ...), custom_call_target="tpu_custom_call" | custom-call | flops 603979776 | bytes 1920000 | tf_op jit(solution)/shard_map/field_rows/pallas_call | solution.py:198
  70.0 2.1 %field_rows.6 = bf16[4,4,32,384]{3,2,1,0:T(8,128)(2,1)} custom-call(s32[6]{0:T(128)S(1)} %stack.93.place_ref, bf16[16,80,128]{2,1,0:T(8,128)(2,1)S(1)} %all-to-all-done.1.message_ref, bf16[4,15,32,320]{3,2,1,0:T(8,128)(2,1)S(1)} %all-to-all-done.refs_0_), custom_call_target="tpu_custom_call" | custom-call | flops 402653184 | bytes 1280000 | tf_op jit(solution)/shard_map/field_rows/pallas_call | solution.py:198
  72.7 3.4 %field_rows.5 = bf16[4,4,48,384]{3,2,1,0:T(8,128)(2,1)} custom-call(s32[6]{0:T(128)S(1)} %stack.84.place_ref, bf16[16,80,128]{2,1,0:T(8,128)(2,1)S(1)} %all-to-all-done.1.message_ref, bf16[15,48,320]{2,1,0:T(8,128)(2,1)S(1)} %copy-done.1, bf16[15,48,320]{2,1,0:T(8,128)(2,1)} %collective-permute-done.7.refs_1_, ...), custom_call_target="tpu_custom_call" | custom-call | flops 603979776 | bytes 1920000 | tf_op jit(solution)/shard_map/field_rows/pallas_call | solution.py:198
  76.0 5.0 %all-to-all-start.2 = ((bf16[4,4,48,384]{3,2,1,0:T(8,128)(2,1)}), bf16[4,4,48,384]{3,2,1,0:T(8,128)(2,1)S(1)}, u32[]{:S(2)}, u32[]{:S(2)}) async-start(bf16[4,4,48,384]{3,2,1,0:T(8,128)(2,1)} %field_rows.5), calls=%async_computation.2 | async-start | bytes 1179648 | tf_op jit(solution)/shard_map/all_to_all | solution.py:351
  81.2 1.8 %field_rows.7 = (bf16[1,4,32,384]{3,2,1,0:T(8,128)(2,1)S(1)}, bf16[1,4,32,384]{3,2,1,0:T(8,128)(2,1)S(1)}, bf16[1,4,32,384]{3,2,1,0:T(8,128)(2,1)S(1)}, bf16[1,4,32,384]{3,2,1,0:T(8,128)(2,1)S(1)}) custom-call(s32[6]{0:T(128)S(1)} %stack.92.place_ref, bf16[16,80,128]{2,1,0:T(8,128)(2,1)S(1)} %all-to-all-done.1.message_ref, ...), custom_call_target="tpu_custom_call" | custom-call | flops 402653184 | bytes 1280000 | tf_op jit(solution)/shard_map/field_rows/pallas_call | solution.py:198
  83.3 2.4 %collective-permute-start.13 = (bf16[1,4,32,384]{3,2,1,0:T(8,128)(2,1)S(1)}, bf16[1,4,32,384]{3,2,1,0:T(8,128)(2,1)S(1)}, u32[]{:S(2)}, u32[]{:S(2)}) collective-permute-start(bf16[1,4,32,384]{3,2,1,0:T(8,128)(2,1)S(1)} %get-tuple-element.40), channel_id=1, source_target_pairs={{0,128},{64,192},{128,0},{192,64},{1,129},{65,193},{129,1},{193,65... | collective-permute-start | bytes 294920 | tf_op jit(solution)/shard_map/ppermute | solution.py:349
  87.0 3.8 %collective-permute-done.12.refs_2_ = bf16[1,4,32,384]{3,2,1,0:T(8,128)(2,1)S(1)} collective-permute-done((bf16[1,4,32,384]{3,2,1,0:T(8,128)(2,1)S(1)}, bf16[1,4,32,384]{3,2,1,0:T(8,128)(2,1)S(1)}, u32[]{:S(2)}, u32[]{:S(2)}) %collective-permute-start.12) | collective-permute-done | bytes 98336 | tf_op jit(solution)/shard_map/ppermute | solution.py:349
  91.6 21.1 %all_to_all.25.in_ref = bf16[8,80,384]{2,1,0:T(8,128)(2,1)S(1)} all-to-all(bf16[8,80,384]{2,1,0:T(8,128)(2,1)S(1)} %sum_plane.1), channel_id=1, replica_groups=mesh['x'=4,'zh'=2,'y'=4,'zl'=4,'core'=2] {'zh','zl'}, dimensions={0} | all-to-all | bytes 983040 | tf_op jit(solution)/shard_map/all_to_all | solution.py:358
  113.7 7.8 %all-to-all-start.4 = ((bf16[16,80,384]{2,1,0:T(8,128)(2,1)}), bf16[16,80,384]{2,1,0:T(8,128)(2,1)S(1)}, u32[]{:S(2)}, u32[]{:S(2)}) async-start(bf16[16,80,384]{2,1,0:T(8,128)(2,1)} %get-tuple-element.42), calls=%async_computation.4 | async-start | bytes 1966080 | tf_op jit(solution)/shard_map/all_to_all | solution.py:361
  122.4 9.0 %collective-permute-done.15 = bf16[16,40,120]{2,1,0:T(8,128)(2,1)S(1)} collective-permute-done((bf16[16,40,120]{2,1,0:T(8,128)(2,1)S(1)}, bf16[16,40,120]{2,1,0:T(8,128)(2,1)S(1)}, u32[]{:S(2)}, u32[]{:S(2)}) %collective-permute-start.15) | collective-permute-done | bytes 153632 | tf_op jit(solution)/shard_map/ppermute | solution.py:353
  134.2 2.7 %taylor.1 = bf16[4,320,120]{2,1,0:T(8,128)(2,1)S(1)} custom-call(bf16[16,80,384]{2,1,0:T(8,128)(2,1)S(1)} %all-to-all-done.4.in_ref, bf16[4,320,120]{2,1,0:T(8,128)(2,1)S(1)} %copy.25.walkers_ref), custom_call_target="tpu_custom_call" | custom-call | tf_op jit(solution)/shard_map/taylor/pallas_call | solution.py:285
  (80 shorter events, 18.7 us)
Async XLA Ops:
  0.6 6.1 %slice-start = ((bf16[15,320,320]{2,1,0:T(8,128)(2,1)}), bf16[15,128,320]{2,1,0:T(8,128)(2,1)S(1)}, s32[]{:S(2)}) async-start(bf16[15,320,320]{2,1,0:T(8,128)(2,1)} %param.9), calls=%async_computation.5 | async-start | bytes 2949120 | tf_op jit(solution)/shard_map/slice | solution.py:318
  0.6 16.0 %collective-permute-start = (bf16[4,320,120]{2,1,0:T(8,128)(2,1)}, bf16[4,320,120]{2,1,0:T(8,128)(2,1)S(1)}, u32[]{:S(2)}, u32[]{:S(2)}) collective-permute-start(bf16[4,320,120]{2,1,0:T(8,128)(2,1)} %bitcast.37), channel_id=1, source_target_pairs={{0,1},{1,0},{2,3},{3,2},{4,5},{5,4},{6,7},{7,6},{8,9},{9,8},{10,11... | collective-permute-start | bytes 921608 | tf_op jit(solution)/shard_map/ppermute | solution.py:303
  0.7 21.1 %collective-permute-start.5 = (bf16[4,320,120]{2,1,0:T(8,128)(2,1)}, bf16[4,320,120]{2,1,0:T(8,128)(2,1)}, u32[]{:S(2)}, u32[]{:S(2)}) collective-permute-start(bf16[4,320,120]{2,1,0:T(8,128)(2,1)} %bitcast.38), channel_id=1, source_target_pairs={{0,38},{2,0},{4,2},{6,4},{32,6},{34,32},{36,34},{38,36},{1,39},{3,... | collective-permute-start | bytes 921608 | tf_op jit(solution)/shard_map/ppermute | solution.py:307
  8.0 43.9 %all-to-all-start = ((bf16[4,15,32,320]{3,2,1,0:T(8,128)(2,1)}), bf16[4,15,32,320]{3,2,1,0:T(8,128)(2,1)S(1)}, u32[]{:S(2)}, u32[]{:S(2)}) async-start(bf16[4,15,32,320]{3,2,1,0:T(8,128)(2,1)} %bitcast.45), calls=%async_computation | async-start | bytes 2949120 | tf_op jit(solution)/shard_map/all_to_all | solution.py:320
  13.0 14.1 %collective-permute-start.3 = (bf16[4,320,120]{2,1,0:T(8,128)(2,1)S(1)}, bf16[4,320,120]{2,1,0:T(8,128)(2,1)}, u32[]{:S(2)}, u32[]{:S(2)}) collective-permute-start(bf16[4,320,120]{2,1,0:T(8,128)(2,1)S(1)} %bitcast.39), channel_id=1, source_target_pairs={{0,4},{1,37},{2,6},{3,39},{4,32},{5,1},{6,34},{7,3},{32,36},{33,5}... | collective-permute-start | bytes 921608 | tf_op jit(solution)/shard_map/ppermute | solution.py:309
  13.0 16.9 %collective-permute-start.1 = (bf16[4,320,120]{2,1,0:T(8,128)(2,1)S(1)}, bf16[4,320,120]{2,1,0:T(8,128)(2,1)}, u32[]{:S(2)}, u32[]{:S(2)}) collective-permute-start(bf16[4,320,120]{2,1,0:T(8,128)(2,1)S(1)} %bitcast.40), channel_id=1, source_target_pairs={{0,2},{2,4},{4,6},{6,32},{32,34},{34,36},{36,38},{38,0},{1,3},{3,5... | collective-permute-start | bytes 921608 | tf_op jit(solution)/shard_map/ppermute | solution.py:306
  13.5 17.8 %copy-start.9 = (bf16[4,10,120]{2,0,1:T(4,128)(2,1)S(1)}, bf16[4,10,120]{2,0,1:T(4,128)(2,1)}, u32[]{:S(2)}) copy-start(bf16[4,10,120]{2,0,1:T(4,128)(2,1)} %param.7) | copy-start | bytes 28804
  16.6 14.5 %copy-start.10 = (f32[15,32]{1,0:T(8,128)S(1)}, f32[15,32]{1,0:T(8,128)}, u32[]{:S(2)}) copy-start(f32[15,32]{1,0:T(8,128)} %param.10) | copy-start | bytes 5764
  21.9 8.0 %collective-permute-start.6 = (bf16[4,320,120]{2,1,0:T(8,128)(2,1)}, bf16[4,320,120]{2,1,0:T(8,128)(2,1)S(1)}, u32[]{:S(2)}, u32[]{:S(2)}) collective-permute-start(bf16[4,320,120]{2,1,0:T(8,128)(2,1)} %collective-permute-done.5.refs_1_), channel_id=1, source_target_pairs={{0,1},{1,0},{2,3},{3,2},{4,5},{5,4},{6,7},{7,6},{8,9},{9,8},{10,11... | collective-permute-start | bytes 921608 | tf_op jit(solution)/shard_map/ppermute | solution.py:303
  23.0 23.7 %collective-permute-start.7 = (bf16[15,48,320]{2,1,0:T(8,128)(2,1)}, bf16[15,48,320]{2,1,0:T(8,128)(2,1)}, u32[]{:S(2)}, u32[]{:S(2)}) collective-permute-start(bf16[15,48,320]{2,1,0:T(8,128)(2,1)} %get-tuple-element.55), channel_id=1, source_target_pairs={{0,64},{64,128},{128,192},{192,0},{1,65},{65,129},{129,193},{193,1... | collective-permute-start | bytes 1382408 | tf_op jit(solution)/shard_map/ppermute | solution.py:316
  24.4 27.4 %collective-permute-start.8 = (bf16[15,48,320]{2,1,0:T(8,128)(2,1)}, bf16[15,48,320]{2,1,0:T(8,128)(2,1)}, u32[]{:S(2)}, u32[]{:S(2)}) collective-permute-start(bf16[15,48,320]{2,1,0:T(8,128)(2,1)} %get-tuple-element.54), channel_id=1, source_target_pairs={{0,128},{64,192},{128,0},{192,64},{1,129},{65,193},{129,1},{193,65... | collective-permute-start | bytes 1382408 | tf_op jit(solution)/shard_map/ppermute | solution.py:316
  27.2 24.7 %collective-permute-start.9 = (bf16[15,48,320]{2,1,0:T(8,128)(2,1)}, bf16[15,48,320]{2,1,0:T(8,128)(2,1)}, u32[]{:S(2)}, u32[]{:S(2)}) collective-permute-start(bf16[15,48,320]{2,1,0:T(8,128)(2,1)} %get-tuple-element.53), channel_id=1, source_target_pairs={{0,192},{64,0},{128,64},{192,128},{1,193},{65,1},{129,65},{193,129... | collective-permute-start | bytes 1382408 | tf_op jit(solution)/shard_map/ppermute | solution.py:316
  29.9 6.6 %collective-permute-start.4 = (bf16[4,320,120]{2,1,0:T(8,128)(2,1)}, bf16[4,320,120]{2,1,0:T(8,128)(2,1)}, u32[]{:S(2)}, u32[]{:S(2)}) collective-permute-start(bf16[4,320,120]{2,1,0:T(8,128)(2,1)} %collective-permute-done.3.refs_1_), channel_id=1, source_target_pairs={{0,1},{1,0},{2,3},{3,2},{4,5},{5,4},{6,7},{7,6},{8,9},{9,8},{10,11... | collective-permute-start | bytes 921608 | tf_op jit(solution)/shard_map/ppermute | solution.py:303
  30.6 10.1 %collective-permute-start.2 = (bf16[4,320,120]{2,1,0:T(8,128)(2,1)}, bf16[4,320,120]{2,1,0:T(8,128)(2,1)}, u32[]{:S(2)}, u32[]{:S(2)}) collective-permute-start(bf16[4,320,120]{2,1,0:T(8,128)(2,1)} %collective-permute-done.1.refs_1_), channel_id=1, source_target_pairs={{0,1},{1,0},{2,3},{3,2},{4,5},{5,4},{6,7},{7,6},{8,9},{9,8},{10,11... | collective-permute-start | bytes 921608 | tf_op jit(solution)/shard_map/ppermute | solution.py:303
  51.9 14.4 %all-to-all-start.1 = ((bf16[16,80,128]{2,1,0:T(8,128)(2,1)}), bf16[16,80,128]{2,1,0:T(8,128)(2,1)S(1)}, u32[]{:S(2)}, u32[]{:S(2)}) async-start(bf16[16,80,128]{2,1,0:T(8,128)(2,1)} %message.1), calls=%async_computation.1 | async-start | bytes 655360 | tf_op jit(solution)/shard_map/all_to_all | solution.py:336
  69.8 2.9 %collective-permute-start.10 = (bf16[4,4,48,384]{3,2,1,0:T(8,128)(2,1)S(1)}, bf16[4,4,48,384]{3,2,1,0:T(8,128)(2,1)S(1)}, u32[]{:S(2)}, u32[]{:S(2)}) collective-permute-start(bf16[4,4,48,384]{3,2,1,0:T(8,128)(2,1)S(1)} %field_rows.4), channel_id=1, source_target_pairs={{0,1},{1,0},{2,3},{3,2},{4,5},{5,4},{6,7},{7,6},{8,9},{9,8},{10,11... | collective-permute-start | bytes 1769480 | tf_op jit(solution)/shard_map/ppermute | solution.py:303
  72.1 9.1 %collective-permute-start.11 = (bf16[4,4,32,384]{3,2,1,0:T(8,128)(2,1)}, bf16[4,4,32,384]{3,2,1,0:T(8,128)(2,1)}, u32[]{:S(2)}, u32[]{:S(2)}) collective-permute-start(bf16[4,4,32,384]{3,2,1,0:T(8,128)(2,1)} %field_rows.6), channel_id=1, source_target_pairs={{0,1},{1,0},{2,3},{3,2},{4,5},{5,4},{6,7},{7,6},{8,9},{9,8},{10,11... | collective-permute-start | bytes 1179656 | tf_op jit(solution)/shard_map/ppermute | solution.py:303
  76.0 15.4 %all-to-all-start.2 = ((bf16[4,4,48,384]{3,2,1,0:T(8,128)(2,1)}), bf16[4,4,48,384]{3,2,1,0:T(8,128)(2,1)S(1)}, u32[]{:S(2)}, u32[]{:S(2)}) async-start(bf16[4,4,48,384]{3,2,1,0:T(8,128)(2,1)} %field_rows.5), calls=%async_computation.2 | async-start | bytes 1179648 | tf_op jit(solution)/shard_map/all_to_all | solution.py:351
  83.0 7.8 %collective-permute-start.12 = (bf16[1,4,32,384]{3,2,1,0:T(8,128)(2,1)S(1)}, bf16[1,4,32,384]{3,2,1,0:T(8,128)(2,1)S(1)}, u32[]{:S(2)}, u32[]{:S(2)}) collective-permute-start(bf16[1,4,32,384]{3,2,1,0:T(8,128)(2,1)S(1)} %get-tuple-element.39), channel_id=1, source_target_pairs={{0,64},{64,128},{128,192},{192,0},{1,65},{65,129},{129,193},{193,1... | collective-permute-start | bytes 294920 | tf_op jit(solution)/shard_map/ppermute | solution.py:349
  83.3 7.5 %collective-permute-start.13 = (bf16[1,4,32,384]{3,2,1,0:T(8,128)(2,1)S(1)}, bf16[1,4,32,384]{3,2,1,0:T(8,128)(2,1)S(1)}, u32[]{:S(2)}, u32[]{:S(2)}) collective-permute-start(bf16[1,4,32,384]{3,2,1,0:T(8,128)(2,1)S(1)} %get-tuple-element.40), channel_id=1, source_target_pairs={{0,128},{64,192},{128,0},{192,64},{1,129},{65,193},{129,1},{193,65... | collective-permute-start | bytes 294920 | tf_op jit(solution)/shard_map/ppermute | solution.py:349
  85.7 5.7 %collective-permute-start.14 = (bf16[1,4,32,384]{3,2,1,0:T(8,128)(2,1)S(1)}, bf16[1,4,32,384]{3,2,1,0:T(8,128)(2,1)S(1)}, u32[]{:S(2)}, u32[]{:S(2)}) collective-permute-start(bf16[1,4,32,384]{3,2,1,0:T(8,128)(2,1)S(1)} %get-tuple-element.41), channel_id=1, source_target_pairs={{0,192},{64,0},{128,64},{192,128},{1,193},{65,1},{129,65},{193,129... | collective-permute-start | bytes 294920 | tf_op jit(solution)/shard_map/ppermute | solution.py:349
  113.7 20.5 %all-to-all-start.4 = ((bf16[16,80,384]{2,1,0:T(8,128)(2,1)}), bf16[16,80,384]{2,1,0:T(8,128)(2,1)S(1)}, u32[]{:S(2)}, u32[]{:S(2)}) async-start(bf16[16,80,384]{2,1,0:T(8,128)(2,1)} %get-tuple-element.42), calls=%async_computation.4 | async-start | bytes 1966080 | tf_op jit(solution)/shard_map/all_to_all | solution.py:361
  121.5 9.9 %collective-permute-start.15 = (bf16[16,40,120]{2,1,0:T(8,128)(2,1)S(1)}, bf16[16,40,120]{2,1,0:T(8,128)(2,1)S(1)}, u32[]{:S(2)}, u32[]{:S(2)}) collective-permute-start(bf16[16,40,120]{2,1,0:T(8,128)(2,1)S(1)} %slice.16), channel_id=1, source_target_pairs={{0,32},{32,0},{1,33},{33,1},{2,34},{34,2},{3,35},{35,3},{4,36},{36... | collective-permute-start | bytes 460808 | tf_op jit(solution)/shard_map/ppermute | solution.py:353
  122.4 9.4 %collective-permute-start.16 = (f32[1,128]{1,0:T(1,128)S(1)}, f32[1,128]{1,0:T(1,128)S(1)}, u32[]{:S(2)}, u32[]{:S(2)}) collective-permute-start(f32[1,128]{1,0:T(1,128)S(1)} %get-tuple-element.44), channel_id=1, source_target_pairs={{0,1},{1,0},{2,3},{3,2},{4,5},{5,4},{6,7},{7,6},{8,9},{9,8},{10,11... | collective-permute-start | bytes 1544 | tf_op jit(solution)/shard_map/ppermute | solution.py:303
  (9 other events, 20.4 us)

commit v4 on v3

v4 whole, which is shorter than its diff:
```python
import functools

import jax
import jax.numpy as jnp
from jax import lax
from jax.experimental import pallas as pl
from jax.experimental.pallas import tpu as pltpu
from jax.sharding import Mesh, PartitionSpec as P

ORDER = 4
step_root = 0.1

AXES = ("x", "zh", "y", "zl", "core")
SIZES = (4, 2, 4, 4, 2)
Z = ("zh", "zl")
HIGH = ("x", "zh", "y")
LOW = ("zl", "core")

ROW = 128
WIDE = 384
TILE = 16
f32 = jnp.float32
bf16 = jnp.bfloat16
CONTRACT_LAST = (((1,), (1,)), ((), ()))


def after(value, *others):
    return lax.optimization_barrier((value, *others))[0]


def ring(count, shift):
    return [(i, (i + shift) % count) for i in range(count)]


def parts_of(value):
    high = value.astype(bf16).astype(f32)
    rest = value - high
    middle = rest.astype(bf16).astype(f32)
    low = (rest - middle).astype(bf16).astype(f32)
    row = lax.broadcasted_iota(jnp.int32, (TILE, value.shape[1]), 0)
    zero = jnp.zeros((TILE, value.shape[1]), f32)
    return jnp.where(
        row == 0, high, jnp.where(row == 1, middle, jnp.where(row == 2, low, zero))
    )


def pair_kernel(vectors, first, count, *refs):
    inputs, (trace_ref, square_ref) = refs[:count], refs[count : count + 2]
    held, semaphores = refs[-1 - count : -1], refs[-1]
    loads = [
        pltpu.make_async_copy(src, dst, semaphores.at[i])
        for i, (src, dst) in enumerate(zip(inputs, held, strict=True))
    ]
    for load in loads:
        load.start()
    loads[0].wait()
    rot_ref, greens = held[0], held[1:]
    if first:
        rot_ref = refs[count + 2]
        for g in range(vectors):
            rot_ref[g] = widen(held[0][g]).T
    orbitals = rot_ref.shape[2]
    eye = (
        lax.broadcasted_iota(jnp.int32, (ROW, ROW), 0)
        == lax.broadcasted_iota(jnp.int32, (ROW, ROW), 1)
    ).astype(f32)
    base = 0
    for load, green_ref in zip(loads[1:], greens, strict=True):
        load.wait()
        count = green_ref.shape[0] // 2

        def two_walkers(i, carry, green_ref=green_ref, base=base):
            green = jnp.concatenate([widen(green_ref[2 * i]), widen(green_ref[2 * i + 1])], axis=1)
            rot = rot_ref[...].reshape(vectors * ROW, orbitals)
            pairs = jnp.dot(rot, green, preferred_element_type=f32)
            for w in range(2):
                total = jnp.zeros((8, ROW), f32)
                for g in range(vectors):
                    block = pairs[g * ROW : (g + 1) * ROW, w * ROW : (w + 1) * ROW]
                    total = total + jnp.sum((block * block.T).reshape(ROW // 8, 8, ROW), axis=0)
                    trace_ref[base + 2 * i + w, pl.ds(g, 1), :] = jnp.sum(
                        block * eye, axis=0, keepdims=True
                    )
                square_ref[base + 2 * i + w] = total
            return carry

        if count == 1:
            two_walkers(0, 0)
        else:
            lax.fori_loop(0, count, two_walkers, 0)
        base += 2 * count


def widen(a):
    return jnp.concatenate([a, jnp.zeros((a.shape[0], ROW - a.shape[1]), a.dtype)], axis=1)


def pair_sums(rot, greens, first):
    vectors = rot.shape[0]
    walkers = sum(g.shape[0] for g in greens)
    out_shape = [
        jax.ShapeDtypeStruct((walkers, vectors, ROW), f32),
        jax.ShapeDtypeStruct((walkers, 8, ROW), f32),
    ]
    if first:
        out_shape.append(jax.ShapeDtypeStruct((vectors, ROW, rot.shape[1]), bf16))
    return pl.pallas_call(
        functools.partial(pair_kernel, vectors, first, 1 + len(greens)),
        out_shape=out_shape,
        in_specs=[pl.BlockSpec(memory_space=pl.ANY)] * (1 + len(greens)),
        scratch_shapes=[pltpu.VMEM(a.shape, bf16) for a in (rot, *greens)]
        + [pltpu.SemaphoreType.DMA((1 + len(greens),))],
        compiler_params=pltpu.CompilerParams(vmem_limit_bytes=56 * 2**20),
        cost_estimate=pl.CostEstimate(flops=1, bytes_accessed=1, transcendentals=0),
        name="pairs",
    )(rot, *greens)


def message_kernel(vector_total, place_ref, *refs):
    fields_ref, green_ref, one_body_ref, give_ref, keep_ref = refs[4:]
    traces, squares = ([ref.at[w] for ref in refs[k : k + 2] for w in range(ref.shape[0])] for k in (0, 2))
    zl, core = place_ref[0], place_ref[1]
    vectors = fields_ref.shape[0]
    lanes = lax.broadcasted_iota(jnp.int32, (vectors, 128), 1)
    lane = lax.broadcasted_iota(jnp.int32, (1, 128), 1)
    intersection = jnp.zeros((vectors, 128), f32)
    exchange = jnp.zeros((1, 128), f32)
    single = jnp.zeros((1, 128), f32)
    one_body = one_body_ref[...].astype(f32)
    for d in range(4):
        for w in range(8):
            owner = core if w < 4 else 1 - core
            index = lax.rem(zl + 4 - d, 4) * 8 + owner * 4 + w % 4
            trace = jnp.sum(traces[8 * d + w][...], axis=1, keepdims=True)
            intersection = jnp.where(lanes == index, trace, intersection)
            exchange = jnp.where(lane == index, jnp.sum(squares[8 * d + w][...], keepdims=True), exchange)
            if d == 0 and w < 4:
                own = jnp.sum(green_ref[w].astype(f32) * one_body, keepdims=True)
                single = jnp.where(lane == index, own * (2.0 / 32.0), single)
    bias = 2.0 * step_root * intersection
    noise = jnp.concatenate([fields_ref[...], jnp.zeros((vectors, 96), f32)], axis=1)
    weight = jnp.sum(noise * bias - 0.5 * bias * bias, axis=0, keepdims=True) / vector_total**0.5
    energy = jnp.sum(2.0 * intersection * intersection, axis=0, keepdims=True) - exchange
    energy = energy / vector_total + single
    shifted = jnp.concatenate([noise - bias, jnp.zeros((128 - vectors, 128), f32)]).T.astype(bf16)
    row = lax.broadcasted_iota(jnp.int32, (TILE, 128), 0)
    column = lax.broadcasted_iota(jnp.int32, (TILE, 128), 1)

    def rows_of(owner):
        source = jnp.bitwise_and(row, 3) * 8 + owner * 4 + lax.shift_right_logical(row, 2)
        return jnp.dot((column == source).astype(bf16), shifted, preferred_element_type=f32)

    scalars = parts_of(pltpu.roll(energy, 64, 1) + pltpu.roll(weight, 96, 1))
    give_ref[...] = rows_of(1 - core).astype(bf16)
    keep_ref[...] = (rows_of(core) + scalars).astype(bf16)


def messages(place, sums, fields, green, one_body):
    vectors = fields.shape[0]
    return pl.pallas_call(
        functools.partial(message_kernel, vectors * 256),
        out_shape=[jax.ShapeDtypeStruct((TILE, 128), bf16)] * 2,
        in_specs=[pl.BlockSpec(memory_space=pltpu.SMEM)]
        + [pl.BlockSpec(memory_space=pltpu.VMEM)] * 7,
        compiler_params=pltpu.CompilerParams(vmem_limit_bytes=56 * 2**20),
        name="message",
    )(place, *[p[0] for p in sums], *[p[1] for p in sums], fields, green, one_body)


def copies_kernel(place_ref, keep_ref, got_ref, near_ref, other_ref, out_ref):
    rows = near_ref.shape[0]
    near = pl.ds(pl.multiple_of(TILE + rows * place_ref[0], TILE), rows)
    other = pl.ds(pl.multiple_of(TILE + rows * (1 - place_ref[0]), TILE), rows)
    got = pltpu.roll(got_ref[...].astype(f32), TILE, 1)
    top = (keep_ref[...].astype(f32) + got).astype(bf16)
    for k in range(out_ref.shape[0]):
        out_ref[k, 0:TILE] = top
        out_ref[k, near] = near_ref[...]
        out_ref[k, other] = other_ref[...]


def copies(place, keep, got, near, other):
    return pl.pallas_call(
        copies_kernel,
        out_shape=jax.ShapeDtypeStruct((16, TILE + 2 * near.shape[0], 128), bf16),
        in_specs=[pl.BlockSpec(memory_space=pltpu.SMEM)]
        + [pl.BlockSpec(memory_space=pltpu.VMEM)] * 4,
        compiler_params=pltpu.CompilerParams(vmem_limit_bytes=16 * 2**20),
        name="copies",
    )(place, keep, got, near, other)


def field_kernel(vectors, place_ref, message_ref, *refs):
    inputs = [ref for ref in refs if len(ref.shape) == 3 or ref.shape[1] == vectors]
    outs = [out.at[i] for out in refs[len(inputs) :] for i in range(out.shape[0])]
    blocks = []
    for ref in inputs:
        blocks += [ref] if len(ref.shape) == 3 else [ref.at[k] for k in range(4)]
    rows, orbitals = blocks[0].shape[1:]
    depth = vectors * TILE
    lane = lax.broadcasted_iota(jnp.int32, (ROW, depth), 0)
    vector = lax.shift_right_logical(lax.broadcasted_iota(jnp.int32, (ROW, depth), 1), 4)
    same = (
        jnp.bitwise_and(lax.broadcasted_iota(jnp.int32, (TILE * TILE, depth), 0), TILE - 1)
        == jnp.bitwise_and(lax.broadcasted_iota(jnp.int32, (TILE * TILE, depth), 1), TILE - 1)
    )
    weights = []
    for b in range(8):
        shifted = message_ref[place_ref[b % 4], 0:TILE, :].astype(f32)
        shifted = pltpu.roll(shifted, place_ref[4], 0).astype(bf16)
        spread = (lane == vector + TILE * (b // 4)).astype(bf16)
        wide = jnp.dot(shifted, spread, preferred_element_type=f32)
        wide = jnp.broadcast_to(wide[:, None, :], (TILE, TILE, depth)).reshape(TILE * TILE, depth)
        weights.append(jnp.where(same, wide, 0.0).astype(bf16))
    for out_ref in outs:
        out_ref[:, :, 256:WIDE] = jnp.zeros((4, rows, WIDE - 256), bf16)
    for t in range(rows // TILE):
        here = slice(t * TILE, (t + 1) * TILE)
        total = jnp.zeros((TILE * TILE, orbitals), f32)
        for b, block_ref in enumerate(blocks):
            block = block_ref[:, here, :].reshape(depth, orbitals)
            total = total + jnp.dot(weights[b], block, preferred_element_type=f32)
        total = (step_root * total).astype(bf16).reshape(TILE, TILE, orbitals)
        for w in range(TILE):
            outs[w // 4][w % 4, here, 0:orbitals] = total[w]


def field_rows(place, message, blocks, pieces):
    vectors, rows, _ = blocks[0].shape[-3:]
    return pl.pallas_call(
        functools.partial(field_kernel, vectors),
        out_shape=[jax.ShapeDtypeStruct((4 // pieces, 4, rows, WIDE), bf16)] * pieces,
        in_specs=[pl.BlockSpec(memory_space=pltpu.SMEM)]
        + [pl.BlockSpec(memory_space=pltpu.VMEM)] * (1 + len(blocks)),
        compiler_params=pltpu.CompilerParams(vmem_limit_bytes=20 * 2**20),
        cost_estimate=pl.CostEstimate(
            flops=rows * 256 * 384 * 256, bytes_accessed=rows * 40000, transcendentals=0
        ),
        name="field_rows",
    )(place, message, *blocks)


def sum_kernel(copies, message_ref, *refs):
    upper = lax.broadcasted_iota(jnp.int32, (TILE, 128), 1) >= 64
    scalars = message_ref[0, 0:TILE].astype(f32)
    for s in range(1, message_ref.shape[0]):
        scalars = scalars + message_ref[s, 0:TILE].astype(f32)
    scalars = parts_of(jnp.sum(scalars, axis=0, keepdims=True))
    out_ref = refs[-1]
    pieces = [ref.at[i] for ref in refs[:-1] for i in range(ref.shape[0])]
    firsts, seconds = pieces[:4], pieces[4:]
    groups, rows = firsts[0].shape[:2]
    for g in range(groups):
        total = firsts[0][g].astype(f32)
        below = seconds[0][g].astype(f32)
        for s in range(1, 4):
            total = total + firsts[s][g].astype(f32)
            below = below + seconds[s][g].astype(f32)
        corner = jnp.where(upper, scalars, total[0:TILE, 256:WIDE]).astype(bf16)
        total, below = total.astype(bf16), below.astype(bf16)
        for k in range(g, copies, groups):
            out_ref[k, 0:rows] = total
            out_ref[k, rows:] = below
            out_ref[k, 0:TILE, 256:WIDE] = corner


def sum_second_axis(message, first, second):
    rows, wide = first[0].shape[2] + second[0].shape[2], first[0].shape[3]
    return pl.pallas_call(
        functools.partial(sum_kernel, 8),
        out_shape=jax.ShapeDtypeStruct((8, rows, wide), bf16),
        compiler_params=pltpu.CompilerParams(vmem_limit_bytes=16 * 2**20),
        name="sum_plane",
    )(message, *first, *second)


def last_kernel(in_ref, out_ref, scalars_ref):
    total = in_ref[0].astype(f32)
    for s in range(1, in_ref.shape[0]):
        total = total + in_ref[s].astype(f32)
    rounded = total.astype(bf16)
    scalars_ref[...] = jnp.sum(total[0:TILE, 256:WIDE], axis=0, keepdims=True)
    for k in range(out_ref.shape[0]):
        out_ref[k] = rounded


def sum_over_z(received):
    _, rows, wide = received.shape
    return pl.pallas_call(
        last_kernel,
        out_shape=(
            jax.ShapeDtypeStruct((16, rows, wide), bf16),
            jax.ShapeDtypeStruct((1, 128), f32),
        ),
        compiler_params=pltpu.CompilerParams(vmem_limit_bytes=16 * 2**20),
        name="sum_z",
    )(received)


def taylor_kernel(first_rows, in_ref, walkers_ref, out_ref):
    orbitals = walkers_ref.shape[1]
    for w in range(4):
        field = jnp.concatenate(
            [in_ref[4 * k + w, 0:first_rows] for k in range(4)]
            + [in_ref[4 * w + k, first_rows:] for k in range(4)]
        )[:, 0:orbitals]
        current = walkers_ref[w]
        total = current.astype(f32)
        for order in range(1, ORDER + 1):
            update = jnp.dot(field, current, preferred_element_type=f32) / order
            total = total + update
            current = update.astype(bf16)
        out_ref[w] = total.astype(bf16)


def taylor(gathered, walkers, first_rows):
    return pl.pallas_call(
        functools.partial(taylor_kernel, first_rows),
        out_shape=jax.ShapeDtypeStruct(walkers.shape, bf16),
        compiler_params=pltpu.CompilerParams(vmem_limit_bytes=16 * 2**20),
        name="taylor",
    )(gathered, walkers)


def on_device(green, walkers, chol_rot, chol_full, fields, one_body_rot):
    x, zh, y, zl, core = (lax.axis_index(a) for a in AXES)
    vectors, electrons, orbitals = chol_rot.shape
    vector_total = vectors * 256
    group = green.shape[0]
    tiles = orbitals // TILE
    first_rows = TILE * (tiles // 8)
    second_rows = orbitals // 4 - first_rows

    def swap(a):
        return lax.ppermute(a, "core", ring(2, 1))

    turned = green.swapaxes(1, 2)
    before = lax.ppermute(turned, Z, ring(8, 1))
    behind = lax.ppermute(turned, Z, ring(8, -1))
    opposite = [(2 * i + c, 2 * ((i + 2 - 4 * c) % 8) + c) for i in range(8) for c in range(2)]
    far = lax.ppermute(turned, Z + ("core",), opposite)

    beside = swap(turned)

    first_pieces = [
        lax.dynamic_slice_in_dim(chol_full, lax.rem(x + k, 4) * first_rows, first_rows, axis=1)
        for k in range(4)
    ]
    second_piece = chol_full[:, 4 * first_rows :].reshape(vectors, 4, second_rows, orbitals)
    second_piece = second_piece.transpose(1, 0, 2, 3)

    rot = after(chol_rot.swapaxes(1, 2), *first_pieces, second_piece)
    own = pair_sums(rot, [turned, beside], True)
    arrived = lax.optimization_barrier((before, far, behind, own[0]))[:3]
    first_blocks = first_pieces[:1] + [
        lax.ppermute(after(first_pieces[k], beside), "x", ring(4, k)) for k in (1, 2, 3)
    ]
    second_block = lax.all_to_all(after(second_piece, *arrived), "y", 0, 0)

    greens = []
    for shard in arrived:
        greens += [shard, swap(shard)]
    sums = [own, pair_sums(own[2], greens, False)]

    share = walkers.shape[1]
    near = walkers.transpose(1, 0, 2).reshape(share * group, electrons)
    near = jnp.pad(near, ((0, -share * group % TILE), (0, 128 - electrons)))
    other = lax.ppermute(after(near, own[0]), "zh", ring(2, 1))
    give, keep = messages(
        jnp.stack([zl, core]).astype(jnp.int32), sums, after(fields, other, *first_blocks), turned, one_body_rot.T
    )
    got = swap(give)
    message = copies(jnp.stack([zh]).astype(jnp.int32), keep, got, near, other)
    message = after(message, second_block)
    message = lax.all_to_all(message, ("x", "y"), 0, 0)

    first_blocks = first_blocks + [swap(after(block, got)) for block in first_blocks]
    second_blocks = [second_block, swap(after(second_block, got))]

    def place(positions, shift):
        return jnp.stack([*positions, shift]).astype(jnp.int32)

    along_x = [4 * lax.rem(x + 4 - k, 4) + y for k in range(4)]
    along_y = [4 * x + k for k in range(4)]
    turn = lax.rem(16 - 4 * x, 16)
    (first,) = field_rows(place(along_x, 0), message, first_blocks, 1)
    first = lax.all_to_all(first, "y", 0, 0)
    second = field_rows(place(along_y, turn), message, second_blocks, 4)
    second = [second[0]] + [lax.ppermute(second[k], "x", ring(4, k)) for k in (1, 2, 3)]
    field = sum_second_axis(message, [first], second)
    field = lax.all_to_all(field, Z, 0, 0)
    whole = message[:, TILE:].reshape(4, 4, 2, near.shape[0], 128)[:, :, :, : share * group, :electrons]
    whole = whole.reshape(4, 4, 2, share, group, electrons).transpose(4, 0, 2, 1, 3, 5)
    whole = whole.reshape(group, orbitals, electrons)
    field, scalars = sum_over_z(field)
    scalars = scalars + swap(scalars)
    field = lax.all_to_all(field, ("x", "y"), 0, 0)
    new = taylor(field, whole, first_rows)
    new = lax.dynamic_slice_in_dim(new, share * (8 * x + 4 * zh + y), share, axis=1)
    return new, scalars[0, 64:96], scalars[0, 96:128]


def solution(mesh):
    split = Mesh(mesh.devices.reshape(SIZES), AXES)
    in_specs = (
        P(LOW, None, None),
        P(LOW, HIGH, None),
        P(HIGH + LOW, None, None),
        P(HIGH + LOW, None, None),
        P(HIGH + LOW, None),
        P(),
    )
    out_specs = (P(LOW, HIGH, None), P(), P())
    return jax.shard_map(
        on_device, mesh=split, in_specs=in_specs, out_specs=out_specs, check_vma=False
    )
```

time: 138 us -> 137 us (level)
  local copies, waits for them, and re-layouts: 11.7 us -> 9.64 us
    ppermute x4, waiting for transfers between devices: 14.3 us -> 0.01 us  [the longest x3 0.01 us: on_device(): lax.ppermute(after(first_pieces[k], beside), 'x', ring(4, k))]
    all_to_all x1, waiting for transfers between devices: 0.75 us -> 9.58 us  [on_device(): field = lax.all_to_all(field, ('x', 'y'), 0, 0)]
    ppermute x7 -> x11, waiting for transfers between devices: 0.02 us -> 4.75 us  [swap(): return lax.ppermute(a, 'core', ring(2, 1))]
    ppermute x1, starting transfers between devices: 5.93 us -> 1.32 us  [on_device(): behind = lax.ppermute(turned, Z, ring(8, -1))]
    ppermute x1, starting transfers between devices: 0.01 us -> 3.27 us  [on_device(): far = lax.ppermute(turned, Z + ('core',), opposite)]
    ppermute x4, starting transfers between devices: 7.51 us -> 10.1 us  [the longest x3 5.66 us: on_device(): lax.ppermute(after(first_pieces[k], beside), 'x', ring(4, k))]
    unnamed x24 -> x11, local copies, waits for them, and re-layouts: 5.15 us -> 3.01 us
    slice x2, local copies, waits for them, and re-layouts: 0.01 us -> 1.62 us  [on_device(): chol_full[:, 4 * first_rows:].reshape(vectors, 4, second_rows, orbitals)]
  transfers between devices with their start and end apart: 21 -> 25, of which waited for: 7 -> 11; matrix products, arithmetic and copies ran while one was open for 5% -> 4% of each run, Pallas kernels for 18% -> 21%
where the time goes in v4:
time: 137 us
  starting transfers between devices  46.3 us (34%)
  Pallas kernels  32.4 us (24%)
  waiting for transfers between devices  26.9 us (20%)
  blocking collectives  19.9 us (15%)
  local copies, waits for them, and re-layouts  9.64 us (7%)
    all_to_all x1, blocking collectives, on_device(): field = lax.all_to_all(field, Z, 0, 0)  19.9 us
    pallas_call x2, Pallas kernels, pair_sums(): pl.pallas_call(functools.partial(pair_kernel, vectors, first, 1 + len(gre...  17.4 us
    all_to_all x1, waiting for transfers between devices, on_device(): field = lax.all_to_all(field, ('x', 'y'), 0, 0)  9.58 us
    pallas_call x2, Pallas kernels, field_rows(): pl.pallas_call(functools.partial(field_kernel, vectors), out_shape=[jax.S...  7.87 us
    all_to_all x1, starting transfers between devices, on_device(): field = lax.all_to_all(field, ('x', 'y'), 0, 0)  6.91 us
    all_to_all x1, waiting for transfers between devices, on_device(): message = lax.all_to_all(message, ('x', 'y'), 0, 0)  6.32 us
    ppermute x3, starting transfers between devices, on_device(): lax.ppermute(after(first_pieces[k], beside), 'x', ring(4, k))  5.66 us
    all_to_all x1, starting transfers between devices, on_device(): message = lax.all_to_all(message, ('x', 'y'), 0, 0)  5.48 us
  transfers between devices with their start and end apart: 25, of which 11 were waited for; matrix products, arithmetic and copies ran while one was open for 4% of the time, Pallas kernels for 21%

profile of v4, /device:TPU:8, one launch (start us, length us, event | category | flops | bytes accessed | tf_op | source)
XLA Modules:
  0.0 136.6 jit_solution(6842316452125761250)
XLA Ops:
  0.7 2.0 %collective-permute-start.1 = (bf16[4,320,120]{2,1,0:T(8,128)(2,1)}, bf16[4,320,120]{2,1,0:T(8,128)(2,1)}, u32[]{:S(2)}, u32[]{:S(2)}) collective-permute-start(bf16[4,320,120]{2,1,0:T(8,128)(2,1)} %bitcast.35), channel_id=1, source_target_pairs={{0,2},{2,4},{4,6},{6,32},{32,34},{34,36},{36,38},{38,0},{1,3},{3,5... | collective-permute-start | bytes 921608 | tf_op jit(solution)/shard_map/ppermute | solution.py:338
  2.7 3.3 %collective-permute-start.2 = (bf16[4,320,120]{2,1,0:T(8,128)(2,1)}, bf16[4,320,120]{2,1,0:T(8,128)(2,1)}, u32[]{:S(2)}, u32[]{:S(2)}) collective-permute-start(bf16[4,320,120]{2,1,0:T(8,128)(2,1)} %bitcast.36), channel_id=1, source_target_pairs={{0,4},{1,37},{2,6},{3,39},{4,32},{5,1},{6,34},{7,3},{32,36},{33,5}... | collective-permute-start | bytes 921608 | tf_op jit(solution)/shard_map/ppermute | solution.py:341
  7.3 1.6 %slice-done = bf16[15,192,320]{2,1,0:T(8,128)(2,1)S(1)} async-done(((bf16[15,320,320]{2,1,0:T(8,128)(2,1)}), bf16[15,192,320]{2,1,0:T(8,128)(2,1)S(1)}, s32[]{:S(2)}) %slice-start) | async-done | bytes 1843224 | tf_op jit(solution)/shard_map/slice | solution.py:349
  8.9 1.6 %copy.15 = bf16[15,4,48,320]{3,2,0,1:T(8,128)(2,1)} copy(bf16[15,4,48,320]{3,2,1,0:T(8,128)(2,1)S(1)} %bitcast.32) | data formatting | bytes 3686400 | tf_op jit(solution)/shard_map/reshape | solution.py:349
  10.5 2.4 %constant_dynamic-slice_fusion.1 = (bf16[15,32,320]{2,1,0:T(8,128)(2,1)}, bf16[15,32,320]{2,1,0:T(8,128)(2,1)}, bf16[15,32,320]{2,1,0:T(8,128)(2,1)}, bf16[15,32,320]{2,1,0:T(8,128)(2,1)S(1)}) fusion(bf16[15,320,320]{2,1,0:T(8,128)(2,1)} %param.9, s32[]{:T(128)S(6)} %select_n.18, s32[]{:T(128)S(6)} %select_n.17, s32[]{:T(128)S(6)} %select_n.16, s32[]{:T(128)S(6)} %select_n.15), kind=kLoop, calls=%fused_computation.2 | loop fusion | bytes 2457616 | tf_op jit(solution)/shard_map/dynamic_slice | solution.py:346
  13.7 6.0 %pairs.2 = (f32[8,15,128]{2,1,0:T(8,128)}, f32[8,8,128]{2,1,0:T(8,128)}, bf16[15,128,320]{2,1,0:T(8,128)(2,1)}) custom-call(bf16[15,320,120]{2,1,0:T(8,128)(2,1)} %bitcast.42, bf16[4,320,120]{2,1,0:T(8,128)(2,1)} %bitcast.38, bf16[4,320,120]{2,1,0:T(8,128)(2,1)} %copy-done.3), custom_call_target="tpu_custom_call" | custom-call | flops 1 | bytes 1 | tf_op jit(solution)/shard_map/pairs/pallas_call | solution.py:107
  20.5 5.0 %all-to-all-start = ((bf16[4,15,48,320]{3,2,1,0:T(8,128)(2,1)}), bf16[4,15,48,320]{3,2,1,0:T(8,128)(2,1)S(1)}, u32[]{:S(2)}, u32[]{:S(2)}) async-start(bf16[4,15,48,320]{3,2,1,0:T(8,128)(2,1)} %bitcast.31), calls=%async_computation | async-start | bytes 4423680 | tf_op jit(solution)/shard_map/all_to_all | solution.py:358
  25.6 1.8 %collective-permute-start.4 = (bf16[4,320,120]{2,1,0:T(8,128)(2,1)}, bf16[4,320,120]{2,1,0:T(8,128)(2,1)}, u32[]{:S(2)}, u32[]{:S(2)}) collective-permute-start(bf16[4,320,120]{2,1,0:T(8,128)(2,1)} %collective-permute-done.1.refs_1_), channel_id=1, source_target_pairs={{0,1},{1,0},{2,3},{3,2},{4,5},{5,4},{6,7},{7,6},{8,9},{9,8},{10,11... | collective-permute-start | bytes 921608 | tf_op jit(solution)/shard_map/ppermute | solution.py:335
  27.8 1.5 %collective-permute-start.8 = (bf16[15,32,320]{2,1,0:T(8,128)(2,1)}, bf16[15,32,320]{2,1,0:T(8,128)(2,1)S(1)}, u32[]{:S(2)}, u32[]{:S(2)}) collective-permute-start(bf16[15,32,320]{2,1,0:T(8,128)(2,1)} %get-tuple-element.42), channel_id=1, source_target_pairs={{0,64},{64,128},{128,192},{192,0},{1,65},{65,129},{129,193},{193,1... | collective-permute-start | bytes 921608 | tf_op jit(solution)/shard_map/ppermute | solution.py:356
  29.3 2.7 %collective-permute-start.9 = (bf16[15,32,320]{2,1,0:T(8,128)(2,1)}, bf16[15,32,320]{2,1,0:T(8,128)(2,1)S(1)}, u32[]{:S(2)}, u32[]{:S(2)}) collective-permute-start(bf16[15,32,320]{2,1,0:T(8,128)(2,1)} %get-tuple-element.43), channel_id=1, source_target_pairs={{0,128},{64,192},{128,0},{192,64},{1,129},{65,193},{129,1},{193,65... | collective-permute-start | bytes 921608 | tf_op jit(solution)/shard_map/ppermute | solution.py:356
  33.5 4.5 %collective-permute-start.7 = (bf16[48,128]{1,0:T(8,128)(2,1)S(1)}, bf16[48,128]{1,0:T(8,128)(2,1)S(1)}, u32[]{:S(2)}, u32[]{:S(2)}) collective-permute-start(bf16[48,128]{1,0:T(8,128)(2,1)S(1)} %pad.4.near_ref), channel_id=1, source_target_pairs={{0,32},{32,0},{1,33},{33,1},{2,34},{34,2},{3,35},{35,3},{4,36},{36... | collective-permute-start | bytes 36872 | tf_op jit(solution)/shard_map/ppermute | solution.py:368
  38.6 11.4 %pairs.3 = (f32[24,15,128]{2,1,0:T(8,128)}, f32[24,8,128]{2,1,0:T(8,128)}) custom-call(bf16[15,128,320]{2,1,0:T(8,128)(2,1)} %get-tuple-element.34.refs_0_, bf16[4,320,120]{2,1,0:T(8,128)(2,1)} %collective-permute-done.1.refs_1_, bf16[4,320,120]{2,1,0:T(8,128)(2,1)} %collective-permute-done.4.refs_2_, bf16[4,320,120]{2,1,0:T(8,128)(2,1)} %collective-permute-done.2.refs_3_, ...), custom_call_target="tpu_custom_call" | custom-call | flops 1 | bytes 1 | tf_op jit(solution)/shard_map/pairs/pallas_call | solution.py:107
  50.1 2.3 %message.1 = (bf16[16,128]{1,0:T(8,128)(2,1)}, bf16[16,128]{1,0:T(8,128)(2,1)}) custom-call(s32[2]{0:T(128)} %pad_add_fusion.place_ref, f32[8,15,128]{2,1,0:T(8,128)} %get-tuple-element.33.refs_0_, f32[24,15,128]{2,1,0:T(8,128)} %get-tuple-element.38.refs_1_, f32[8,8,128]{2,1,0:T(8,128)} %get-tuple-element.39.refs_2_, ...), custom_call_target="tpu_custom_call" | custom-call | tf_op jit(solution)/shard_map/message/pallas_call | solution.py:160
  55.5 5.5 %all-to-all-start.1 = ((bf16[16,112,128]{2,1,0:T(8,128)(2,1)}), bf16[16,112,128]{2,1,0:T(8,128)(2,1)S(1)}, u32[]{:S(2)}, u32[]{:S(2)}) async-start(bf16[16,112,128]{2,1,0:T(8,128)(2,1)} %copies.1), calls=%async_computation.1 | async-start | bytes 917504 | tf_op jit(solution)/shard_map/all_to_all | solution.py:375
  64.6 6.3 %all-to-all-done.1.message_ref = bf16[16,112,128]{2,1,0:T(8,128)(2,1)S(1)} async-done(((bf16[16,112,128]{2,1,0:T(8,128)(2,1)}), bf16[16,112,128]{2,1,0:T(8,128)(2,1)S(1)}, u32[]{:S(2)}, u32[]{:S(2)}) %all-to-all-start.1) | async-done | bytes 458784 | tf_op jit(solution)/shard_map/all_to_all | solution.py:375
  71.9 3.6 %field_rows.2 = bf16[4,4,32,384]{3,2,1,0:T(8,128)(2,1)} custom-call(s32[5]{0:T(128)S(1)} %stack.53.place_ref, bf16[16,112,128]{2,1,0:T(8,128)(2,1)S(1)} %all-to-all-done.1.message_ref, bf16[15,32,320]{2,1,0:T(8,128)(2,1)S(1)} %get-tuple-element.50.refs_0_, bf16[15,32,320]{2,1,0:T(8,128)(2,1)S(1)} %collective-permute-done.8.refs_1_, ...), custom_call_target="tpu_custom_call" | custom-call | flops 805306368 | bytes 1280000 | tf_op jit(solution)/shard_map/field_rows/pallas_call | solution.py:230
  75.5 4.9 %all-to-all-start.2 = ((bf16[4,4,32,384]{3,2,1,0:T(8,128)(2,1)}), bf16[4,4,32,384]{3,2,1,0:T(8,128)(2,1)S(1)}, u32[]{:S(2)}, u32[]{:S(2)}) async-start(bf16[4,4,32,384]{3,2,1,0:T(8,128)(2,1)} %field_rows.2), calls=%async_computation.2 | async-start | bytes 786432 | tf_op jit(solution)/shard_map/all_to_all | solution.py:387
  80.5 4.3 %field_rows.3 = (bf16[1,4,48,384]{3,2,1,0:T(8,128)(2,1)S(1)}, bf16[1,4,48,384]{3,2,1,0:T(8,128)(2,1)}, bf16[1,4,48,384]{3,2,1,0:T(8,128)(2,1)}, bf16[1,4,48,384]{3,2,1,0:T(8,128)(2,1)}) custom-call(s32[5]{0:T(128)S(1)} %stack.59.place_ref, bf16[16,112,128]{2,1,0:T(8,128)(2,1)S(1)} %all-to-all-done.1.message_ref, ...), custom_call_target="tpu_custom_call" | custom-call | flops 1207959552 | bytes 1920000 | tf_op jit(solution)/shard_map/field_rows/pallas_call | solution.py:230
  84.8 2.6 %collective-permute-start.18 = (bf16[1,4,48,384]{3,2,1,0:T(8,128)(2,1)}, bf16[1,4,48,384]{3,2,1,0:T(8,128)(2,1)S(1)}, u32[]{:S(2)}, u32[]{:S(2)}) collective-permute-start(bf16[1,4,48,384]{3,2,1,0:T(8,128)(2,1)} %get-tuple-element.57), channel_id=1, source_target_pairs={{0,128},{64,192},{128,0},{192,64},{1,129},{65,193},{129,1},{193,65... | collective-permute-start | bytes 442376 | tf_op jit(solution)/shard_map/ppermute | solution.py:389
  88.5 4.9 %collective-permute-done.17.refs_2_ = bf16[1,4,48,384]{3,2,1,0:T(8,128)(2,1)S(1)} collective-permute-done((bf16[1,4,48,384]{3,2,1,0:T(8,128)(2,1)}, bf16[1,4,48,384]{3,2,1,0:T(8,128)(2,1)S(1)}, u32[]{:S(2)}, u32[]{:S(2)}) %collective-permute-start.17) | collective-permute-done | bytes 147488 | tf_op jit(solution)/shard_map/ppermute | solution.py:389
  94.1 19.9 %all_to_all.25.in_ref = bf16[8,80,384]{2,1,0:T(8,128)(2,1)S(1)} all-to-all(bf16[8,80,384]{2,1,0:T(8,128)(2,1)S(1)} %sum_plane.1), channel_id=1, replica_groups=mesh['x'=4,'zh'=2,'y'=4,'zl'=4,'core'=2] {'zh','zl'}, dimensions={0} | all-to-all | bytes 983040 | tf_op jit(solution)/shard_map/all_to_all | solution.py:391
  115.1 6.9 %all-to-all-start.4 = ((bf16[16,80,384]{2,1,0:T(8,128)(2,1)}), bf16[16,80,384]{2,1,0:T(8,128)(2,1)S(1)}, u32[]{:S(2)}, u32[]{:S(2)}) async-start(bf16[16,80,384]{2,1,0:T(8,128)(2,1)} %get-tuple-element.59), calls=%async_computation.4 | async-start | bytes 1966080 | tf_op jit(solution)/shard_map/all_to_all | solution.py:397
  123.7 9.6 %all-to-all-done.4.in_ref = bf16[16,80,384]{2,1,0:T(8,128)(2,1)S(1)} async-done(((bf16[16,80,384]{2,1,0:T(8,128)(2,1)}), bf16[16,80,384]{2,1,0:T(8,128)(2,1)S(1)}, u32[]{:S(2)}, u32[]{:S(2)}) %all-to-all-start.4) | async-done | bytes 983072 | tf_op jit(solution)/shard_map/all_to_all | solution.py:397
  133.3 2.7 %taylor.1 = bf16[4,320,120]{2,1,0:T(8,128)(2,1)S(1)} custom-call(bf16[16,80,384]{2,1,0:T(8,128)(2,1)S(1)} %all-to-all-done.4.in_ref, bf16[4,320,120]{2,1,0:T(8,128)(2,1)S(1)} %copy.12.walkers_ref), custom_call_target="tpu_custom_call" | custom-call | tf_op jit(solution)/shard_map/taylor/pallas_call | solution.py:317
  (62 shorter events, 18.4 us)
Async XLA Ops:
  0.6 12.3 %collective-permute-start = (bf16[4,320,120]{2,1,0:T(8,128)(2,1)}, bf16[4,320,120]{2,1,0:T(8,128)(2,1)S(1)}, u32[]{:S(2)}, u32[]{:S(2)}) collective-permute-start(bf16[4,320,120]{2,1,0:T(8,128)(2,1)} %bitcast.34), channel_id=1, source_target_pairs={{0,1},{1,0},{2,3},{3,2},{4,5},{5,4},{6,7},{7,6},{8,9},{9,8},{10,11... | collective-permute-start | bytes 921608 | tf_op jit(solution)/shard_map/ppermute | solution.py:335
  0.7 19.0 %collective-permute-start.1 = (bf16[4,320,120]{2,1,0:T(8,128)(2,1)}, bf16[4,320,120]{2,1,0:T(8,128)(2,1)}, u32[]{:S(2)}, u32[]{:S(2)}) collective-permute-start(bf16[4,320,120]{2,1,0:T(8,128)(2,1)} %bitcast.35), channel_id=1, source_target_pairs={{0,2},{2,4},{4,6},{6,32},{32,34},{34,36},{36,38},{38,0},{1,3},{3,5... | collective-permute-start | bytes 921608 | tf_op jit(solution)/shard_map/ppermute | solution.py:338
  2.7 17.8 %collective-permute-start.2 = (bf16[4,320,120]{2,1,0:T(8,128)(2,1)}, bf16[4,320,120]{2,1,0:T(8,128)(2,1)}, u32[]{:S(2)}, u32[]{:S(2)}) collective-permute-start(bf16[4,320,120]{2,1,0:T(8,128)(2,1)} %bitcast.36), channel_id=1, source_target_pairs={{0,4},{1,37},{2,6},{3,39},{4,32},{5,1},{6,34},{7,3},{32,36},{33,5}... | collective-permute-start | bytes 921608 | tf_op jit(solution)/shard_map/ppermute | solution.py:341
  6.0 14.5 %collective-permute-start.3 = (bf16[4,320,120]{2,1,0:T(8,128)(2,1)}, bf16[4,320,120]{2,1,0:T(8,128)(2,1)}, u32[]{:S(2)}, u32[]{:S(2)}) collective-permute-start(bf16[4,320,120]{2,1,0:T(8,128)(2,1)} %bitcast.37), channel_id=1, source_target_pairs={{0,38},{2,0},{4,2},{6,4},{32,6},{34,32},{36,34},{38,36},{1,39},{3,... | collective-permute-start | bytes 921608 | tf_op jit(solution)/shard_map/ppermute | solution.py:339
  20.5 33.2 %all-to-all-start = ((bf16[4,15,48,320]{3,2,1,0:T(8,128)(2,1)}), bf16[4,15,48,320]{3,2,1,0:T(8,128)(2,1)S(1)}, u32[]{:S(2)}, u32[]{:S(2)}) async-start(bf16[4,15,48,320]{3,2,1,0:T(8,128)(2,1)} %bitcast.31), calls=%async_computation | async-start | bytes 4423680 | tf_op jit(solution)/shard_map/all_to_all | solution.py:358
  25.6 6.5 %collective-permute-start.4 = (bf16[4,320,120]{2,1,0:T(8,128)(2,1)}, bf16[4,320,120]{2,1,0:T(8,128)(2,1)}, u32[]{:S(2)}, u32[]{:S(2)}) collective-permute-start(bf16[4,320,120]{2,1,0:T(8,128)(2,1)} %collective-permute-done.1.refs_1_), channel_id=1, source_target_pairs={{0,1},{1,0},{2,3},{3,2},{4,5},{5,4},{6,7},{7,6},{8,9},{9,8},{10,11... | collective-permute-start | bytes 921608 | tf_op jit(solution)/shard_map/ppermute | solution.py:335
  27.3 6.2 %collective-permute-start.5 = (bf16[4,320,120]{2,1,0:T(8,128)(2,1)}, bf16[4,320,120]{2,1,0:T(8,128)(2,1)}, u32[]{:S(2)}, u32[]{:S(2)}) collective-permute-start(bf16[4,320,120]{2,1,0:T(8,128)(2,1)} %collective-permute-done.2.refs_3_), channel_id=1, source_target_pairs={{0,1},{1,0},{2,3},{3,2},{4,5},{5,4},{6,7},{7,6},{8,9},{9,8},{10,11... | collective-permute-start | bytes 921608 | tf_op jit(solution)/shard_map/ppermute | solution.py:335
  27.3 11.2 %collective-permute-start.6 = (bf16[4,320,120]{2,1,0:T(8,128)(2,1)}, bf16[4,320,120]{2,1,0:T(8,128)(2,1)}, u32[]{:S(2)}, u32[]{:S(2)}) collective-permute-start(bf16[4,320,120]{2,1,0:T(8,128)(2,1)} %collective-permute-done.3.refs_5_), channel_id=1, source_target_pairs={{0,1},{1,0},{2,3},{3,2},{4,5},{5,4},{6,7},{7,6},{8,9},{9,8},{10,11... | collective-permute-start | bytes 921608 | tf_op jit(solution)/shard_map/ppermute | solution.py:335
  27.8 22.2 %collective-permute-start.8 = (bf16[15,32,320]{2,1,0:T(8,128)(2,1)}, bf16[15,32,320]{2,1,0:T(8,128)(2,1)S(1)}, u32[]{:S(2)}, u32[]{:S(2)}) collective-permute-start(bf16[15,32,320]{2,1,0:T(8,128)(2,1)} %get-tuple-element.42), channel_id=1, source_target_pairs={{0,64},{64,128},{128,192},{192,0},{1,65},{65,129},{129,193},{193,1... | collective-permute-start | bytes 921608 | tf_op jit(solution)/shard_map/ppermute | solution.py:356
  29.3 20.7 %collective-permute-start.9 = (bf16[15,32,320]{2,1,0:T(8,128)(2,1)}, bf16[15,32,320]{2,1,0:T(8,128)(2,1)S(1)}, u32[]{:S(2)}, u32[]{:S(2)}) collective-permute-start(bf16[15,32,320]{2,1,0:T(8,128)(2,1)} %get-tuple-element.43), channel_id=1, source_target_pairs={{0,128},{64,192},{128,0},{192,64},{1,129},{65,193},{129,1},{193,65... | collective-permute-start | bytes 921608 | tf_op jit(solution)/shard_map/ppermute | solution.py:356
  32.1 18.0 %collective-permute-start.10 = (bf16[15,32,320]{2,1,0:T(8,128)(2,1)}, bf16[15,32,320]{2,1,0:T(8,128)(2,1)}, u32[]{:S(2)}, u32[]{:S(2)}) collective-permute-start(bf16[15,32,320]{2,1,0:T(8,128)(2,1)} %get-tuple-element.44), channel_id=1, source_target_pairs={{0,192},{64,0},{128,64},{192,128},{1,193},{65,1},{129,65},{193,129... | collective-permute-start | bytes 921608 | tf_op jit(solution)/shard_map/ppermute | solution.py:356
  33.5 16.5 %collective-permute-start.7 = (bf16[48,128]{1,0:T(8,128)(2,1)S(1)}, bf16[48,128]{1,0:T(8,128)(2,1)S(1)}, u32[]{:S(2)}, u32[]{:S(2)}) collective-permute-start(bf16[48,128]{1,0:T(8,128)(2,1)S(1)} %pad.4.near_ref), channel_id=1, source_target_pairs={{0,32},{32,0},{1,33},{33,1},{2,34},{34,2},{3,35},{35,3},{4,36},{36... | collective-permute-start | bytes 36872 | tf_op jit(solution)/shard_map/ppermute | solution.py:368
  52.4 1.4 %collective-permute-start.11 = (bf16[16,128]{1,0:T(8,128)(2,1)}, bf16[16,128]{1,0:T(8,128)(2,1)S(1)}, u32[]{:S(2)}, u32[]{:S(2)}) collective-permute-start(bf16[16,128]{1,0:T(8,128)(2,1)} %get-tuple-element.47), channel_id=1, source_target_pairs={{0,1},{1,0},{2,3},{3,2},{4,5},{5,4},{6,7},{7,6},{8,9},{9,8},{10,11... | collective-permute-start | bytes 12296 | tf_op jit(solution)/shard_map/ppermute | solution.py:335
  53.8 26.7 %collective-permute-start.16 = (bf16[4,15,48,320]{3,2,1,0:T(8,128)(2,1)S(1)}, bf16[4,15,48,320]{3,2,1,0:T(8,128)(2,1)}, u32[]{:S(2)}, u32[]{:S(2)}) collective-permute-start(bf16[4,15,48,320]{3,2,1,0:T(8,128)(2,1)S(1)} %all-to-all-done.refs_0_), channel_id=1, source_target_pairs={{0,1},{1,0},{2,3},{3,2},{4,5},{5,4},{6,7},{7,6},{8,9},{9,8},{10,11... | collective-permute-start | bytes 5529608 | tf_op jit(solution)/shard_map/ppermute | solution.py:335
  55.5 15.4 %all-to-all-start.1 = ((bf16[16,112,128]{2,1,0:T(8,128)(2,1)}), bf16[16,112,128]{2,1,0:T(8,128)(2,1)S(1)}, u32[]{:S(2)}, u32[]{:S(2)}) async-start(bf16[16,112,128]{2,1,0:T(8,128)(2,1)} %copies.1), calls=%async_computation.1 | async-start | bytes 917504 | tf_op jit(solution)/shard_map/all_to_all | solution.py:375
  61.0 1.8 %collective-permute-start.12 = (bf16[15,32,320]{2,1,0:T(8,128)(2,1)S(1)}, bf16[15,32,320]{2,1,0:T(8,128)(2,1)}, u32[]{:S(2)}, u32[]{:S(2)}) collective-permute-start(bf16[15,32,320]{2,1,0:T(8,128)(2,1)S(1)} %get-tuple-element.50.refs_0_), channel_id=1, source_target_pairs={{0,1},{1,0},{2,3},{3,2},{4,5},{5,4},{6,7},{7,6},{8,9},{9,8},{10,11... | collective-permute-start | bytes 921608 | tf_op jit(solution)/shard_map/ppermute | solution.py:335
  61.0 2.9 %collective-permute-start.13 = (bf16[15,32,320]{2,1,0:T(8,128)(2,1)S(1)}, bf16[15,32,320]{2,1,0:T(8,128)(2,1)}, u32[]{:S(2)}, u32[]{:S(2)}) collective-permute-start(bf16[15,32,320]{2,1,0:T(8,128)(2,1)S(1)} %collective-permute-done.8.refs_1_), channel_id=1, source_target_pairs={{0,1},{1,0},{2,3},{3,2},{4,5},{5,4},{6,7},{7,6},{8,9},{9,8},{10,11... | collective-permute-start | bytes 921608 | tf_op jit(solution)/shard_map/ppermute | solution.py:335
  61.5 2.6 %collective-permute-start.14 = (bf16[15,32,320]{2,1,0:T(8,128)(2,1)}, bf16[15,32,320]{2,1,0:T(8,128)(2,1)}, u32[]{:S(2)}, u32[]{:S(2)}) collective-permute-start(bf16[15,32,320]{2,1,0:T(8,128)(2,1)} %copy-done), channel_id=1, source_target_pairs={{0,1},{1,0},{2,3},{3,2},{4,5},{5,4},{6,7},{7,6},{8,9},{9,8},{10,11... | collective-permute-start | bytes 921608 | tf_op jit(solution)/shard_map/ppermute | solution.py:335
  61.6 3.0 %collective-permute-start.15 = (bf16[15,32,320]{2,1,0:T(8,128)(2,1)}, bf16[15,32,320]{2,1,0:T(8,128)(2,1)}, u32[]{:S(2)}, u32[]{:S(2)}) collective-permute-start(bf16[15,32,320]{2,1,0:T(8,128)(2,1)} %collective-permute-done.10.refs_3_), channel_id=1, source_target_pairs={{0,1},{1,0},{2,3},{3,2},{4,5},{5,4},{6,7},{7,6},{8,9},{9,8},{10,11... | collective-permute-start | bytes 921608 | tf_op jit(solution)/shard_map/ppermute | solution.py:335
  75.5 13.0 %all-to-all-start.2 = ((bf16[4,4,32,384]{3,2,1,0:T(8,128)(2,1)}), bf16[4,4,32,384]{3,2,1,0:T(8,128)(2,1)S(1)}, u32[]{:S(2)}, u32[]{:S(2)}) async-start(bf16[4,4,32,384]{3,2,1,0:T(8,128)(2,1)} %field_rows.2), calls=%async_computation.2 | async-start | bytes 786432 | tf_op jit(solution)/shard_map/all_to_all | solution.py:387
  84.8 8.6 %collective-permute-start.17 = (bf16[1,4,48,384]{3,2,1,0:T(8,128)(2,1)}, bf16[1,4,48,384]{3,2,1,0:T(8,128)(2,1)S(1)}, u32[]{:S(2)}, u32[]{:S(2)}) collective-permute-start(bf16[1,4,48,384]{3,2,1,0:T(8,128)(2,1)} %get-tuple-element.56), channel_id=1, source_target_pairs={{0,64},{64,128},{128,192},{192,0},{1,65},{65,129},{129,193},{193,1... | collective-permute-start | bytes 442376 | tf_op jit(solution)/shard_map/ppermute | solution.py:389
  84.8 8.6 %collective-permute-start.18 = (bf16[1,4,48,384]{3,2,1,0:T(8,128)(2,1)}, bf16[1,4,48,384]{3,2,1,0:T(8,128)(2,1)S(1)}, u32[]{:S(2)}, u32[]{:S(2)}) collective-permute-start(bf16[1,4,48,384]{3,2,1,0:T(8,128)(2,1)} %get-tuple-element.57), channel_id=1, source_target_pairs={{0,128},{64,192},{128,0},{192,64},{1,129},{65,193},{129,1},{193,65... | collective-permute-start | bytes 442376 | tf_op jit(solution)/shard_map/ppermute | solution.py:389
  87.4 6.6 %collective-permute-start.19 = (bf16[1,4,48,384]{3,2,1,0:T(8,128)(2,1)}, bf16[1,4,48,384]{3,2,1,0:T(8,128)(2,1)S(1)}, u32[]{:S(2)}, u32[]{:S(2)}) collective-permute-start(bf16[1,4,48,384]{3,2,1,0:T(8,128)(2,1)} %get-tuple-element.58), channel_id=1, source_target_pairs={{0,192},{64,0},{128,64},{192,128},{1,193},{65,1},{129,65},{193,129... | collective-permute-start | bytes 442376 | tf_op jit(solution)/shard_map/ppermute | solution.py:389
  115.1 18.2 %all-to-all-start.4 = ((bf16[16,80,384]{2,1,0:T(8,128)(2,1)}), bf16[16,80,384]{2,1,0:T(8,128)(2,1)S(1)}, u32[]{:S(2)}, u32[]{:S(2)}) async-start(bf16[16,80,384]{2,1,0:T(8,128)(2,1)} %get-tuple-element.59), calls=%async_computation.4 | async-start | bytes 1966080 | tf_op jit(solution)/shard_map/all_to_all | solution.py:397
  (7 other events, 21.9 us)

commit v5 on v4

--- a/solution.py
+++ b/solution.py
@@ -46,7 +46,9 @@
 
 def pair_kernel(vectors, first, count, *refs):
     inputs, (trace_ref, square_ref) = refs[:count], refs[count : count + 2]
-    held, semaphores = refs[-1 - count : -1], refs[-1]
+    rot_ref, green_ref, semaphores = refs[-3:]
+    group = green_ref.shape[1]
+    held = [rot_ref] + [green_ref.at[k] for k in range(count - 1)]
     loads = [
         pltpu.make_async_copy(src, dst, semaphores.at[i])
         for i, (src, dst) in enumerate(zip(inputs, held, strict=True))
@@ -54,41 +56,29 @@
     for load in loads:
         load.start()
     loads[0].wait()
-    rot_ref, greens = held[0], held[1:]
     if first:
-        rot_ref = refs[count + 2]
+        raw_ref, rot_ref = rot_ref, refs[count + 2]
         for g in range(vectors):
-            rot_ref[g] = widen(held[0][g]).T
+            rot_ref[g] = widen(raw_ref[g]).T
     orbitals = rot_ref.shape[2]
     eye = (
         lax.broadcasted_iota(jnp.int32, (ROW, ROW), 0)
         == lax.broadcasted_iota(jnp.int32, (ROW, ROW), 1)
     ).astype(f32)
-    base = 0
-    for load, green_ref in zip(loads[1:], greens, strict=True):
+
+    for load in loads[1:]:
         load.wait()
-        count = green_ref.shape[0] // 2
-
-        def two_walkers(i, carry, green_ref=green_ref, base=base):
-            green = jnp.concatenate([widen(green_ref[2 * i]), widen(green_ref[2 * i + 1])], axis=1)
-            rot = rot_ref[...].reshape(vectors * ROW, orbitals)
-            pairs = jnp.dot(rot, green, preferred_element_type=f32)
-            for w in range(2):
-                total = jnp.zeros((8, ROW), f32)
-                for g in range(vectors):
-                    block = pairs[g * ROW : (g + 1) * ROW, w * ROW : (w + 1) * ROW]
-                    total = total + jnp.sum((block * block.T).reshape(ROW // 8, 8, ROW), axis=0)
-                    trace_ref[base + 2 * i + w, pl.ds(g, 1), :] = jnp.sum(
-                        block * eye, axis=0, keepdims=True
-                    )
-                square_ref[base + 2 * i + w] = total
-            return carry
-
-        if count == 1:
-            two_walkers(0, 0)
-        else:
-            lax.fori_loop(0, count, two_walkers, 0)
-        base += 2 * count
+    for k in range(count - 1):
+        green = jnp.concatenate([widen(green_ref[k, w]) for w in range(group)], axis=1)
+        rot = rot_ref[...].reshape(vectors * ROW, orbitals)
+        pairs = jnp.dot(rot, green, preferred_element_type=f32)
+        for w in range(group):
+            total = jnp.zeros((8, ROW), f32)
+            for g in range(vectors):
+                block = pairs[g * ROW : (g + 1) * ROW, w * ROW : (w + 1) * ROW]
+                total = total + jnp.sum((block * block.T).reshape(ROW // 8, 8, ROW), axis=0)
+                trace_ref[group * k + w, pl.ds(g, 1), :] = jnp.sum(block * eye, axis=0, keepdims=True)
+            square_ref[group * k + w] = total
 
 
 def widen(a):
@@ -108,8 +98,11 @@
         functools.partial(pair_kernel, vectors, first, 1 + len(greens)),
         out_shape=out_shape,
         in_specs=[pl.BlockSpec(memory_space=pl.ANY)] * (1 + len(greens)),
-        scratch_shapes=[pltpu.VMEM(a.shape, bf16) for a in (rot, *greens)]
-        + [pltpu.SemaphoreType.DMA((1 + len(greens),))],
+        scratch_shapes=[
+            pltpu.VMEM(rot.shape, bf16),
+            pltpu.VMEM((len(greens), *greens[0].shape), bf16),
+            pltpu.SemaphoreType.DMA((1 + len(greens),)),
+        ],
         compiler_params=pltpu.CompilerParams(vmem_limit_bytes=56 * 2**20),
         cost_estimate=pl.CostEstimate(flops=1, bytes_accessed=1, transcendentals=0),
         name="pairs",
@@ -197,29 +190,34 @@
     for ref in inputs:
         blocks += [ref] if len(ref.shape) == 3 else [ref.at[k] for k in range(4)]
     rows, orbitals = blocks[0].shape[1:]
-    depth = vectors * TILE
-    lane = lax.broadcasted_iota(jnp.int32, (ROW, depth), 0)
-    vector = lax.shift_right_logical(lax.broadcasted_iota(jnp.int32, (ROW, depth), 1), 4)
+    depth = TILE * TILE
+    place = lax.broadcasted_iota(jnp.int32, (ROW, 2 * depth), 1)
+    spread = lax.broadcasted_iota(jnp.int32, (ROW, 2 * depth), 0) == lax.shift_right_logical(place, 4)
+    spread = spread.astype(bf16)
+    shifted = [
+        pltpu.roll(message_ref[place_ref[k], 0:TILE, :].astype(f32), place_ref[4], 0) for k in range(4)
+    ]
+    shifted = jnp.concatenate(shifted).astype(bf16)
+    wide = jnp.dot(shifted, spread, preferred_element_type=f32)
     same = (
-        jnp.bitwise_and(lax.broadcasted_iota(jnp.int32, (TILE * TILE, depth), 0), TILE - 1)
-        == jnp.bitwise_and(lax.broadcasted_iota(jnp.int32, (TILE * TILE, depth), 1), TILE - 1)
+        jnp.bitwise_and(lax.broadcasted_iota(jnp.int32, (depth, depth), 0), TILE - 1)
+        == jnp.bitwise_and(lax.broadcasted_iota(jnp.int32, (depth, depth), 1), TILE - 1)
     )
     weights = []
     for b in range(8):
-        shifted = message_ref[place_ref[b % 4], 0:TILE, :].astype(f32)
-        shifted = pltpu.roll(shifted, place_ref[4], 0).astype(bf16)
-        spread = (lane == vector + TILE * (b // 4)).astype(bf16)
-        wide = jnp.dot(shifted, spread, preferred_element_type=f32)
-        wide = jnp.broadcast_to(wide[:, None, :], (TILE, TILE, depth)).reshape(TILE * TILE, depth)
-        weights.append(jnp.where(same, wide, 0.0).astype(bf16))
+        part = wide[(b % 4) * TILE : (b % 4 + 1) * TILE, (b // 4) * depth : (b // 4 + 1) * depth]
+        part = jnp.broadcast_to(part[:, None, :], (TILE, TILE, depth)).reshape(depth, depth)
+        weights.append(jnp.where(same, part, 0.0).astype(bf16))
+    weights = jnp.concatenate(weights, axis=1)
+    nought = jnp.zeros((TILE, orbitals), bf16)
     for out_ref in outs:
         out_ref[:, :, 256:WIDE] = jnp.zeros((4, rows, WIDE - 256), bf16)
     for t in range(rows // TILE):
         here = slice(t * TILE, (t + 1) * TILE)
-        total = jnp.zeros((TILE * TILE, orbitals), f32)
-        for b, block_ref in enumerate(blocks):
-            block = block_ref[:, here, :].reshape(depth, orbitals)
-            total = total + jnp.dot(weights[b], block, preferred_element_type=f32)
+        column = []
+        for block_ref in blocks:
+            column += [block_ref[:, here, :].reshape(vectors * TILE, orbitals), nought]
+        total = jnp.dot(weights, jnp.concatenate(column), preferred_element_type=f32)
         total = (step_root * total).astype(bf16).reshape(TILE, TILE, orbitals)
         for w in range(TILE):
             outs[w // 4][w % 4, here, 0:orbitals] = total[w]
@@ -299,18 +297,22 @@
 
 def taylor_kernel(first_rows, in_ref, walkers_ref, out_ref):
     orbitals = walkers_ref.shape[1]
-    for w in range(4):
-        field = jnp.concatenate(
+    fields = [
+        jnp.concatenate(
             [in_ref[4 * k + w, 0:first_rows] for k in range(4)]
             + [in_ref[4 * w + k, first_rows:] for k in range(4)]
         )[:, 0:orbitals]
-        current = walkers_ref[w]
-        total = current.astype(f32)
-        for order in range(1, ORDER + 1):
-            update = jnp.dot(field, current, preferred_element_type=f32) / order
-            total = total + update
-            current = update.astype(bf16)
-        out_ref[w] = total.astype(bf16)
+        for w in range(4)
+    ]
+    currents = [walkers_ref[w] for w in range(4)]
+    totals = [current.astype(f32) for current in currents]
+    for order in range(1, ORDER + 1):
+        for w in range(4):
+            update = jnp.dot(fields[w], currents[w], preferred_element_type=f32) / order
+            totals[w] = totals[w] + update
+            currents[w] = update.astype(bf16)
+    for w in range(4):
+        out_ref[w] = totals[w].astype(bf16)
 
 
 def taylor(gathered, walkers, first_rows):
@@ -382,12 +384,11 @@
 
     along_x = [4 * lax.rem(x + 4 - k, 4) + y for k in range(4)]
     along_y = [4 * x + k for k in range(4)]
-    turn = lax.rem(16 - 4 * x, 16)
-    (first,) = field_rows(place(along_x, 0), message, first_blocks, 1)
-    first = lax.all_to_all(first, "y", 0, 0)
-    second = field_rows(place(along_y, turn), message, second_blocks, 4)
+    second = field_rows(place(along_y, lax.rem(16 - 4 * x, 16)), message, second_blocks, 4)
     second = [second[0]] + [lax.ppermute(second[k], "x", ring(4, k)) for k in (1, 2, 3)]
-    field = sum_second_axis(message, [first], second)
+    first = field_rows(place(along_x, lax.rem(16 - 4 * y, 16)), message, first_blocks, 4)
+    first = [first[0]] + [lax.ppermute(first[k], "y", ring(4, k)) for k in (1, 2, 3)]
+    field = sum_second_axis(message, first, second)
     field = lax.all_to_all(field, Z, 0, 0)
     whole = message[:, TILE:].reshape(4, 4, 2, near.shape[0], 128)[:, :, :, : share * group, :electrons]
     whole = whole.reshape(4, 4, 2, share, group, electrons).transpose(4, 0, 2, 1, 3, 5)

time: 137 us -> 133 us (0.971)
  Pallas kernels: 32.4 us -> 27.6 us
    ppermute x3, waiting for transfers between devices: 5.44 us -> 0.01 us  [on_device(): lax.ppermute(second[k], 'x', ring(4, k))]
    all_to_all x1 -> x0, starting transfers between devices: 4.89 us -> none  [on_device(): first = lax.all_to_all(first, 'y', 0, 0)]
    ppermute x0 -> x3, waiting for transfers between devices: none -> 4.25 us  [on_device(): lax.ppermute(first[k], 'y', ring(4, k))]
    ppermute x0 -> x3, starting transfers between devices: none -> 3.58 us  [on_device(): lax.ppermute(first[k], 'y', ring(4, k))]
    pallas_call x2, Pallas kernels: 17.4 us -> 15.6 us  [pair_sums(): pl.pallas_call(functools.partial(pair_kernel, vectors, first, 1 + len(gre...]
    pallas_call x2, Pallas kernels: 7.87 us -> 6.35 us  [field_rows(): pl.pallas_call(functools.partial(field_kernel, vectors), out_shape=[jax.S...]
    pallas_call x1, Pallas kernels: 2.69 us -> 1.2 us  [taylor(): pl.pallas_call(functools.partial(taylor_kernel, first_rows), out_shape=ja...]
  transfers between devices with their start and end apart: 25 -> 27, of which waited for: 11 -> 12; matrix products, arithmetic and copies ran while one was open for 4% -> 4% of each run, Pallas kernels for 21% -> 19%
where the time goes in v5:
time: 133 us; the launch traced here: 132 us
  starting transfers between devices  46.4 us (35%)
  Pallas kernels  27.6 us (21%)
  waiting for transfers between devices  27.2 us (20%)
  blocking collectives  20.1 us (15%)
  local copies, waits for them, and re-layouts  9.64 us (7%)
    all_to_all x1, blocking collectives, on_device(): field = lax.all_to_all(field, Z, 0, 0)  20.1 us
    pallas_call x2, Pallas kernels, pair_sums(): pl.pallas_call(functools.partial(pair_kernel, vectors, first, 1 + len(gre...  15.6 us
    all_to_all x1, waiting for transfers between devices, on_device(): field = lax.all_to_all(field, ('x', 'y'), 0, 0)  10.8 us
    all_to_all x1, starting transfers between devices, on_device(): message = lax.all_to_all(message, ('x', 'y'), 0, 0)  6.51 us
    all_to_all x1, starting transfers between devices, on_device(): field = lax.all_to_all(field, ('x', 'y'), 0, 0)  6.42 us
    pallas_call x2, Pallas kernels, field_rows(): pl.pallas_call(functools.partial(field_kernel, vectors), out_shape=[jax.S...  6.35 us
    all_to_all x1, waiting for transfers between devices, on_device(): message = lax.all_to_all(message, ('x', 'y'), 0, 0)  6.32 us
    ppermute x3, starting transfers between devices, on_device(): lax.ppermute(after(first_pieces[k], beside), 'x', ring(4, k))  5.66 us
  transfers between devices with their start and end apart: 27, of which 12 were waited for; matrix products, arithmetic and copies ran while one was open for 4% of the time, Pallas kernels for 19%

profile of v5, /device:TPU:8, one launch (start us, length us, event | category | flops | bytes accessed | tf_op | source)
XLA Modules:
  0.0 132.4 jit_solution(10737357142569602775)
XLA Ops:
  0.7 2.0 %collective-permute-start.1 = (bf16[4,320,120]{2,1,0:T(8,128)(2,1)}, bf16[4,320,120]{2,1,0:T(8,128)(2,1)}, u32[]{:S(2)}, u32[]{:S(2)}) collective-permute-start(bf16[4,320,120]{2,1,0:T(8,128)(2,1)} %bitcast.36), channel_id=1, source_target_pairs={{0,2},{2,4},{4,6},{6,32},{32,34},{34,36},{36,38},{38,0},{1,3},{3,5... | collective-permute-start | bytes 921608 | tf_op jit(solution)/shard_map/ppermute | solution.py:340
  2.7 3.3 %collective-permute-start.2 = (bf16[4,320,120]{2,1,0:T(8,128)(2,1)}, bf16[4,320,120]{2,1,0:T(8,128)(2,1)}, u32[]{:S(2)}, u32[]{:S(2)}) collective-permute-start(bf16[4,320,120]{2,1,0:T(8,128)(2,1)} %bitcast.37), channel_id=1, source_target_pairs={{0,4},{1,37},{2,6},{3,39},{4,32},{5,1},{6,34},{7,3},{32,36},{33,5}... | collective-permute-start | bytes 921608 | tf_op jit(solution)/shard_map/ppermute | solution.py:343
  7.3 1.6 %slice-done = bf16[15,192,320]{2,1,0:T(8,128)(2,1)S(1)} async-done(((bf16[15,320,320]{2,1,0:T(8,128)(2,1)}), bf16[15,192,320]{2,1,0:T(8,128)(2,1)S(1)}, s32[]{:S(2)}) %slice-start) | async-done | bytes 1843224 | tf_op jit(solution)/shard_map/slice | solution.py:351
  8.9 1.6 %copy.15 = bf16[15,4,48,320]{3,2,0,1:T(8,128)(2,1)} copy(bf16[15,4,48,320]{3,2,1,0:T(8,128)(2,1)S(1)} %bitcast.33) | data formatting | bytes 3686400 | tf_op jit(solution)/shard_map/reshape | solution.py:351
  10.5 2.4 %constant_dynamic-slice_fusion.1 = (bf16[15,32,320]{2,1,0:T(8,128)(2,1)}, bf16[15,32,320]{2,1,0:T(8,128)(2,1)}, bf16[15,32,320]{2,1,0:T(8,128)(2,1)}, bf16[15,32,320]{2,1,0:T(8,128)(2,1)S(1)}) fusion(bf16[15,320,320]{2,1,0:T(8,128)(2,1)} %param.9, s32[]{:T(128)S(6)} %select_n.18, s32[]{:T(128)S(6)} %select_n.17, s32[]{:T(128)S(6)} %select_n.16, s32[]{:T(128)S(6)} %select_n.15), kind=kLoop, calls=%fused_computation.2 | loop fusion | bytes 2457616 | tf_op jit(solution)/shard_map/dynamic_slice | solution.py:348
  13.7 5.8 %pairs.2 = (f32[8,15,128]{2,1,0:T(8,128)}, f32[8,8,128]{2,1,0:T(8,128)}, bf16[15,128,320]{2,1,0:T(8,128)(2,1)}) custom-call(bf16[15,320,120]{2,1,0:T(8,128)(2,1)} %bitcast.43, bf16[4,320,120]{2,1,0:T(8,128)(2,1)} %bitcast.39, bf16[4,320,120]{2,1,0:T(8,128)(2,1)} %copy-done.3), custom_call_target="tpu_custom_call" | custom-call | flops 1 | bytes 1 | tf_op jit(solution)/shard_map/pairs/pallas_call | solution.py:97
  20.5 5.0 %all-to-all-start = ((bf16[4,15,48,320]{3,2,1,0:T(8,128)(2,1)}), bf16[4,15,48,320]{3,2,1,0:T(8,128)(2,1)S(1)}, u32[]{:S(2)}, u32[]{:S(2)}) async-start(bf16[4,15,48,320]{3,2,1,0:T(8,128)(2,1)} %bitcast.32), calls=%async_computation | async-start | bytes 4423680 | tf_op jit(solution)/shard_map/all_to_all | solution.py:360
  25.6 1.8 %collective-permute-start.4 = (bf16[4,320,120]{2,1,0:T(8,128)(2,1)}, bf16[4,320,120]{2,1,0:T(8,128)(2,1)}, u32[]{:S(2)}, u32[]{:S(2)}) collective-permute-start(bf16[4,320,120]{2,1,0:T(8,128)(2,1)} %collective-permute-done.1.refs_1_), channel_id=1, source_target_pairs={{0,1},{1,0},{2,3},{3,2},{4,5},{5,4},{6,7},{7,6},{8,9},{9,8},{10,11... | collective-permute-start | bytes 921608 | tf_op jit(solution)/shard_map/ppermute | solution.py:337
  27.8 1.5 %collective-permute-start.8 = (bf16[15,32,320]{2,1,0:T(8,128)(2,1)}, bf16[15,32,320]{2,1,0:T(8,128)(2,1)S(1)}, u32[]{:S(2)}, u32[]{:S(2)}) collective-permute-start(bf16[15,32,320]{2,1,0:T(8,128)(2,1)} %get-tuple-element.46), channel_id=1, source_target_pairs={{0,64},{64,128},{128,192},{192,0},{1,65},{65,129},{129,193},{193,1... | collective-permute-start | bytes 921608 | tf_op jit(solution)/shard_map/ppermute | solution.py:358
  29.3 2.7 %collective-permute-start.9 = (bf16[15,32,320]{2,1,0:T(8,128)(2,1)}, bf16[15,32,320]{2,1,0:T(8,128)(2,1)S(1)}, u32[]{:S(2)}, u32[]{:S(2)}) collective-permute-start(bf16[15,32,320]{2,1,0:T(8,128)(2,1)} %get-tuple-element.47), channel_id=1, source_target_pairs={{0,128},{64,192},{128,0},{192,64},{1,129},{65,193},{129,1},{193,65... | collective-permute-start | bytes 921608 | tf_op jit(solution)/shard_map/ppermute | solution.py:358
  33.5 4.5 %collective-permute-start.7 = (bf16[48,128]{1,0:T(8,128)(2,1)S(1)}, bf16[48,128]{1,0:T(8,128)(2,1)S(1)}, u32[]{:S(2)}, u32[]{:S(2)}) collective-permute-start(bf16[48,128]{1,0:T(8,128)(2,1)S(1)} %pad.4.near_ref), channel_id=1, source_target_pairs={{0,32},{32,0},{1,33},{33,1},{2,34},{34,2},{3,35},{35,3},{4,36},{36... | collective-permute-start | bytes 36872 | tf_op jit(solution)/shard_map/ppermute | solution.py:370
  38.6 9.8 %pairs.3 = (f32[24,15,128]{2,1,0:T(8,128)}, f32[24,8,128]{2,1,0:T(8,128)}) custom-call(bf16[15,128,320]{2,1,0:T(8,128)(2,1)} %get-tuple-element.38.refs_0_, bf16[4,320,120]{2,1,0:T(8,128)(2,1)} %collective-permute-done.1.refs_1_, bf16[4,320,120]{2,1,0:T(8,128)(2,1)} %collective-permute-done.4.refs_2_, bf16[4,320,120]{2,1,0:T(8,128)(2,1)} %collective-permute-done.2.refs_3_, ...), custom_call_target="tpu_custom_call" | custom-call | flops 1 | bytes 1 | tf_op jit(solution)/shard_map/pairs/pallas_call | solution.py:97
  48.6 2.3 %message.1 = (bf16[16,128]{1,0:T(8,128)(2,1)}, bf16[16,128]{1,0:T(8,128)(2,1)}) custom-call(s32[2]{0:T(128)} %pad_add_fusion.place_ref, f32[8,15,128]{2,1,0:T(8,128)} %get-tuple-element.37.refs_0_, f32[24,15,128]{2,1,0:T(8,128)} %get-tuple-element.42.refs_1_, f32[8,8,128]{2,1,0:T(8,128)} %get-tuple-element.43.refs_2_, ...), custom_call_target="tpu_custom_call" | custom-call | tf_op jit(solution)/shard_map/message/pallas_call | solution.py:153
  54.5 6.5 %all-to-all-start.1 = ((bf16[16,112,128]{2,1,0:T(8,128)(2,1)}), bf16[16,112,128]{2,1,0:T(8,128)(2,1)S(1)}, u32[]{:S(2)}, u32[]{:S(2)}) async-start(bf16[16,112,128]{2,1,0:T(8,128)(2,1)} %copies.1), calls=%async_computation.1 | async-start | bytes 917504 | tf_op jit(solution)/shard_map/all_to_all | solution.py:377
  64.6 6.3 %all-to-all-done.1.message_ref = bf16[16,112,128]{2,1,0:T(8,128)(2,1)S(1)} async-done(((bf16[16,112,128]{2,1,0:T(8,128)(2,1)}), bf16[16,112,128]{2,1,0:T(8,128)(2,1)S(1)}, u32[]{:S(2)}, u32[]{:S(2)}) %all-to-all-start.1) | async-done | bytes 458784 | tf_op jit(solution)/shard_map/all_to_all | solution.py:377
  71.9 2.8 %field_rows.2 = (bf16[1,4,32,384]{3,2,1,0:T(8,128)(2,1)S(1)}, bf16[1,4,32,384]{3,2,1,0:T(8,128)(2,1)S(1)}, bf16[1,4,32,384]{3,2,1,0:T(8,128)(2,1)S(1)}, bf16[1,4,32,384]{3,2,1,0:T(8,128)(2,1)S(1)}) custom-call(s32[5]{0:T(128)S(1)} %stack.57.place_ref, bf16[16,112,128]{2,1,0:T(8,128)(2,1)S(1)} %all-to-all-done.1.message_ref, ...), custom_call_target="tpu_custom_call" | custom-call | flops 805306368 | bytes 1280000 | tf_op jit(solution)/shard_map/field_rows/pallas_call | solution.py:228
  75.4 3.6 %field_rows.3 = (bf16[1,4,48,384]{3,2,1,0:T(8,128)(2,1)S(1)}, bf16[1,4,48,384]{3,2,1,0:T(8,128)(2,1)S(1)}, bf16[1,4,48,384]{3,2,1,0:T(8,128)(2,1)S(1)}, bf16[1,4,48,384]{3,2,1,0:T(8,128)(2,1)S(1)}) custom-call(s32[5]{0:T(128)S(1)} %stack.63.place_ref, bf16[16,112,128]{2,1,0:T(8,128)(2,1)S(1)} %all-to-all-done.1.message_ref, ...), custom_call_target="tpu_custom_call" | custom-call | flops 1207959552 | bytes 1920000 | tf_op jit(solution)/shard_map/field_rows/pallas_call | solution.py:228
  79.3 2.3 %collective-permute-start.21 = (bf16[1,4,48,384]{3,2,1,0:T(8,128)(2,1)S(1)}, bf16[1,4,48,384]{3,2,1,0:T(8,128)(2,1)S(1)}, u32[]{:S(2)}, u32[]{:S(2)}) collective-permute-start(bf16[1,4,48,384]{3,2,1,0:T(8,128)(2,1)S(1)} %get-tuple-element.65), channel_id=1, source_target_pairs={{0,128},{64,192},{128,0},{192,64},{1,129},{65,193},{129,1},{193,65... | collective-permute-start | bytes 442376 | tf_op jit(solution)/shard_map/ppermute | solution.py:388
  81.6 1.5 %collective-permute-start.22 = (bf16[1,4,48,384]{3,2,1,0:T(8,128)(2,1)S(1)}, bf16[1,4,48,384]{3,2,1,0:T(8,128)(2,1)S(1)}, u32[]{:S(2)}, u32[]{:S(2)}) collective-permute-start(bf16[1,4,48,384]{3,2,1,0:T(8,128)(2,1)S(1)} %get-tuple-element.66), channel_id=1, source_target_pairs={{0,192},{64,0},{128,64},{192,128},{1,193},{65,1},{129,65},{193,129... | collective-permute-start | bytes 442376 | tf_op jit(solution)/shard_map/ppermute | solution.py:388
  83.1 2.6 %collective-permute-start.17 = (bf16[1,4,32,384]{3,2,1,0:T(8,128)(2,1)S(1)}, bf16[1,4,32,384]{3,2,1,0:T(8,128)(2,1)S(1)}, u32[]{:S(2)}, u32[]{:S(2)}) collective-permute-start(bf16[1,4,32,384]{3,2,1,0:T(8,128)(2,1)S(1)} %get-tuple-element.60), channel_id=1, source_target_pairs={{0,16},{8,24},{16,0},{24,8},{1,17},{9,25},{17,1},{25,9},{2,18},{10... | collective-permute-start | bytes 294920 | tf_op jit(solution)/shard_map/ppermute | solution.py:390
  86.1 3.2 %collective-permute-done.17.refs_2_ = bf16[1,4,32,384]{3,2,1,0:T(8,128)(2,1)S(1)} collective-permute-done((bf16[1,4,32,384]{3,2,1,0:T(8,128)(2,1)S(1)}, bf16[1,4,32,384]{3,2,1,0:T(8,128)(2,1)S(1)}, u32[]{:S(2)}, u32[]{:S(2)}) %collective-permute-start.17) | collective-permute-done | bytes 98336 | tf_op jit(solution)/shard_map/ppermute | solution.py:390
  90.5 20.1 %all_to_all.20.in_ref = bf16[8,80,384]{2,1,0:T(8,128)(2,1)S(1)} all-to-all(bf16[8,80,384]{2,1,0:T(8,128)(2,1)S(1)} %sum_plane.1), channel_id=1, replica_groups=mesh['x'=4,'zh'=2,'y'=4,'zl'=4,'core'=2] {'zh','zl'}, dimensions={0} | all-to-all | bytes 983040 | tf_op jit(solution)/shard_map/all_to_all | solution.py:392
  111.6 6.4 %all-to-all-start.3 = ((bf16[16,80,384]{2,1,0:T(8,128)(2,1)}), bf16[16,80,384]{2,1,0:T(8,128)(2,1)S(1)}, u32[]{:S(2)}, u32[]{:S(2)}) async-start(bf16[16,80,384]{2,1,0:T(8,128)(2,1)} %get-tuple-element.67), calls=%async_computation.3 | async-start | bytes 1966080 | tf_op jit(solution)/shard_map/all_to_all | solution.py:398
  119.7 10.8 %all-to-all-done.3.in_ref = bf16[16,80,384]{2,1,0:T(8,128)(2,1)S(1)} async-done(((bf16[16,80,384]{2,1,0:T(8,128)(2,1)}), bf16[16,80,384]{2,1,0:T(8,128)(2,1)S(1)}, u32[]{:S(2)}, u32[]{:S(2)}) %all-to-all-start.3) | async-done | bytes 983072 | tf_op jit(solution)/shard_map/all_to_all | solution.py:398
  (66 shorter events, 21.2 us)
Async XLA Ops:
  0.6 12.3 %collective-permute-start = (bf16[4,320,120]{2,1,0:T(8,128)(2,1)}, bf16[4,320,120]{2,1,0:T(8,128)(2,1)S(1)}, u32[]{:S(2)}, u32[]{:S(2)}) collective-permute-start(bf16[4,320,120]{2,1,0:T(8,128)(2,1)} %bitcast.35), channel_id=1, source_target_pairs={{0,1},{1,0},{2,3},{3,2},{4,5},{5,4},{6,7},{7,6},{8,9},{9,8},{10,11... | collective-permute-start | bytes 921608 | tf_op jit(solution)/shard_map/ppermute | solution.py:337
  0.7 18.8 %collective-permute-start.1 = (bf16[4,320,120]{2,1,0:T(8,128)(2,1)}, bf16[4,320,120]{2,1,0:T(8,128)(2,1)}, u32[]{:S(2)}, u32[]{:S(2)}) collective-permute-start(bf16[4,320,120]{2,1,0:T(8,128)(2,1)} %bitcast.36), channel_id=1, source_target_pairs={{0,2},{2,4},{4,6},{6,32},{32,34},{34,36},{36,38},{38,0},{1,3},{3,5... | collective-permute-start | bytes 921608 | tf_op jit(solution)/shard_map/ppermute | solution.py:340
  2.7 17.8 %collective-permute-start.2 = (bf16[4,320,120]{2,1,0:T(8,128)(2,1)}, bf16[4,320,120]{2,1,0:T(8,128)(2,1)}, u32[]{:S(2)}, u32[]{:S(2)}) collective-permute-start(bf16[4,320,120]{2,1,0:T(8,128)(2,1)} %bitcast.37), channel_id=1, source_target_pairs={{0,4},{1,37},{2,6},{3,39},{4,32},{5,1},{6,34},{7,3},{32,36},{33,5}... | collective-permute-start | bytes 921608 | tf_op jit(solution)/shard_map/ppermute | solution.py:343
  6.0 14.5 %collective-permute-start.3 = (bf16[4,320,120]{2,1,0:T(8,128)(2,1)}, bf16[4,320,120]{2,1,0:T(8,128)(2,1)}, u32[]{:S(2)}, u32[]{:S(2)}) collective-permute-start(bf16[4,320,120]{2,1,0:T(8,128)(2,1)} %bitcast.38), channel_id=1, source_target_pairs={{0,38},{2,0},{4,2},{6,4},{32,6},{34,32},{36,34},{38,36},{1,39},{3,... | collective-permute-start | bytes 921608 | tf_op jit(solution)/shard_map/ppermute | solution.py:341
  20.5 31.8 %all-to-all-start = ((bf16[4,15,48,320]{3,2,1,0:T(8,128)(2,1)}), bf16[4,15,48,320]{3,2,1,0:T(8,128)(2,1)S(1)}, u32[]{:S(2)}, u32[]{:S(2)}) async-start(bf16[4,15,48,320]{3,2,1,0:T(8,128)(2,1)} %bitcast.32), calls=%async_computation | async-start | bytes 4423680 | tf_op jit(solution)/shard_map/all_to_all | solution.py:360
  25.6 6.5 %collective-permute-start.4 = (bf16[4,320,120]{2,1,0:T(8,128)(2,1)}, bf16[4,320,120]{2,1,0:T(8,128)(2,1)}, u32[]{:S(2)}, u32[]{:S(2)}) collective-permute-start(bf16[4,320,120]{2,1,0:T(8,128)(2,1)} %collective-permute-done.1.refs_1_), channel_id=1, source_target_pairs={{0,1},{1,0},{2,3},{3,2},{4,5},{5,4},{6,7},{7,6},{8,9},{9,8},{10,11... | collective-permute-start | bytes 921608 | tf_op jit(solution)/shard_map/ppermute | solution.py:337
  27.3 6.2 %collective-permute-start.5 = (bf16[4,320,120]{2,1,0:T(8,128)(2,1)}, bf16[4,320,120]{2,1,0:T(8,128)(2,1)}, u32[]{:S(2)}, u32[]{:S(2)}) collective-permute-start(bf16[4,320,120]{2,1,0:T(8,128)(2,1)} %collective-permute-done.2.refs_3_), channel_id=1, source_target_pairs={{0,1},{1,0},{2,3},{3,2},{4,5},{5,4},{6,7},{7,6},{8,9},{9,8},{10,11... | collective-permute-start | bytes 921608 | tf_op jit(solution)/shard_map/ppermute | solution.py:337
  27.3 11.3 %collective-permute-start.6 = (bf16[4,320,120]{2,1,0:T(8,128)(2,1)}, bf16[4,320,120]{2,1,0:T(8,128)(2,1)}, u32[]{:S(2)}, u32[]{:S(2)}) collective-permute-start(bf16[4,320,120]{2,1,0:T(8,128)(2,1)} %collective-permute-done.3.refs_5_), channel_id=1, source_target_pairs={{0,1},{1,0},{2,3},{3,2},{4,5},{5,4},{6,7},{7,6},{8,9},{9,8},{10,11... | collective-permute-start | bytes 921608 | tf_op jit(solution)/shard_map/ppermute | solution.py:337
  27.8 20.6 %collective-permute-start.8 = (bf16[15,32,320]{2,1,0:T(8,128)(2,1)}, bf16[15,32,320]{2,1,0:T(8,128)(2,1)S(1)}, u32[]{:S(2)}, u32[]{:S(2)}) collective-permute-start(bf16[15,32,320]{2,1,0:T(8,128)(2,1)} %get-tuple-element.46), channel_id=1, source_target_pairs={{0,64},{64,128},{128,192},{192,0},{1,65},{65,129},{129,193},{193,1... | collective-permute-start | bytes 921608 | tf_op jit(solution)/shard_map/ppermute | solution.py:358
  29.3 19.3 %collective-permute-start.9 = (bf16[15,32,320]{2,1,0:T(8,128)(2,1)}, bf16[15,32,320]{2,1,0:T(8,128)(2,1)S(1)}, u32[]{:S(2)}, u32[]{:S(2)}) collective-permute-start(bf16[15,32,320]{2,1,0:T(8,128)(2,1)} %get-tuple-element.47), channel_id=1, source_target_pairs={{0,128},{64,192},{128,0},{192,64},{1,129},{65,193},{129,1},{193,65... | collective-permute-start | bytes 921608 | tf_op jit(solution)/shard_map/ppermute | solution.py:358
  32.1 16.6 %collective-permute-start.10 = (bf16[15,32,320]{2,1,0:T(8,128)(2,1)}, bf16[15,32,320]{2,1,0:T(8,128)(2,1)}, u32[]{:S(2)}, u32[]{:S(2)}) collective-permute-start(bf16[15,32,320]{2,1,0:T(8,128)(2,1)} %get-tuple-element.48), channel_id=1, source_target_pairs={{0,192},{64,0},{128,64},{192,128},{1,193},{65,1},{129,65},{193,129... | collective-permute-start | bytes 921608 | tf_op jit(solution)/shard_map/ppermute | solution.py:358
  33.5 14.9 %collective-permute-start.7 = (bf16[48,128]{1,0:T(8,128)(2,1)S(1)}, bf16[48,128]{1,0:T(8,128)(2,1)S(1)}, u32[]{:S(2)}, u32[]{:S(2)}) collective-permute-start(bf16[48,128]{1,0:T(8,128)(2,1)S(1)} %pad.4.near_ref), channel_id=1, source_target_pairs={{0,32},{32,0},{1,33},{33,1},{2,34},{34,2},{3,35},{35,3},{4,36},{36... | collective-permute-start | bytes 36872 | tf_op jit(solution)/shard_map/ppermute | solution.py:370
  52.4 23.0 %collective-permute-start.19 = (bf16[4,15,48,320]{3,2,1,0:T(8,128)(2,1)S(1)}, bf16[4,15,48,320]{3,2,1,0:T(8,128)(2,1)}, u32[]{:S(2)}, u32[]{:S(2)}) collective-permute-start(bf16[4,15,48,320]{3,2,1,0:T(8,128)(2,1)S(1)} %all-to-all-done.refs_0_), channel_id=1, source_target_pairs={{0,1},{1,0},{2,3},{3,2},{4,5},{5,4},{6,7},{7,6},{8,9},{9,8},{10,11... | collective-permute-start | bytes 5529608 | tf_op jit(solution)/shard_map/ppermute | solution.py:337
  54.5 16.4 %all-to-all-start.1 = ((bf16[16,112,128]{2,1,0:T(8,128)(2,1)}), bf16[16,112,128]{2,1,0:T(8,128)(2,1)S(1)}, u32[]{:S(2)}, u32[]{:S(2)}) async-start(bf16[16,112,128]{2,1,0:T(8,128)(2,1)} %copies.1), calls=%async_computation.1 | async-start | bytes 917504 | tf_op jit(solution)/shard_map/all_to_all | solution.py:377
  61.0 2.9 %collective-permute-start.13 = (bf16[15,32,320]{2,1,0:T(8,128)(2,1)S(1)}, bf16[15,32,320]{2,1,0:T(8,128)(2,1)}, u32[]{:S(2)}, u32[]{:S(2)}) collective-permute-start(bf16[15,32,320]{2,1,0:T(8,128)(2,1)S(1)} %collective-permute-done.8.refs_1_), channel_id=1, source_target_pairs={{0,1},{1,0},{2,3},{3,2},{4,5},{5,4},{6,7},{7,6},{8,9},{9,8},{10,11... | collective-permute-start | bytes 921608 | tf_op jit(solution)/shard_map/ppermute | solution.py:337
  61.5 2.6 %collective-permute-start.14 = (bf16[15,32,320]{2,1,0:T(8,128)(2,1)}, bf16[15,32,320]{2,1,0:T(8,128)(2,1)}, u32[]{:S(2)}, u32[]{:S(2)}) collective-permute-start(bf16[15,32,320]{2,1,0:T(8,128)(2,1)} %copy-done), channel_id=1, source_target_pairs={{0,1},{1,0},{2,3},{3,2},{4,5},{5,4},{6,7},{7,6},{8,9},{9,8},{10,11... | collective-permute-start | bytes 921608 | tf_op jit(solution)/shard_map/ppermute | solution.py:337
  61.6 3.0 %collective-permute-start.15 = (bf16[15,32,320]{2,1,0:T(8,128)(2,1)}, bf16[15,32,320]{2,1,0:T(8,128)(2,1)}, u32[]{:S(2)}, u32[]{:S(2)}) collective-permute-start(bf16[15,32,320]{2,1,0:T(8,128)(2,1)} %collective-permute-done.10.refs_3_), channel_id=1, source_target_pairs={{0,1},{1,0},{2,3},{3,2},{4,5},{5,4},{6,7},{7,6},{8,9},{9,8},{10,11... | collective-permute-start | bytes 921608 | tf_op jit(solution)/shard_map/ppermute | solution.py:337
  74.7 11.0 %collective-permute-start.16 = (bf16[1,4,32,384]{3,2,1,0:T(8,128)(2,1)S(1)}, bf16[1,4,32,384]{3,2,1,0:T(8,128)(2,1)S(1)}, u32[]{:S(2)}, u32[]{:S(2)}) collective-permute-start(bf16[1,4,32,384]{3,2,1,0:T(8,128)(2,1)S(1)} %get-tuple-element.59), channel_id=1, source_target_pairs={{0,8},{8,16},{16,24},{24,0},{1,9},{9,17},{17,25},{25,1},{2,10},{10... | collective-permute-start | bytes 294920 | tf_op jit(solution)/shard_map/ppermute | solution.py:390
  78.9 11.4 %collective-permute-start.20 = (bf16[1,4,48,384]{3,2,1,0:T(8,128)(2,1)S(1)}, bf16[1,4,48,384]{3,2,1,0:T(8,128)(2,1)S(1)}, u32[]{:S(2)}, u32[]{:S(2)}) collective-permute-start(bf16[1,4,48,384]{3,2,1,0:T(8,128)(2,1)S(1)} %get-tuple-element.64), channel_id=1, source_target_pairs={{0,64},{64,128},{128,192},{192,0},{1,65},{65,129},{129,193},{193,1... | collective-permute-start | bytes 442376 | tf_op jit(solution)/shard_map/ppermute | solution.py:388
  79.3 11.0 %collective-permute-start.21 = (bf16[1,4,48,384]{3,2,1,0:T(8,128)(2,1)S(1)}, bf16[1,4,48,384]{3,2,1,0:T(8,128)(2,1)S(1)}, u32[]{:S(2)}, u32[]{:S(2)}) collective-permute-start(bf16[1,4,48,384]{3,2,1,0:T(8,128)(2,1)S(1)} %get-tuple-element.65), channel_id=1, source_target_pairs={{0,128},{64,192},{128,0},{192,64},{1,129},{65,193},{129,1},{193,65... | collective-permute-start | bytes 442376 | tf_op jit(solution)/shard_map/ppermute | solution.py:388
  81.6 8.7 %collective-permute-start.22 = (bf16[1,4,48,384]{3,2,1,0:T(8,128)(2,1)S(1)}, bf16[1,4,48,384]{3,2,1,0:T(8,128)(2,1)S(1)}, u32[]{:S(2)}, u32[]{:S(2)}) collective-permute-start(bf16[1,4,48,384]{3,2,1,0:T(8,128)(2,1)S(1)} %get-tuple-element.66), channel_id=1, source_target_pairs={{0,192},{64,0},{128,64},{192,128},{1,193},{65,1},{129,65},{193,129... | collective-permute-start | bytes 442376 | tf_op jit(solution)/shard_map/ppermute | solution.py:388
  83.1 6.1 %collective-permute-start.17 = (bf16[1,4,32,384]{3,2,1,0:T(8,128)(2,1)S(1)}, bf16[1,4,32,384]{3,2,1,0:T(8,128)(2,1)S(1)}, u32[]{:S(2)}, u32[]{:S(2)}) collective-permute-start(bf16[1,4,32,384]{3,2,1,0:T(8,128)(2,1)S(1)} %get-tuple-element.60), channel_id=1, source_target_pairs={{0,16},{8,24},{16,0},{24,8},{1,17},{9,25},{17,1},{25,9},{2,18},{10... | collective-permute-start | bytes 294920 | tf_op jit(solution)/shard_map/ppermute | solution.py:390
  85.7 4.6 %collective-permute-start.18 = (bf16[1,4,32,384]{3,2,1,0:T(8,128)(2,1)S(1)}, bf16[1,4,32,384]{3,2,1,0:T(8,128)(2,1)S(1)}, u32[]{:S(2)}, u32[]{:S(2)}) collective-permute-start(bf16[1,4,32,384]{3,2,1,0:T(8,128)(2,1)S(1)} %get-tuple-element.61), channel_id=1, source_target_pairs={{0,24},{8,0},{16,8},{24,16},{1,25},{9,1},{17,9},{25,17},{2,26},{10... | collective-permute-start | bytes 294920 | tf_op jit(solution)/shard_map/ppermute | solution.py:390
  111.6 18.9 %all-to-all-start.3 = ((bf16[16,80,384]{2,1,0:T(8,128)(2,1)}), bf16[16,80,384]{2,1,0:T(8,128)(2,1)S(1)}, u32[]{:S(2)}, u32[]{:S(2)}) async-start(bf16[16,80,384]{2,1,0:T(8,128)(2,1)} %get-tuple-element.67), calls=%async_computation.3 | async-start | bytes 1966080 | tf_op jit(solution)/shard_map/all_to_all | solution.py:398
  (9 other events, 27.2 us)

commit v6 on v5

--- a/solution.py
+++ b/solution.py
@@ -239,7 +239,6 @@
 
 
 def sum_kernel(copies, message_ref, *refs):
-    upper = lax.broadcasted_iota(jnp.int32, (TILE, 128), 1) >= 64
     scalars = message_ref[0, 0:TILE].astype(f32)
     for s in range(1, message_ref.shape[0]):
         scalars = scalars + message_ref[s, 0:TILE].astype(f32)
@@ -248,25 +247,28 @@
     pieces = [ref.at[i] for ref in refs[:-1] for i in range(ref.shape[0])]
     firsts, seconds = pieces[:4], pieces[4:]
     groups, rows = firsts[0].shape[:2]
+    rest = seconds[0].shape[1]
+    lower = lax.broadcasted_iota(jnp.int32, (rest, 128), 1) < 64
     for g in range(groups):
         total = firsts[0][g].astype(f32)
         below = seconds[0][g].astype(f32)
         for s in range(1, 4):
             total = total + firsts[s][g].astype(f32)
             below = below + seconds[s][g].astype(f32)
-        corner = jnp.where(upper, scalars, total[0:TILE, 256:WIDE]).astype(bf16)
-        total, below = total.astype(bf16), below.astype(bf16)
+        last = jnp.concatenate([pltpu.roll(total[:, 256:WIDE], 64, 1), scalars])
+        last = jnp.where(lower, below[:, 256:WIDE], last)
+        packed = [total[:, 0:128], below[:, 0:128], total[:, 128:256], below[:, 128:256], last]
+        packed = jnp.concatenate(packed).astype(bf16)
         for k in range(g, copies, groups):
-            out_ref[k, 0:rows] = total
-            out_ref[k, rows:] = below
-            out_ref[k, 0:TILE, 256:WIDE] = corner
+            out_ref[k] = packed
 
 
 def sum_second_axis(message, first, second):
-    rows, wide = first[0].shape[2] + second[0].shape[2], first[0].shape[3]
+    rows, rest = first[0].shape[2], second[0].shape[2]
+    assert rows + TILE == rest
     return pl.pallas_call(
         functools.partial(sum_kernel, 8),
-        out_shape=jax.ShapeDtypeStruct((8, rows, wide), bf16),
+        out_shape=jax.ShapeDtypeStruct((8, 2 * rows + 3 * rest, 128), bf16),
         compiler_params=pltpu.CompilerParams(vmem_limit_bytes=16 * 2**20),
         name="sum_plane",
     )(message, *first, *second)
@@ -277,7 +279,7 @@
     for s in range(1, in_ref.shape[0]):
         total = total + in_ref[s].astype(f32)
     rounded = total.astype(bf16)
-    scalars_ref[...] = jnp.sum(total[0:TILE, 256:WIDE], axis=0, keepdims=True)
+    scalars_ref[...] = jnp.sum(total[total.shape[0] - TILE :], axis=0, keepdims=True)
     for k in range(out_ref.shape[0]):
         out_ref[k] = rounded
 
@@ -295,12 +297,25 @@
     )(received)
 
 
-def taylor_kernel(first_rows, in_ref, walkers_ref, out_ref):
+def taylor_kernel(rows, in_ref, walkers_ref, out_ref):
     orbitals = walkers_ref.shape[1]
+    rest = orbitals // 4 - rows
+    end = 2 * (rows + rest)
+
+    def first_part(k):
+        last = pltpu.roll(in_ref[k, end : end + rows].astype(f32), 64, 1).astype(bf16)
+        return jnp.concatenate(
+            [in_ref[k, 0:rows], in_ref[k, rows + rest : 2 * rows + rest], last], axis=1
+        )
+
+    def second_part(k):
+        return jnp.concatenate(
+            [in_ref[k, rows : rows + rest], in_ref[k, 2 * rows + rest : end], in_ref[k, end:]], axis=1
+        )
+
     fields = [
         jnp.concatenate(
-            [in_ref[4 * k + w, 0:first_rows] for k in range(4)]
-            + [in_ref[4 * w + k, first_rows:] for k in range(4)]
+            [first_part(4 * k + w) for k in range(4)] + [second_part(4 * w + k) for k in range(4)]
         )[:, 0:orbitals]
         for w in range(4)
     ]

time: 133 us -> 130 us (0.977)
  waiting for transfers between devices: 27.2 us -> 25.7 us
  blocking collectives: 20.1 us -> 18.7 us
    all_to_all x1, waiting for transfers between devices: 10.8 us -> 9.19 us  [on_device(): field = lax.all_to_all(field, ('x', 'y'), 0, 0)]
    all_to_all x1, blocking collectives: 20.1 us -> 18.7 us  [on_device(): field = lax.all_to_all(field, Z, 0, 0)]
where the time goes in v6:
time: 130 us; the launch traced here: 129 us
  starting transfers between devices  46.4 us (36%)
  Pallas kernels  27.6 us (21%)
  waiting for transfers between devices  25.7 us (20%)
  blocking collectives  18.7 us (14%)
  local copies, waits for them, and re-layouts  9.64 us (7%)
    all_to_all x1, blocking collectives, on_device(): field = lax.all_to_all(field, Z, 0, 0)  18.7 us
    pallas_call x2, Pallas kernels, pair_sums(): pl.pallas_call(functools.partial(pair_kernel, vectors, first, 1 + len(gre...  15.6 us
    all_to_all x1, waiting for transfers between devices, on_device(): field = lax.all_to_all(field, ('x', 'y'), 0, 0)  9.19 us
    all_to_all x1, starting transfers between devices, on_device(): message = lax.all_to_all(message, ('x', 'y'), 0, 0)  6.51 us
    all_to_all x1, starting transfers between devices, on_device(): field = lax.all_to_all(field, ('x', 'y'), 0, 0)  6.42 us
    pallas_call x2, Pallas kernels, field_rows(): pl.pallas_call(functools.partial(field_kernel, vectors), out_shape=[jax.S...  6.35 us
    all_to_all x1, waiting for transfers between devices, on_device(): message = lax.all_to_all(message, ('x', 'y'), 0, 0)  6.32 us
    ppermute x3, starting transfers between devices, on_device(): lax.ppermute(after(first_pieces[k], beside), 'x', ring(4, k))  5.66 us
  transfers between devices with their start and end apart: 27, of which 12 were waited for; matrix products, arithmetic and copies ran while one was open for 4% of the time, Pallas kernels for 19%

profile of v6, /device:TPU:8, one launch (start us, length us, event | category | flops | bytes accessed | tf_op | source)
XLA Modules:
  0.0 129.4 jit_solution(14305570630907981677)
XLA Ops:
  0.7 2.0 %collective-permute-start.1 = (bf16[4,320,120]{2,1,0:T(8,128)(2,1)}, bf16[4,320,120]{2,1,0:T(8,128)(2,1)}, u32[]{:S(2)}, u32[]{:S(2)}) collective-permute-start(bf16[4,320,120]{2,1,0:T(8,128)(2,1)} %bitcast.36), channel_id=1, source_target_pairs={{0,2},{2,4},{4,6},{6,32},{32,34},{34,36},{36,38},{38,0},{1,3},{3,5... | collective-permute-start | bytes 921608 | tf_op jit(solution)/shard_map/ppermute | solution.py:355
  2.7 3.3 %collective-permute-start.2 = (bf16[4,320,120]{2,1,0:T(8,128)(2,1)}, bf16[4,320,120]{2,1,0:T(8,128)(2,1)}, u32[]{:S(2)}, u32[]{:S(2)}) collective-permute-start(bf16[4,320,120]{2,1,0:T(8,128)(2,1)} %bitcast.37), channel_id=1, source_target_pairs={{0,4},{1,37},{2,6},{3,39},{4,32},{5,1},{6,34},{7,3},{32,36},{33,5}... | collective-permute-start | bytes 921608 | tf_op jit(solution)/shard_map/ppermute | solution.py:358
  7.3 1.6 %slice-done = bf16[15,192,320]{2,1,0:T(8,128)(2,1)S(1)} async-done(((bf16[15,320,320]{2,1,0:T(8,128)(2,1)}), bf16[15,192,320]{2,1,0:T(8,128)(2,1)S(1)}, s32[]{:S(2)}) %slice-start) | async-done | bytes 1843224 | tf_op jit(solution)/shard_map/slice | solution.py:366
  8.9 1.6 %copy.15 = bf16[15,4,48,320]{3,2,0,1:T(8,128)(2,1)} copy(bf16[15,4,48,320]{3,2,1,0:T(8,128)(2,1)S(1)} %bitcast.33) | data formatting | bytes 3686400 | tf_op jit(solution)/shard_map/reshape | solution.py:366
  10.5 2.4 %constant_dynamic-slice_fusion.1 = (bf16[15,32,320]{2,1,0:T(8,128)(2,1)}, bf16[15,32,320]{2,1,0:T(8,128)(2,1)}, bf16[15,32,320]{2,1,0:T(8,128)(2,1)}, bf16[15,32,320]{2,1,0:T(8,128)(2,1)S(1)}) fusion(bf16[15,320,320]{2,1,0:T(8,128)(2,1)} %param.9, s32[]{:T(128)S(6)} %select_n.18, s32[]{:T(128)S(6)} %select_n.17, s32[]{:T(128)S(6)} %select_n.16, s32[]{:T(128)S(6)} %select_n.15), kind=kLoop, calls=%fused_computation.2 | loop fusion | bytes 2457616 | tf_op jit(solution)/shard_map/dynamic_slice | solution.py:363
  13.7 5.8 %pairs.2 = (f32[8,15,128]{2,1,0:T(8,128)}, f32[8,8,128]{2,1,0:T(8,128)}, bf16[15,128,320]{2,1,0:T(8,128)(2,1)}) custom-call(bf16[15,320,120]{2,1,0:T(8,128)(2,1)} %bitcast.43, bf16[4,320,120]{2,1,0:T(8,128)(2,1)} %bitcast.39, bf16[4,320,120]{2,1,0:T(8,128)(2,1)} %copy-done.3), custom_call_target="tpu_custom_call" | custom-call | flops 1 | bytes 1 | tf_op jit(solution)/shard_map/pairs/pallas_call | solution.py:97
  20.5 5.0 %all-to-all-start = ((bf16[4,15,48,320]{3,2,1,0:T(8,128)(2,1)}), bf16[4,15,48,320]{3,2,1,0:T(8,128)(2,1)S(1)}, u32[]{:S(2)}, u32[]{:S(2)}) async-start(bf16[4,15,48,320]{3,2,1,0:T(8,128)(2,1)} %bitcast.32), calls=%async_computation | async-start | bytes 4423680 | tf_op jit(solution)/shard_map/all_to_all | solution.py:375
  25.6 1.8 %collective-permute-start.4 = (bf16[4,320,120]{2,1,0:T(8,128)(2,1)}, bf16[4,320,120]{2,1,0:T(8,128)(2,1)}, u32[]{:S(2)}, u32[]{:S(2)}) collective-permute-start(bf16[4,320,120]{2,1,0:T(8,128)(2,1)} %collective-permute-done.1.refs_1_), channel_id=1, source_target_pairs={{0,1},{1,0},{2,3},{3,2},{4,5},{5,4},{6,7},{7,6},{8,9},{9,8},{10,11... | collective-permute-start | bytes 921608 | tf_op jit(solution)/shard_map/ppermute | solution.py:352
  27.8 1.5 %collective-permute-start.8 = (bf16[15,32,320]{2,1,0:T(8,128)(2,1)}, bf16[15,32,320]{2,1,0:T(8,128)(2,1)S(1)}, u32[]{:S(2)}, u32[]{:S(2)}) collective-permute-start(bf16[15,32,320]{2,1,0:T(8,128)(2,1)} %get-tuple-element.46), channel_id=1, source_target_pairs={{0,64},{64,128},{128,192},{192,0},{1,65},{65,129},{129,193},{193,1... | collective-permute-start | bytes 921608 | tf_op jit(solution)/shard_map/ppermute | solution.py:373
  29.3 2.7 %collective-permute-start.9 = (bf16[15,32,320]{2,1,0:T(8,128)(2,1)}, bf16[15,32,320]{2,1,0:T(8,128)(2,1)S(1)}, u32[]{:S(2)}, u32[]{:S(2)}) collective-permute-start(bf16[15,32,320]{2,1,0:T(8,128)(2,1)} %get-tuple-element.47), channel_id=1, source_target_pairs={{0,128},{64,192},{128,0},{192,64},{1,129},{65,193},{129,1},{193,65... | collective-permute-start | bytes 921608 | tf_op jit(solution)/shard_map/ppermute | solution.py:373
  33.5 4.5 %collective-permute-start.7 = (bf16[48,128]{1,0:T(8,128)(2,1)S(1)}, bf16[48,128]{1,0:T(8,128)(2,1)S(1)}, u32[]{:S(2)}, u32[]{:S(2)}) collective-permute-start(bf16[48,128]{1,0:T(8,128)(2,1)S(1)} %pad.4.near_ref), channel_id=1, source_target_pairs={{0,32},{32,0},{1,33},{33,1},{2,34},{34,2},{3,35},{35,3},{4,36},{36... | collective-permute-start | bytes 36872 | tf_op jit(solution)/shard_map/ppermute | solution.py:385
  38.6 9.8 %pairs.3 = (f32[24,15,128]{2,1,0:T(8,128)}, f32[24,8,128]{2,1,0:T(8,128)}) custom-call(bf16[15,128,320]{2,1,0:T(8,128)(2,1)} %get-tuple-element.38.refs_0_, bf16[4,320,120]{2,1,0:T(8,128)(2,1)} %collective-permute-done.1.refs_1_, bf16[4,320,120]{2,1,0:T(8,128)(2,1)} %collective-permute-done.4.refs_2_, bf16[4,320,120]{2,1,0:T(8,128)(2,1)} %collective-permute-done.2.refs_3_, ...), custom_call_target="tpu_custom_call" | custom-call | flops 1 | bytes 1 | tf_op jit(solution)/shard_map/pairs/pallas_call | solution.py:97
  48.6 2.3 %message.1 = (bf16[16,128]{1,0:T(8,128)(2,1)}, bf16[16,128]{1,0:T(8,128)(2,1)}) custom-call(s32[2]{0:T(128)} %pad_add_fusion.place_ref, f32[8,15,128]{2,1,0:T(8,128)} %get-tuple-element.37.refs_0_, f32[24,15,128]{2,1,0:T(8,128)} %get-tuple-element.42.refs_1_, f32[8,8,128]{2,1,0:T(8,128)} %get-tuple-element.43.refs_2_, ...), custom_call_target="tpu_custom_call" | custom-call | tf_op jit(solution)/shard_map/message/pallas_call | solution.py:153
  54.5 6.5 %all-to-all-start.1 = ((bf16[16,112,128]{2,1,0:T(8,128)(2,1)}), bf16[16,112,128]{2,1,0:T(8,128)(2,1)S(1)}, u32[]{:S(2)}, u32[]{:S(2)}) async-start(bf16[16,112,128]{2,1,0:T(8,128)(2,1)} %copies.1), calls=%async_computation.1 | async-start | bytes 917504 | tf_op jit(solution)/shard_map/all_to_all | solution.py:392
  64.6 6.3 %all-to-all-done.1.message_ref = bf16[16,112,128]{2,1,0:T(8,128)(2,1)S(1)} async-done(((bf16[16,112,128]{2,1,0:T(8,128)(2,1)}), bf16[16,112,128]{2,1,0:T(8,128)(2,1)S(1)}, u32[]{:S(2)}, u32[]{:S(2)}) %all-to-all-start.1) | async-done | bytes 458784 | tf_op jit(solution)/shard_map/all_to_all | solution.py:392
  71.9 2.8 %field_rows.2 = (bf16[1,4,32,384]{3,2,1,0:T(8,128)(2,1)S(1)}, bf16[1,4,32,384]{3,2,1,0:T(8,128)(2,1)S(1)}, bf16[1,4,32,384]{3,2,1,0:T(8,128)(2,1)S(1)}, bf16[1,4,32,384]{3,2,1,0:T(8,128)(2,1)S(1)}) custom-call(s32[5]{0:T(128)S(1)} %stack.57.place_ref, bf16[16,112,128]{2,1,0:T(8,128)(2,1)S(1)} %all-to-all-done.1.message_ref, ...), custom_call_target="tpu_custom_call" | custom-call | flops 805306368 | bytes 1280000 | tf_op jit(solution)/shard_map/field_rows/pallas_call | solution.py:228
  75.4 3.6 %field_rows.3 = (bf16[1,4,48,384]{3,2,1,0:T(8,128)(2,1)S(1)}, bf16[1,4,48,384]{3,2,1,0:T(8,128)(2,1)S(1)}, bf16[1,4,48,384]{3,2,1,0:T(8,128)(2,1)S(1)}, bf16[1,4,48,384]{3,2,1,0:T(8,128)(2,1)S(1)}) custom-call(s32[5]{0:T(128)S(1)} %stack.63.place_ref, bf16[16,112,128]{2,1,0:T(8,128)(2,1)S(1)} %all-to-all-done.1.message_ref, ...), custom_call_target="tpu_custom_call" | custom-call | flops 1207959552 | bytes 1920000 | tf_op jit(solution)/shard_map/field_rows/pallas_call | solution.py:228
  79.3 2.3 %collective-permute-start.21 = (bf16[1,4,48,384]{3,2,1,0:T(8,128)(2,1)S(1)}, bf16[1,4,48,384]{3,2,1,0:T(8,128)(2,1)S(1)}, u32[]{:S(2)}, u32[]{:S(2)}) collective-permute-start(bf16[1,4,48,384]{3,2,1,0:T(8,128)(2,1)S(1)} %get-tuple-element.65), channel_id=1, source_target_pairs={{0,128},{64,192},{128,0},{192,64},{1,129},{65,193},{129,1},{193,65... | collective-permute-start | bytes 442376 | tf_op jit(solution)/shard_map/ppermute | solution.py:403
  81.6 1.5 %collective-permute-start.22 = (bf16[1,4,48,384]{3,2,1,0:T(8,128)(2,1)S(1)}, bf16[1,4,48,384]{3,2,1,0:T(8,128)(2,1)S(1)}, u32[]{:S(2)}, u32[]{:S(2)}) collective-permute-start(bf16[1,4,48,384]{3,2,1,0:T(8,128)(2,1)S(1)} %get-tuple-element.66), channel_id=1, source_target_pairs={{0,192},{64,0},{128,64},{192,128},{1,193},{65,1},{129,65},{193,129... | collective-permute-start | bytes 442376 | tf_op jit(solution)/shard_map/ppermute | solution.py:403
  83.1 2.6 %collective-permute-start.17 = (bf16[1,4,32,384]{3,2,1,0:T(8,128)(2,1)S(1)}, bf16[1,4,32,384]{3,2,1,0:T(8,128)(2,1)S(1)}, u32[]{:S(2)}, u32[]{:S(2)}) collective-permute-start(bf16[1,4,32,384]{3,2,1,0:T(8,128)(2,1)S(1)} %get-tuple-element.60), channel_id=1, source_target_pairs={{0,16},{8,24},{16,0},{24,8},{1,17},{9,25},{17,1},{25,9},{2,18},{10... | collective-permute-start | bytes 294920 | tf_op jit(solution)/shard_map/ppermute | solution.py:405
  86.1 3.2 %collective-permute-done.17.refs_2_ = bf16[1,4,32,384]{3,2,1,0:T(8,128)(2,1)S(1)} collective-permute-done((bf16[1,4,32,384]{3,2,1,0:T(8,128)(2,1)S(1)}, bf16[1,4,32,384]{3,2,1,0:T(8,128)(2,1)S(1)}, u32[]{:S(2)}, u32[]{:S(2)}) %collective-permute-start.17) | collective-permute-done | bytes 98336 | tf_op jit(solution)/shard_map/ppermute | solution.py:405
  90.5 18.7 %all_to_all.20.in_ref = bf16[8,208,128]{2,1,0:T(8,128)(2,1)S(1)} all-to-all(bf16[8,208,128]{2,1,0:T(8,128)(2,1)S(1)} %sum_plane.1), channel_id=1, replica_groups=mesh['x'=4,'zh'=2,'y'=4,'zl'=4,'core'=2] {'zh','zl'}, dimensions={0} | all-to-all | bytes 851968 | tf_op jit(solution)/shard_map/all_to_all | solution.py:407
  110.2 6.4 %all-to-all-start.3 = ((bf16[16,208,128]{2,1,0:T(8,128)(2,1)}), bf16[16,208,128]{2,1,0:T(8,128)(2,1)S(1)}, u32[]{:S(2)}, u32[]{:S(2)}) async-start(bf16[16,208,128]{2,1,0:T(8,128)(2,1)} %get-tuple-element.67), calls=%async_computation.3 | async-start | bytes 1703936 | tf_op jit(solution)/shard_map/all_to_all | solution.py:413
  118.3 9.2 %all-to-all-done.3.in_ref = bf16[16,208,128]{2,1,0:T(8,128)(2,1)S(1)} async-done(((bf16[16,208,128]{2,1,0:T(8,128)(2,1)}), bf16[16,208,128]{2,1,0:T(8,128)(2,1)S(1)}, u32[]{:S(2)}, u32[]{:S(2)}) %all-to-all-start.3) | async-done | bytes 852000 | tf_op jit(solution)/shard_map/all_to_all | solution.py:413
  (66 shorter events, 21.2 us)
Async XLA Ops:
  0.6 12.3 %collective-permute-start = (bf16[4,320,120]{2,1,0:T(8,128)(2,1)}, bf16[4,320,120]{2,1,0:T(8,128)(2,1)S(1)}, u32[]{:S(2)}, u32[]{:S(2)}) collective-permute-start(bf16[4,320,120]{2,1,0:T(8,128)(2,1)} %bitcast.35), channel_id=1, source_target_pairs={{0,1},{1,0},{2,3},{3,2},{4,5},{5,4},{6,7},{7,6},{8,9},{9,8},{10,11... | collective-permute-start | bytes 921608 | tf_op jit(solution)/shard_map/ppermute | solution.py:352
  0.7 18.8 %collective-permute-start.1 = (bf16[4,320,120]{2,1,0:T(8,128)(2,1)}, bf16[4,320,120]{2,1,0:T(8,128)(2,1)}, u32[]{:S(2)}, u32[]{:S(2)}) collective-permute-start(bf16[4,320,120]{2,1,0:T(8,128)(2,1)} %bitcast.36), channel_id=1, source_target_pairs={{0,2},{2,4},{4,6},{6,32},{32,34},{34,36},{36,38},{38,0},{1,3},{3,5... | collective-permute-start | bytes 921608 | tf_op jit(solution)/shard_map/ppermute | solution.py:355
  2.7 17.8 %collective-permute-start.2 = (bf16[4,320,120]{2,1,0:T(8,128)(2,1)}, bf16[4,320,120]{2,1,0:T(8,128)(2,1)}, u32[]{:S(2)}, u32[]{:S(2)}) collective-permute-start(bf16[4,320,120]{2,1,0:T(8,128)(2,1)} %bitcast.37), channel_id=1, source_target_pairs={{0,4},{1,37},{2,6},{3,39},{4,32},{5,1},{6,34},{7,3},{32,36},{33,5}... | collective-permute-start | bytes 921608 | tf_op jit(solution)/shard_map/ppermute | solution.py:358
  6.0 14.5 %collective-permute-start.3 = (bf16[4,320,120]{2,1,0:T(8,128)(2,1)}, bf16[4,320,120]{2,1,0:T(8,128)(2,1)}, u32[]{:S(2)}, u32[]{:S(2)}) collective-permute-start(bf16[4,320,120]{2,1,0:T(8,128)(2,1)} %bitcast.38), channel_id=1, source_target_pairs={{0,38},{2,0},{4,2},{6,4},{32,6},{34,32},{36,34},{38,36},{1,39},{3,... | collective-permute-start | bytes 921608 | tf_op jit(solution)/shard_map/ppermute | solution.py:356
  20.5 31.8 %all-to-all-start = ((bf16[4,15,48,320]{3,2,1,0:T(8,128)(2,1)}), bf16[4,15,48,320]{3,2,1,0:T(8,128)(2,1)S(1)}, u32[]{:S(2)}, u32[]{:S(2)}) async-start(bf16[4,15,48,320]{3,2,1,0:T(8,128)(2,1)} %bitcast.32), calls=%async_computation | async-start | bytes 4423680 | tf_op jit(solution)/shard_map/all_to_all | solution.py:375
  25.6 6.5 %collective-permute-start.4 = (bf16[4,320,120]{2,1,0:T(8,128)(2,1)}, bf16[4,320,120]{2,1,0:T(8,128)(2,1)}, u32[]{:S(2)}, u32[]{:S(2)}) collective-permute-start(bf16[4,320,120]{2,1,0:T(8,128)(2,1)} %collective-permute-done.1.refs_1_), channel_id=1, source_target_pairs={{0,1},{1,0},{2,3},{3,2},{4,5},{5,4},{6,7},{7,6},{8,9},{9,8},{10,11... | collective-permute-start | bytes 921608 | tf_op jit(solution)/shard_map/ppermute | solution.py:352
  27.3 6.2 %collective-permute-start.5 = (bf16[4,320,120]{2,1,0:T(8,128)(2,1)}, bf16[4,320,120]{2,1,0:T(8,128)(2,1)}, u32[]{:S(2)}, u32[]{:S(2)}) collective-permute-start(bf16[4,320,120]{2,1,0:T(8,128)(2,1)} %collective-permute-done.2.refs_3_), channel_id=1, source_target_pairs={{0,1},{1,0},{2,3},{3,2},{4,5},{5,4},{6,7},{7,6},{8,9},{9,8},{10,11... | collective-permute-start | bytes 921608 | tf_op jit(solution)/shard_map/ppermute | solution.py:352
  27.3 11.3 %collective-permute-start.6 = (bf16[4,320,120]{2,1,0:T(8,128)(2,1)}, bf16[4,320,120]{2,1,0:T(8,128)(2,1)}, u32[]{:S(2)}, u32[]{:S(2)}) collective-permute-start(bf16[4,320,120]{2,1,0:T(8,128)(2,1)} %collective-permute-done.3.refs_5_), channel_id=1, source_target_pairs={{0,1},{1,0},{2,3},{3,2},{4,5},{5,4},{6,7},{7,6},{8,9},{9,8},{10,11... | collective-permute-start | bytes 921608 | tf_op jit(solution)/shard_map/ppermute | solution.py:352
  27.8 20.6 %collective-permute-start.8 = (bf16[15,32,320]{2,1,0:T(8,128)(2,1)}, bf16[15,32,320]{2,1,0:T(8,128)(2,1)S(1)}, u32[]{:S(2)}, u32[]{:S(2)}) collective-permute-start(bf16[15,32,320]{2,1,0:T(8,128)(2,1)} %get-tuple-element.46), channel_id=1, source_target_pairs={{0,64},{64,128},{128,192},{192,0},{1,65},{65,129},{129,193},{193,1... | collective-permute-start | bytes 921608 | tf_op jit(solution)/shard_map/ppermute | solution.py:373
  29.3 19.3 %collective-permute-start.9 = (bf16[15,32,320]{2,1,0:T(8,128)(2,1)}, bf16[15,32,320]{2,1,0:T(8,128)(2,1)S(1)}, u32[]{:S(2)}, u32[]{:S(2)}) collective-permute-start(bf16[15,32,320]{2,1,0:T(8,128)(2,1)} %get-tuple-element.47), channel_id=1, source_target_pairs={{0,128},{64,192},{128,0},{192,64},{1,129},{65,193},{129,1},{193,65... | collective-permute-start | bytes 921608 | tf_op jit(solution)/shard_map/ppermute | solution.py:373
  32.1 16.6 %collective-permute-start.10 = (bf16[15,32,320]{2,1,0:T(8,128)(2,1)}, bf16[15,32,320]{2,1,0:T(8,128)(2,1)}, u32[]{:S(2)}, u32[]{:S(2)}) collective-permute-start(bf16[15,32,320]{2,1,0:T(8,128)(2,1)} %get-tuple-element.48), channel_id=1, source_target_pairs={{0,192},{64,0},{128,64},{192,128},{1,193},{65,1},{129,65},{193,129... | collective-permute-start | bytes 921608 | tf_op jit(solution)/shard_map/ppermute | solution.py:373
  33.5 14.9 %collective-permute-start.7 = (bf16[48,128]{1,0:T(8,128)(2,1)S(1)}, bf16[48,128]{1,0:T(8,128)(2,1)S(1)}, u32[]{:S(2)}, u32[]{:S(2)}) collective-permute-start(bf16[48,128]{1,0:T(8,128)(2,1)S(1)} %pad.4.near_ref), channel_id=1, source_target_pairs={{0,32},{32,0},{1,33},{33,1},{2,34},{34,2},{3,35},{35,3},{4,36},{36... | collective-permute-start | bytes 36872 | tf_op jit(solution)/shard_map/ppermute | solution.py:385
  52.4 23.0 %collective-permute-start.19 = (bf16[4,15,48,320]{3,2,1,0:T(8,128)(2,1)S(1)}, bf16[4,15,48,320]{3,2,1,0:T(8,128)(2,1)}, u32[]{:S(2)}, u32[]{:S(2)}) collective-permute-start(bf16[4,15,48,320]{3,2,1,0:T(8,128)(2,1)S(1)} %all-to-all-done.refs_0_), channel_id=1, source_target_pairs={{0,1},{1,0},{2,3},{3,2},{4,5},{5,4},{6,7},{7,6},{8,9},{9,8},{10,11... | collective-permute-start | bytes 5529608 | tf_op jit(solution)/shard_map/ppermute | solution.py:352
  54.5 16.4 %all-to-all-start.1 = ((bf16[16,112,128]{2,1,0:T(8,128)(2,1)}), bf16[16,112,128]{2,1,0:T(8,128)(2,1)S(1)}, u32[]{:S(2)}, u32[]{:S(2)}) async-start(bf16[16,112,128]{2,1,0:T(8,128)(2,1)} %copies.1), calls=%async_computation.1 | async-start | bytes 917504 | tf_op jit(solution)/shard_map/all_to_all | solution.py:392
  61.0 2.9 %collective-permute-start.13 = (bf16[15,32,320]{2,1,0:T(8,128)(2,1)S(1)}, bf16[15,32,320]{2,1,0:T(8,128)(2,1)}, u32[]{:S(2)}, u32[]{:S(2)}) collective-permute-start(bf16[15,32,320]{2,1,0:T(8,128)(2,1)S(1)} %collective-permute-done.8.refs_1_), channel_id=1, source_target_pairs={{0,1},{1,0},{2,3},{3,2},{4,5},{5,4},{6,7},{7,6},{8,9},{9,8},{10,11... | collective-permute-start | bytes 921608 | tf_op jit(solution)/shard_map/ppermute | solution.py:352
  61.5 2.6 %collective-permute-start.14 = (bf16[15,32,320]{2,1,0:T(8,128)(2,1)}, bf16[15,32,320]{2,1,0:T(8,128)(2,1)}, u32[]{:S(2)}, u32[]{:S(2)}) collective-permute-start(bf16[15,32,320]{2,1,0:T(8,128)(2,1)} %copy-done), channel_id=1, source_target_pairs={{0,1},{1,0},{2,3},{3,2},{4,5},{5,4},{6,7},{7,6},{8,9},{9,8},{10,11... | collective-permute-start | bytes 921608 | tf_op jit(solution)/shard_map/ppermute | solution.py:352
  61.6 3.0 %collective-permute-start.15 = (bf16[15,32,320]{2,1,0:T(8,128)(2,1)}, bf16[15,32,320]{2,1,0:T(8,128)(2,1)}, u32[]{:S(2)}, u32[]{:S(2)}) collective-permute-start(bf16[15,32,320]{2,1,0:T(8,128)(2,1)} %collective-permute-done.10.refs_3_), channel_id=1, source_target_pairs={{0,1},{1,0},{2,3},{3,2},{4,5},{5,4},{6,7},{7,6},{8,9},{9,8},{10,11... | collective-permute-start | bytes 921608 | tf_op jit(solution)/shard_map/ppermute | solution.py:352
  74.7 11.0 %collective-permute-start.16 = (bf16[1,4,32,384]{3,2,1,0:T(8,128)(2,1)S(1)}, bf16[1,4,32,384]{3,2,1,0:T(8,128)(2,1)S(1)}, u32[]{:S(2)}, u32[]{:S(2)}) collective-permute-start(bf16[1,4,32,384]{3,2,1,0:T(8,128)(2,1)S(1)} %get-tuple-element.59), channel_id=1, source_target_pairs={{0,8},{8,16},{16,24},{24,0},{1,9},{9,17},{17,25},{25,1},{2,10},{10... | collective-permute-start | bytes 294920 | tf_op jit(solution)/shard_map/ppermute | solution.py:405
  78.9 11.4 %collective-permute-start.20 = (bf16[1,4,48,384]{3,2,1,0:T(8,128)(2,1)S(1)}, bf16[1,4,48,384]{3,2,1,0:T(8,128)(2,1)S(1)}, u32[]{:S(2)}, u32[]{:S(2)}) collective-permute-start(bf16[1,4,48,384]{3,2,1,0:T(8,128)(2,1)S(1)} %get-tuple-element.64), channel_id=1, source_target_pairs={{0,64},{64,128},{128,192},{192,0},{1,65},{65,129},{129,193},{193,1... | collective-permute-start | bytes 442376 | tf_op jit(solution)/shard_map/ppermute | solution.py:403
  79.3 11.0 %collective-permute-start.21 = (bf16[1,4,48,384]{3,2,1,0:T(8,128)(2,1)S(1)}, bf16[1,4,48,384]{3,2,1,0:T(8,128)(2,1)S(1)}, u32[]{:S(2)}, u32[]{:S(2)}) collective-permute-start(bf16[1,4,48,384]{3,2,1,0:T(8,128)(2,1)S(1)} %get-tuple-element.65), channel_id=1, source_target_pairs={{0,128},{64,192},{128,0},{192,64},{1,129},{65,193},{129,1},{193,65... | collective-permute-start | bytes 442376 | tf_op jit(solution)/shard_map/ppermute | solution.py:403
  81.6 8.7 %collective-permute-start.22 = (bf16[1,4,48,384]{3,2,1,0:T(8,128)(2,1)S(1)}, bf16[1,4,48,384]{3,2,1,0:T(8,128)(2,1)S(1)}, u32[]{:S(2)}, u32[]{:S(2)}) collective-permute-start(bf16[1,4,48,384]{3,2,1,0:T(8,128)(2,1)S(1)} %get-tuple-element.66), channel_id=1, source_target_pairs={{0,192},{64,0},{128,64},{192,128},{1,193},{65,1},{129,65},{193,129... | collective-permute-start | bytes 442376 | tf_op jit(solution)/shard_map/ppermute | solution.py:403
  83.1 6.1 %collective-permute-start.17 = (bf16[1,4,32,384]{3,2,1,0:T(8,128)(2,1)S(1)}, bf16[1,4,32,384]{3,2,1,0:T(8,128)(2,1)S(1)}, u32[]{:S(2)}, u32[]{:S(2)}) collective-permute-start(bf16[1,4,32,384]{3,2,1,0:T(8,128)(2,1)S(1)} %get-tuple-element.60), channel_id=1, source_target_pairs={{0,16},{8,24},{16,0},{24,8},{1,17},{9,25},{17,1},{25,9},{2,18},{10... | collective-permute-start | bytes 294920 | tf_op jit(solution)/shard_map/ppermute | solution.py:405
  85.7 4.6 %collective-permute-start.18 = (bf16[1,4,32,384]{3,2,1,0:T(8,128)(2,1)S(1)}, bf16[1,4,32,384]{3,2,1,0:T(8,128)(2,1)S(1)}, u32[]{:S(2)}, u32[]{:S(2)}) collective-permute-start(bf16[1,4,32,384]{3,2,1,0:T(8,128)(2,1)S(1)} %get-tuple-element.61), channel_id=1, source_target_pairs={{0,24},{8,0},{16,8},{24,16},{1,25},{9,1},{17,9},{25,17},{2,26},{10... | collective-permute-start | bytes 294920 | tf_op jit(solution)/shard_map/ppermute | solution.py:405
  110.2 17.3 %all-to-all-start.3 = ((bf16[16,208,128]{2,1,0:T(8,128)(2,1)}), bf16[16,208,128]{2,1,0:T(8,128)(2,1)S(1)}, u32[]{:S(2)}, u32[]{:S(2)}) async-start(bf16[16,208,128]{2,1,0:T(8,128)(2,1)} %get-tuple-element.67), calls=%async_computation.3 | async-start | bytes 1703936 | tf_op jit(solution)/shard_map/all_to_all | solution.py:413
  (9 other events, 27.2 us)

commit v7 on v5

--- a/solution.py
+++ b/solution.py
@@ -210,24 +210,37 @@
         weights.append(jnp.where(same, part, 0.0).astype(bf16))
     weights = jnp.concatenate(weights, axis=1)
     nought = jnp.zeros((TILE, orbitals), bf16)
-    for out_ref in outs:
-        out_ref[:, :, 256:WIDE] = jnp.zeros((4, rows, WIDE - 256), bf16)
     for t in range(rows // TILE):
         here = slice(t * TILE, (t + 1) * TILE)
         column = []
         for block_ref in blocks:
             column += [block_ref[:, here, :].reshape(vectors * TILE, orbitals), nought]
         total = jnp.dot(weights, jnp.concatenate(column), preferred_element_type=f32)
-        total = (step_root * total).astype(bf16).reshape(TILE, TILE, orbitals)
-        for w in range(TILE):
-            outs[w // 4][w % 4, here, 0:orbitals] = total[w]
+        total = step_root * total
+        last = total[:, 256:orbitals]
+        if t % 2 == 0:
+            packed = jnp.concatenate([last, jnp.zeros_like(last)], axis=1)
+        else:
+            packed = packed + jnp.concatenate([jnp.zeros_like(last), last], axis=1)
+        for first, part in (
+            (t * TILE, total[:, 0:128]),
+            (rows + t * TILE, total[:, 128:256]),
+            (2 * rows + t // 2 * TILE, packed),
+        ):
+            part = part.astype(bf16).reshape(TILE, TILE, 128)
+            for w in range(TILE):
+                outs[w // 4][w % 4, first : first + TILE, :] = part[w]
+
+
+def packed_rows(rows):
+    return 2 * rows + (rows // TILE + 1) // 2 * TILE
 
 
 def field_rows(place, message, blocks, pieces):
     vectors, rows, _ = blocks[0].shape[-3:]
     return pl.pallas_call(
         functools.partial(field_kernel, vectors),
-        out_shape=[jax.ShapeDtypeStruct((4 // pieces, 4, rows, WIDE), bf16)] * pieces,
+        out_shape=[jax.ShapeDtypeStruct((4 // pieces, 4, packed_rows(rows), 128), bf16)] * pieces,
         in_specs=[pl.BlockSpec(memory_space=pltpu.SMEM)]
         + [pl.BlockSpec(memory_space=pltpu.VMEM)] * (1 + len(blocks)),
         compiler_params=pltpu.CompilerParams(vmem_limit_bytes=20 * 2**20),
@@ -239,7 +252,6 @@
 
 
 def sum_kernel(copies, message_ref, *refs):
-    upper = lax.broadcasted_iota(jnp.int32, (TILE, 128), 1) >= 64
     scalars = message_ref[0, 0:TILE].astype(f32)
     for s in range(1, message_ref.shape[0]):
         scalars = scalars + message_ref[s, 0:TILE].astype(f32)
@@ -248,25 +260,24 @@
     pieces = [ref.at[i] for ref in refs[:-1] for i in range(ref.shape[0])]
     firsts, seconds = pieces[:4], pieces[4:]
     groups, rows = firsts[0].shape[:2]
+    upper = lax.broadcasted_iota(jnp.int32, (TILE, 128), 1) >= 64
     for g in range(groups):
         total = firsts[0][g].astype(f32)
         below = seconds[0][g].astype(f32)
         for s in range(1, 4):
             total = total + firsts[s][g].astype(f32)
             below = below + seconds[s][g].astype(f32)
-        corner = jnp.where(upper, scalars, total[0:TILE, 256:WIDE]).astype(bf16)
-        total, below = total.astype(bf16), below.astype(bf16)
+        end = jnp.where(upper, scalars, below[below.shape[0] - TILE :])
+        packed = jnp.concatenate([total, below[: below.shape[0] - TILE], end]).astype(bf16)
         for k in range(g, copies, groups):
-            out_ref[k, 0:rows] = total
-            out_ref[k, rows:] = below
-            out_ref[k, 0:TILE, 256:WIDE] = corner
+            out_ref[k] = packed
 
 
 def sum_second_axis(message, first, second):
-    rows, wide = first[0].shape[2] + second[0].shape[2], first[0].shape[3]
+    rows = first[0].shape[2] + second[0].shape[2]
     return pl.pallas_call(
         functools.partial(sum_kernel, 8),
-        out_shape=jax.ShapeDtypeStruct((8, rows, wide), bf16),
+        out_shape=jax.ShapeDtypeStruct((8, rows, 128), bf16),
         compiler_params=pltpu.CompilerParams(vmem_limit_bytes=16 * 2**20),
         name="sum_plane",
     )(message, *first, *second)
@@ -277,7 +288,7 @@
     for s in range(1, in_ref.shape[0]):
         total = total + in_ref[s].astype(f32)
     rounded = total.astype(bf16)
-    scalars_ref[...] = jnp.sum(total[0:TILE, 256:WIDE], axis=0, keepdims=True)
+    scalars_ref[...] = jnp.sum(total[total.shape[0] - TILE :], axis=0, keepdims=True)
     for k in range(out_ref.shape[0]):
         out_ref[k] = rounded
 
@@ -295,12 +306,24 @@
     )(received)
 
 
-def taylor_kernel(first_rows, in_ref, walkers_ref, out_ref):
+def taylor_kernel(rows, in_ref, walkers_ref, out_ref):
     orbitals = walkers_ref.shape[1]
+    rest = orbitals // 4 - rows
+
+    def part(k, start, count):
+        last = []
+        for t in range(count // TILE):
+            here = start + 2 * count + t // 2 * TILE
+            tile = in_ref[k, here : here + TILE]
+            last.append(pltpu.roll(tile.astype(f32), 64, 1).astype(bf16) if t % 2 else tile)
+        left, right = in_ref[k, start : start + count], in_ref[k, start + count : start + 2 * count]
+        return jnp.concatenate([left, right, jnp.concatenate(last)], axis=1)
+
+    start = packed_rows(rows)
     fields = [
         jnp.concatenate(
-            [in_ref[4 * k + w, 0:first_rows] for k in range(4)]
-            + [in_ref[4 * w + k, first_rows:] for k in range(4)]
+            [part(4 * k + w, 0, rows) for k in range(4)]
+            + [part(4 * w + k, start, rest) for k in range(4)]
         )[:, 0:orbitals]
         for w in range(4)
     ]

time: 133 us -> 129 us (0.970)
  waiting for transfers between devices: 27.2 us -> 25.1 us
  blocking collectives: 20.1 us -> 18.5 us
    all_to_all x1, waiting for transfers between devices: 10.8 us -> 8.77 us  [on_device(): field = lax.all_to_all(field, ('x', 'y'), 0, 0)]
    all_to_all x1, blocking collectives: 20.1 us -> 18.5 us  [on_device(): field = lax.all_to_all(field, Z, 0, 0)]
  transfers between devices with their start and end apart: 27 -> 27, of which waited for: 12 -> 12; matrix products, arithmetic and copies ran while one was open for 4% -> 4% of each run, Pallas kernels for 19% -> 20%
where the time goes in v7:
time: 129 us
  starting transfers between devices  46.3 us (36%)
  Pallas kernels  27.6 us (21%)
  waiting for transfers between devices  25.1 us (19%)
  blocking collectives  18.5 us (14%)
  local copies, waits for them, and re-layouts  9.64 us (7%)
    all_to_all x1, blocking collectives, on_device(): field = lax.all_to_all(field, Z, 0, 0)  18.5 us
    pallas_call x2, Pallas kernels, pair_sums(): pl.pallas_call(functools.partial(pair_kernel, vectors, first, 1 + len(gre...  15.6 us
    all_to_all x1, waiting for transfers between devices, on_device(): field = lax.all_to_all(field, ('x', 'y'), 0, 0)  8.77 us
    all_to_all x1, starting transfers between devices, on_device(): message = lax.all_to_all(message, ('x', 'y'), 0, 0)  6.51 us
    pallas_call x2, Pallas kernels, field_rows(): pl.pallas_call(functools.partial(field_kernel, vectors), out_shape=[jax.S...  6.39 us
    all_to_all x1, starting transfers between devices, on_device(): field = lax.all_to_all(field, ('x', 'y'), 0, 0)  6.37 us
    all_to_all x1, waiting for transfers between devices, on_device(): message = lax.all_to_all(message, ('x', 'y'), 0, 0)  6.32 us
    ppermute x3, starting transfers between devices, on_device(): lax.ppermute(after(first_pieces[k], beside), 'x', ring(4, k))  5.66 us
  transfers between devices with their start and end apart: 27, of which 12 were waited for; matrix products, arithmetic and copies ran while one was open for 4% of the time, Pallas kernels for 20%

profile of v7, /device:TPU:8, one launch (start us, length us, event | category | flops | bytes accessed | tf_op | source)
XLA Modules:
  0.0 128.6 jit_solution(9522424211950920103)
XLA Ops:
  0.7 2.0 %collective-permute-start.1 = (bf16[4,320,120]{2,1,0:T(8,128)(2,1)}, bf16[4,320,120]{2,1,0:T(8,128)(2,1)}, u32[]{:S(2)}, u32[]{:S(2)}) collective-permute-start(bf16[4,320,120]{2,1,0:T(8,128)(2,1)} %bitcast.36), channel_id=1, source_target_pairs={{0,2},{2,4},{4,6},{6,32},{32,34},{34,36},{36,38},{38,0},{1,3},{3,5... | collective-permute-start | bytes 921608 | tf_op jit(solution)/shard_map/ppermute | solution.py:363
  2.7 3.3 %collective-permute-start.2 = (bf16[4,320,120]{2,1,0:T(8,128)(2,1)}, bf16[4,320,120]{2,1,0:T(8,128)(2,1)}, u32[]{:S(2)}, u32[]{:S(2)}) collective-permute-start(bf16[4,320,120]{2,1,0:T(8,128)(2,1)} %bitcast.37), channel_id=1, source_target_pairs={{0,4},{1,37},{2,6},{3,39},{4,32},{5,1},{6,34},{7,3},{32,36},{33,5}... | collective-permute-start | bytes 921608 | tf_op jit(solution)/shard_map/ppermute | solution.py:366
  7.3 1.6 %slice-done = bf16[15,192,320]{2,1,0:T(8,128)(2,1)S(1)} async-done(((bf16[15,320,320]{2,1,0:T(8,128)(2,1)}), bf16[15,192,320]{2,1,0:T(8,128)(2,1)S(1)}, s32[]{:S(2)}) %slice-start) | async-done | bytes 1843224 | tf_op jit(solution)/shard_map/slice | solution.py:374
  8.9 1.6 %copy.15 = bf16[15,4,48,320]{3,2,0,1:T(8,128)(2,1)} copy(bf16[15,4,48,320]{3,2,1,0:T(8,128)(2,1)S(1)} %bitcast.33) | data formatting | bytes 3686400 | tf_op jit(solution)/shard_map/reshape | solution.py:374
  10.5 2.4 %constant_dynamic-slice_fusion.1 = (bf16[15,32,320]{2,1,0:T(8,128)(2,1)}, bf16[15,32,320]{2,1,0:T(8,128)(2,1)}, bf16[15,32,320]{2,1,0:T(8,128)(2,1)}, bf16[15,32,320]{2,1,0:T(8,128)(2,1)S(1)}) fusion(bf16[15,320,320]{2,1,0:T(8,128)(2,1)} %param.9, s32[]{:T(128)S(6)} %select_n.18, s32[]{:T(128)S(6)} %select_n.17, s32[]{:T(128)S(6)} %select_n.16, s32[]{:T(128)S(6)} %select_n.15), kind=kLoop, calls=%fused_computation.2 | loop fusion | bytes 2457616 | tf_op jit(solution)/shard_map/dynamic_slice | solution.py:371
  13.7 5.8 %pairs.2 = (f32[8,15,128]{2,1,0:T(8,128)}, f32[8,8,128]{2,1,0:T(8,128)}, bf16[15,128,320]{2,1,0:T(8,128)(2,1)}) custom-call(bf16[15,320,120]{2,1,0:T(8,128)(2,1)} %bitcast.43, bf16[4,320,120]{2,1,0:T(8,128)(2,1)} %bitcast.39, bf16[4,320,120]{2,1,0:T(8,128)(2,1)} %copy-done.3), custom_call_target="tpu_custom_call" | custom-call | flops 1 | bytes 1 | tf_op jit(solution)/shard_map/pairs/pallas_call | solution.py:97
  20.5 5.0 %all-to-all-start = ((bf16[4,15,48,320]{3,2,1,0:T(8,128)(2,1)}), bf16[4,15,48,320]{3,2,1,0:T(8,128)(2,1)S(1)}, u32[]{:S(2)}, u32[]{:S(2)}) async-start(bf16[4,15,48,320]{3,2,1,0:T(8,128)(2,1)} %bitcast.32), calls=%async_computation | async-start | bytes 4423680 | tf_op jit(solution)/shard_map/all_to_all | solution.py:383
  25.6 1.8 %collective-permute-start.4 = (bf16[4,320,120]{2,1,0:T(8,128)(2,1)}, bf16[4,320,120]{2,1,0:T(8,128)(2,1)}, u32[]{:S(2)}, u32[]{:S(2)}) collective-permute-start(bf16[4,320,120]{2,1,0:T(8,128)(2,1)} %collective-permute-done.1.refs_1_), channel_id=1, source_target_pairs={{0,1},{1,0},{2,3},{3,2},{4,5},{5,4},{6,7},{7,6},{8,9},{9,8},{10,11... | collective-permute-start | bytes 921608 | tf_op jit(solution)/shard_map/ppermute | solution.py:360
  27.8 1.5 %collective-permute-start.8 = (bf16[15,32,320]{2,1,0:T(8,128)(2,1)}, bf16[15,32,320]{2,1,0:T(8,128)(2,1)S(1)}, u32[]{:S(2)}, u32[]{:S(2)}) collective-permute-start(bf16[15,32,320]{2,1,0:T(8,128)(2,1)} %get-tuple-element.46), channel_id=1, source_target_pairs={{0,64},{64,128},{128,192},{192,0},{1,65},{65,129},{129,193},{193,1... | collective-permute-start | bytes 921608 | tf_op jit(solution)/shard_map/ppermute | solution.py:381
  29.3 2.7 %collective-permute-start.9 = (bf16[15,32,320]{2,1,0:T(8,128)(2,1)}, bf16[15,32,320]{2,1,0:T(8,128)(2,1)S(1)}, u32[]{:S(2)}, u32[]{:S(2)}) collective-permute-start(bf16[15,32,320]{2,1,0:T(8,128)(2,1)} %get-tuple-element.47), channel_id=1, source_target_pairs={{0,128},{64,192},{128,0},{192,64},{1,129},{65,193},{129,1},{193,65... | collective-permute-start | bytes 921608 | tf_op jit(solution)/shard_map/ppermute | solution.py:381
  33.5 4.5 %collective-permute-start.7 = (bf16[48,128]{1,0:T(8,128)(2,1)S(1)}, bf16[48,128]{1,0:T(8,128)(2,1)S(1)}, u32[]{:S(2)}, u32[]{:S(2)}) collective-permute-start(bf16[48,128]{1,0:T(8,128)(2,1)S(1)} %pad.4.near_ref), channel_id=1, source_target_pairs={{0,32},{32,0},{1,33},{33,1},{2,34},{34,2},{3,35},{35,3},{4,36},{36... | collective-permute-start | bytes 36872 | tf_op jit(solution)/shard_map/ppermute | solution.py:393
  38.6 9.8 %pairs.3 = (f32[24,15,128]{2,1,0:T(8,128)}, f32[24,8,128]{2,1,0:T(8,128)}) custom-call(bf16[15,128,320]{2,1,0:T(8,128)(2,1)} %get-tuple-element.38.refs_0_, bf16[4,320,120]{2,1,0:T(8,128)(2,1)} %collective-permute-done.1.refs_1_, bf16[4,320,120]{2,1,0:T(8,128)(2,1)} %collective-permute-done.4.refs_2_, bf16[4,320,120]{2,1,0:T(8,128)(2,1)} %collective-permute-done.2.refs_3_, ...), custom_call_target="tpu_custom_call" | custom-call | flops 1 | bytes 1 | tf_op jit(solution)/shard_map/pairs/pallas_call | solution.py:97
  48.6 2.3 %message.1 = (bf16[16,128]{1,0:T(8,128)(2,1)}, bf16[16,128]{1,0:T(8,128)(2,1)}) custom-call(s32[2]{0:T(128)} %pad_add_fusion.place_ref, f32[8,15,128]{2,1,0:T(8,128)} %get-tuple-element.37.refs_0_, f32[24,15,128]{2,1,0:T(8,128)} %get-tuple-element.42.refs_1_, f32[8,8,128]{2,1,0:T(8,128)} %get-tuple-element.43.refs_2_, ...), custom_call_target="tpu_custom_call" | custom-call | tf_op jit(solution)/shard_map/message/pallas_call | solution.py:153
  54.5 6.5 %all-to-all-start.1 = ((bf16[16,112,128]{2,1,0:T(8,128)(2,1)}), bf16[16,112,128]{2,1,0:T(8,128)(2,1)S(1)}, u32[]{:S(2)}, u32[]{:S(2)}) async-start(bf16[16,112,128]{2,1,0:T(8,128)(2,1)} %copies.1), calls=%async_computation.1 | async-start | bytes 917504 | tf_op jit(solution)/shard_map/all_to_all | solution.py:400
  64.6 6.3 %all-to-all-done.1.message_ref = bf16[16,112,128]{2,1,0:T(8,128)(2,1)S(1)} async-done(((bf16[16,112,128]{2,1,0:T(8,128)(2,1)}), bf16[16,112,128]{2,1,0:T(8,128)(2,1)S(1)}, u32[]{:S(2)}, u32[]{:S(2)}) %all-to-all-start.1) | async-done | bytes 458784 | tf_op jit(solution)/shard_map/all_to_all | solution.py:400
  71.9 2.9 %field_rows.2 = (bf16[1,4,80,128]{3,2,1,0:T(8,128)(2,1)S(1)}, bf16[1,4,80,128]{3,2,1,0:T(8,128)(2,1)S(1)}, bf16[1,4,80,128]{3,2,1,0:T(8,128)(2,1)S(1)}, bf16[1,4,80,128]{3,2,1,0:T(8,128)(2,1)S(1)}) custom-call(s32[5]{0:T(128)S(1)} %stack.57.place_ref, bf16[16,112,128]{2,1,0:T(8,128)(2,1)S(1)} %all-to-all-done.1.message_ref, ...), custom_call_target="tpu_custom_call" | custom-call | flops 805306368 | bytes 1280000 | tf_op jit(solution)/shard_map/field_rows/pallas_call | solution.py:241
  75.4 3.5 %field_rows.3 = (bf16[1,4,128,128]{3,2,1,0:T(8,128)(2,1)S(1)}, bf16[1,4,128,128]{3,2,1,0:T(8,128)(2,1)S(1)}, bf16[1,4,128,128]{3,2,1,0:T(8,128)(2,1)S(1)}, bf16[1,4,128,128]{3,2,1,0:T(8,128)(2,1)S(1)}) custom-call(s32[5]{0:T(128)S(1)} %stack.63.place_ref, bf16[16,112,128]{2,1,0:T(8,128)(2,1)S(1)} %all-to-all-done.1.message_ref, ...), custom_call_target="tpu_custom_call" | custom-call | flops 1207959552 | bytes 1920000 | tf_op jit(solution)/shard_map/field_rows/pallas_call | solution.py:241
  79.3 2.3 %collective-permute-start.21 = (bf16[1,4,128,128]{3,2,1,0:T(8,128)(2,1)S(1)}, bf16[1,4,128,128]{3,2,1,0:T(8,128)(2,1)S(1)}, u32[]{:S(2)}, u32[]{:S(2)}) collective-permute-start(bf16[1,4,128,128]{3,2,1,0:T(8,128)(2,1)S(1)} %get-tuple-element.65), channel_id=1, source_target_pairs={{0,128},{64,192},{128,0},{192,64},{1,129},{65,193},{129,1},{193,65... | collective-permute-start | bytes 393224 | tf_op jit(solution)/shard_map/ppermute | solution.py:411
  81.7 1.5 %collective-permute-start.22 = (bf16[1,4,128,128]{3,2,1,0:T(8,128)(2,1)S(1)}, bf16[1,4,128,128]{3,2,1,0:T(8,128)(2,1)S(1)}, u32[]{:S(2)}, u32[]{:S(2)}) collective-permute-start(bf16[1,4,128,128]{3,2,1,0:T(8,128)(2,1)S(1)} %get-tuple-element.66), channel_id=1, source_target_pairs={{0,192},{64,0},{128,64},{192,128},{1,193},{65,1},{129,65},{193,129... | collective-permute-start | bytes 393224 | tf_op jit(solution)/shard_map/ppermute | solution.py:411
  83.2 2.6 %collective-permute-start.17 = (bf16[1,4,80,128]{3,2,1,0:T(8,128)(2,1)S(1)}, bf16[1,4,80,128]{3,2,1,0:T(8,128)(2,1)S(1)}, u32[]{:S(2)}, u32[]{:S(2)}) collective-permute-start(bf16[1,4,80,128]{3,2,1,0:T(8,128)(2,1)S(1)} %get-tuple-element.60), channel_id=1, source_target_pairs={{0,16},{8,24},{16,0},{24,8},{1,17},{9,25},{17,1},{25,9},{2,18},{10... | collective-permute-start | bytes 245768 | tf_op jit(solution)/shard_map/ppermute | solution.py:413
  86.1 3.0 %collective-permute-done.17.refs_2_ = bf16[1,4,80,128]{3,2,1,0:T(8,128)(2,1)S(1)} collective-permute-done((bf16[1,4,80,128]{3,2,1,0:T(8,128)(2,1)S(1)}, bf16[1,4,80,128]{3,2,1,0:T(8,128)(2,1)S(1)}, u32[]{:S(2)}, u32[]{:S(2)}) %collective-permute-start.17) | collective-permute-done | bytes 81952 | tf_op jit(solution)/shard_map/ppermute | solution.py:413
  90.3 18.5 %all_to_all.20.in_ref = bf16[8,208,128]{2,1,0:T(8,128)(2,1)S(1)} all-to-all(bf16[8,208,128]{2,1,0:T(8,128)(2,1)S(1)} %sum_plane.1), channel_id=1, replica_groups=mesh['x'=4,'zh'=2,'y'=4,'zl'=4,'core'=2] {'zh','zl'}, dimensions={0} | all-to-all | bytes 851968 | tf_op jit(solution)/shard_map/all_to_all | solution.py:415
  109.8 6.4 %all-to-all-start.3 = ((bf16[16,208,128]{2,1,0:T(8,128)(2,1)}), bf16[16,208,128]{2,1,0:T(8,128)(2,1)S(1)}, u32[]{:S(2)}, u32[]{:S(2)}) async-start(bf16[16,208,128]{2,1,0:T(8,128)(2,1)} %get-tuple-element.67), calls=%async_computation.3 | async-start | bytes 1703936 | tf_op jit(solution)/shard_map/all_to_all | solution.py:421
  117.9 8.8 %all-to-all-done.3.in_ref = bf16[16,208,128]{2,1,0:T(8,128)(2,1)S(1)} async-done(((bf16[16,208,128]{2,1,0:T(8,128)(2,1)}), bf16[16,208,128]{2,1,0:T(8,128)(2,1)S(1)}, u32[]{:S(2)}, u32[]{:S(2)}) %all-to-all-start.3) | async-done | bytes 852000 | tf_op jit(solution)/shard_map/all_to_all | solution.py:421
  (66 shorter events, 21.2 us)
Async XLA Ops:
  0.6 12.3 %collective-permute-start = (bf16[4,320,120]{2,1,0:T(8,128)(2,1)}, bf16[4,320,120]{2,1,0:T(8,128)(2,1)S(1)}, u32[]{:S(2)}, u32[]{:S(2)}) collective-permute-start(bf16[4,320,120]{2,1,0:T(8,128)(2,1)} %bitcast.35), channel_id=1, source_target_pairs={{0,1},{1,0},{2,3},{3,2},{4,5},{5,4},{6,7},{7,6},{8,9},{9,8},{10,11... | collective-permute-start | bytes 921608 | tf_op jit(solution)/shard_map/ppermute | solution.py:360
  0.7 18.8 %collective-permute-start.1 = (bf16[4,320,120]{2,1,0:T(8,128)(2,1)}, bf16[4,320,120]{2,1,0:T(8,128)(2,1)}, u32[]{:S(2)}, u32[]{:S(2)}) collective-permute-start(bf16[4,320,120]{2,1,0:T(8,128)(2,1)} %bitcast.36), channel_id=1, source_target_pairs={{0,2},{2,4},{4,6},{6,32},{32,34},{34,36},{36,38},{38,0},{1,3},{3,5... | collective-permute-start | bytes 921608 | tf_op jit(solution)/shard_map/ppermute | solution.py:363
  2.7 17.8 %collective-permute-start.2 = (bf16[4,320,120]{2,1,0:T(8,128)(2,1)}, bf16[4,320,120]{2,1,0:T(8,128)(2,1)}, u32[]{:S(2)}, u32[]{:S(2)}) collective-permute-start(bf16[4,320,120]{2,1,0:T(8,128)(2,1)} %bitcast.37), channel_id=1, source_target_pairs={{0,4},{1,37},{2,6},{3,39},{4,32},{5,1},{6,34},{7,3},{32,36},{33,5}... | collective-permute-start | bytes 921608 | tf_op jit(solution)/shard_map/ppermute | solution.py:366
  6.0 14.5 %collective-permute-start.3 = (bf16[4,320,120]{2,1,0:T(8,128)(2,1)}, bf16[4,320,120]{2,1,0:T(8,128)(2,1)}, u32[]{:S(2)}, u32[]{:S(2)}) collective-permute-start(bf16[4,320,120]{2,1,0:T(8,128)(2,1)} %bitcast.38), channel_id=1, source_target_pairs={{0,38},{2,0},{4,2},{6,4},{32,6},{34,32},{36,34},{38,36},{1,39},{3,... | collective-permute-start | bytes 921608 | tf_op jit(solution)/shard_map/ppermute | solution.py:364
  20.5 31.8 %all-to-all-start = ((bf16[4,15,48,320]{3,2,1,0:T(8,128)(2,1)}), bf16[4,15,48,320]{3,2,1,0:T(8,128)(2,1)S(1)}, u32[]{:S(2)}, u32[]{:S(2)}) async-start(bf16[4,15,48,320]{3,2,1,0:T(8,128)(2,1)} %bitcast.32), calls=%async_computation | async-start | bytes 4423680 | tf_op jit(solution)/shard_map/all_to_all | solution.py:383
  25.6 6.5 %collective-permute-start.4 = (bf16[4,320,120]{2,1,0:T(8,128)(2,1)}, bf16[4,320,120]{2,1,0:T(8,128)(2,1)}, u32[]{:S(2)}, u32[]{:S(2)}) collective-permute-start(bf16[4,320,120]{2,1,0:T(8,128)(2,1)} %collective-permute-done.1.refs_1_), channel_id=1, source_target_pairs={{0,1},{1,0},{2,3},{3,2},{4,5},{5,4},{6,7},{7,6},{8,9},{9,8},{10,11... | collective-permute-start | bytes 921608 | tf_op jit(solution)/shard_map/ppermute | solution.py:360
  27.3 6.2 %collective-permute-start.5 = (bf16[4,320,120]{2,1,0:T(8,128)(2,1)}, bf16[4,320,120]{2,1,0:T(8,128)(2,1)}, u32[]{:S(2)}, u32[]{:S(2)}) collective-permute-start(bf16[4,320,120]{2,1,0:T(8,128)(2,1)} %collective-permute-done.2.refs_3_), channel_id=1, source_target_pairs={{0,1},{1,0},{2,3},{3,2},{4,5},{5,4},{6,7},{7,6},{8,9},{9,8},{10,11... | collective-permute-start | bytes 921608 | tf_op jit(solution)/shard_map/ppermute | solution.py:360
  27.3 11.3 %collective-permute-start.6 = (bf16[4,320,120]{2,1,0:T(8,128)(2,1)}, bf16[4,320,120]{2,1,0:T(8,128)(2,1)}, u32[]{:S(2)}, u32[]{:S(2)}) collective-permute-start(bf16[4,320,120]{2,1,0:T(8,128)(2,1)} %collective-permute-done.3.refs_5_), channel_id=1, source_target_pairs={{0,1},{1,0},{2,3},{3,2},{4,5},{5,4},{6,7},{7,6},{8,9},{9,8},{10,11... | collective-permute-start | bytes 921608 | tf_op jit(solution)/shard_map/ppermute | solution.py:360
  27.8 20.6 %collective-permute-start.8 = (bf16[15,32,320]{2,1,0:T(8,128)(2,1)}, bf16[15,32,320]{2,1,0:T(8,128)(2,1)S(1)}, u32[]{:S(2)}, u32[]{:S(2)}) collective-permute-start(bf16[15,32,320]{2,1,0:T(8,128)(2,1)} %get-tuple-element.46), channel_id=1, source_target_pairs={{0,64},{64,128},{128,192},{192,0},{1,65},{65,129},{129,193},{193,1... | collective-permute-start | bytes 921608 | tf_op jit(solution)/shard_map/ppermute | solution.py:381
  29.3 19.3 %collective-permute-start.9 = (bf16[15,32,320]{2,1,0:T(8,128)(2,1)}, bf16[15,32,320]{2,1,0:T(8,128)(2,1)S(1)}, u32[]{:S(2)}, u32[]{:S(2)}) collective-permute-start(bf16[15,32,320]{2,1,0:T(8,128)(2,1)} %get-tuple-element.47), channel_id=1, source_target_pairs={{0,128},{64,192},{128,0},{192,64},{1,129},{65,193},{129,1},{193,65... | collective-permute-start | bytes 921608 | tf_op jit(solution)/shard_map/ppermute | solution.py:381
  32.1 16.6 %collective-permute-start.10 = (bf16[15,32,320]{2,1,0:T(8,128)(2,1)}, bf16[15,32,320]{2,1,0:T(8,128)(2,1)}, u32[]{:S(2)}, u32[]{:S(2)}) collective-permute-start(bf16[15,32,320]{2,1,0:T(8,128)(2,1)} %get-tuple-element.48), channel_id=1, source_target_pairs={{0,192},{64,0},{128,64},{192,128},{1,193},{65,1},{129,65},{193,129... | collective-permute-start | bytes 921608 | tf_op jit(solution)/shard_map/ppermute | solution.py:381
  33.5 14.9 %collective-permute-start.7 = (bf16[48,128]{1,0:T(8,128)(2,1)S(1)}, bf16[48,128]{1,0:T(8,128)(2,1)S(1)}, u32[]{:S(2)}, u32[]{:S(2)}) collective-permute-start(bf16[48,128]{1,0:T(8,128)(2,1)S(1)} %pad.4.near_ref), channel_id=1, source_target_pairs={{0,32},{32,0},{1,33},{33,1},{2,34},{34,2},{3,35},{35,3},{4,36},{36... | collective-permute-start | bytes 36872 | tf_op jit(solution)/shard_map/ppermute | solution.py:393
  52.4 23.1 %collective-permute-start.19 = (bf16[4,15,48,320]{3,2,1,0:T(8,128)(2,1)S(1)}, bf16[4,15,48,320]{3,2,1,0:T(8,128)(2,1)}, u32[]{:S(2)}, u32[]{:S(2)}) collective-permute-start(bf16[4,15,48,320]{3,2,1,0:T(8,128)(2,1)S(1)} %all-to-all-done.refs_0_), channel_id=1, source_target_pairs={{0,1},{1,0},{2,3},{3,2},{4,5},{5,4},{6,7},{7,6},{8,9},{9,8},{10,11... | collective-permute-start | bytes 5529608 | tf_op jit(solution)/shard_map/ppermute | solution.py:360
  54.5 16.4 %all-to-all-start.1 = ((bf16[16,112,128]{2,1,0:T(8,128)(2,1)}), bf16[16,112,128]{2,1,0:T(8,128)(2,1)S(1)}, u32[]{:S(2)}, u32[]{:S(2)}) async-start(bf16[16,112,128]{2,1,0:T(8,128)(2,1)} %copies.1), calls=%async_computation.1 | async-start | bytes 917504 | tf_op jit(solution)/shard_map/all_to_all | solution.py:400
  61.0 2.9 %collective-permute-start.13 = (bf16[15,32,320]{2,1,0:T(8,128)(2,1)S(1)}, bf16[15,32,320]{2,1,0:T(8,128)(2,1)}, u32[]{:S(2)}, u32[]{:S(2)}) collective-permute-start(bf16[15,32,320]{2,1,0:T(8,128)(2,1)S(1)} %collective-permute-done.8.refs_1_), channel_id=1, source_target_pairs={{0,1},{1,0},{2,3},{3,2},{4,5},{5,4},{6,7},{7,6},{8,9},{9,8},{10,11... | collective-permute-start | bytes 921608 | tf_op jit(solution)/shard_map/ppermute | solution.py:360
  61.5 2.6 %collective-permute-start.14 = (bf16[15,32,320]{2,1,0:T(8,128)(2,1)}, bf16[15,32,320]{2,1,0:T(8,128)(2,1)}, u32[]{:S(2)}, u32[]{:S(2)}) collective-permute-start(bf16[15,32,320]{2,1,0:T(8,128)(2,1)} %copy-done), channel_id=1, source_target_pairs={{0,1},{1,0},{2,3},{3,2},{4,5},{5,4},{6,7},{7,6},{8,9},{9,8},{10,11... | collective-permute-start | bytes 921608 | tf_op jit(solution)/shard_map/ppermute | solution.py:360
  61.6 3.0 %collective-permute-start.15 = (bf16[15,32,320]{2,1,0:T(8,128)(2,1)}, bf16[15,32,320]{2,1,0:T(8,128)(2,1)}, u32[]{:S(2)}, u32[]{:S(2)}) collective-permute-start(bf16[15,32,320]{2,1,0:T(8,128)(2,1)} %collective-permute-done.10.refs_3_), channel_id=1, source_target_pairs={{0,1},{1,0},{2,3},{3,2},{4,5},{5,4},{6,7},{7,6},{8,9},{9,8},{10,11... | collective-permute-start | bytes 921608 | tf_op jit(solution)/shard_map/ppermute | solution.py:360
  74.8 10.9 %collective-permute-start.16 = (bf16[1,4,80,128]{3,2,1,0:T(8,128)(2,1)S(1)}, bf16[1,4,80,128]{3,2,1,0:T(8,128)(2,1)S(1)}, u32[]{:S(2)}, u32[]{:S(2)}) collective-permute-start(bf16[1,4,80,128]{3,2,1,0:T(8,128)(2,1)S(1)} %get-tuple-element.59), channel_id=1, source_target_pairs={{0,8},{8,16},{16,24},{24,0},{1,9},{9,17},{17,25},{25,1},{2,10},{10... | collective-permute-start | bytes 245768 | tf_op jit(solution)/shard_map/ppermute | solution.py:413
  79.0 11.2 %collective-permute-start.20 = (bf16[1,4,128,128]{3,2,1,0:T(8,128)(2,1)S(1)}, bf16[1,4,128,128]{3,2,1,0:T(8,128)(2,1)S(1)}, u32[]{:S(2)}, u32[]{:S(2)}) collective-permute-start(bf16[1,4,128,128]{3,2,1,0:T(8,128)(2,1)S(1)} %get-tuple-element.64), channel_id=1, source_target_pairs={{0,64},{64,128},{128,192},{192,0},{1,65},{65,129},{129,193},{193,1... | collective-permute-start | bytes 393224 | tf_op jit(solution)/shard_map/ppermute | solution.py:411
  79.3 10.9 %collective-permute-start.21 = (bf16[1,4,128,128]{3,2,1,0:T(8,128)(2,1)S(1)}, bf16[1,4,128,128]{3,2,1,0:T(8,128)(2,1)S(1)}, u32[]{:S(2)}, u32[]{:S(2)}) collective-permute-start(bf16[1,4,128,128]{3,2,1,0:T(8,128)(2,1)S(1)} %get-tuple-element.65), channel_id=1, source_target_pairs={{0,128},{64,192},{128,0},{192,64},{1,129},{65,193},{129,1},{193,65... | collective-permute-start | bytes 393224 | tf_op jit(solution)/shard_map/ppermute | solution.py:411
  81.7 8.5 %collective-permute-start.22 = (bf16[1,4,128,128]{3,2,1,0:T(8,128)(2,1)S(1)}, bf16[1,4,128,128]{3,2,1,0:T(8,128)(2,1)S(1)}, u32[]{:S(2)}, u32[]{:S(2)}) collective-permute-start(bf16[1,4,128,128]{3,2,1,0:T(8,128)(2,1)S(1)} %get-tuple-element.66), channel_id=1, source_target_pairs={{0,192},{64,0},{128,64},{192,128},{1,193},{65,1},{129,65},{193,129... | collective-permute-start | bytes 393224 | tf_op jit(solution)/shard_map/ppermute | solution.py:411
  83.2 5.9 %collective-permute-start.17 = (bf16[1,4,80,128]{3,2,1,0:T(8,128)(2,1)S(1)}, bf16[1,4,80,128]{3,2,1,0:T(8,128)(2,1)S(1)}, u32[]{:S(2)}, u32[]{:S(2)}) collective-permute-start(bf16[1,4,80,128]{3,2,1,0:T(8,128)(2,1)S(1)} %get-tuple-element.60), channel_id=1, source_target_pairs={{0,16},{8,24},{16,0},{24,8},{1,17},{9,25},{17,1},{25,9},{2,18},{10... | collective-permute-start | bytes 245768 | tf_op jit(solution)/shard_map/ppermute | solution.py:413
  85.7 4.4 %collective-permute-start.18 = (bf16[1,4,80,128]{3,2,1,0:T(8,128)(2,1)S(1)}, bf16[1,4,80,128]{3,2,1,0:T(8,128)(2,1)S(1)}, u32[]{:S(2)}, u32[]{:S(2)}) collective-permute-start(bf16[1,4,80,128]{3,2,1,0:T(8,128)(2,1)S(1)} %get-tuple-element.61), channel_id=1, source_target_pairs={{0,24},{8,0},{16,8},{24,16},{1,25},{9,1},{17,9},{25,17},{2,26},{10... | collective-permute-start | bytes 245768 | tf_op jit(solution)/shard_map/ppermute | solution.py:413
  109.8 16.9 %all-to-all-start.3 = ((bf16[16,208,128]{2,1,0:T(8,128)(2,1)}), bf16[16,208,128]{2,1,0:T(8,128)(2,1)S(1)}, u32[]{:S(2)}, u32[]{:S(2)}) async-start(bf16[16,208,128]{2,1,0:T(8,128)(2,1)} %get-tuple-element.67), calls=%async_computation.3 | async-start | bytes 1703936 | tf_op jit(solution)/shard_map/all_to_all | solution.py:421
  (9 other events, 27.2 us)

commit v8 on v7

--- a/solution.py
+++ b/solution.py
@@ -409,7 +409,8 @@
     along_y = [4 * x + k for k in range(4)]
     second = field_rows(place(along_y, lax.rem(16 - 4 * x, 16)), message, second_blocks, 4)
     second = [second[0]] + [lax.ppermute(second[k], "x", ring(4, k)) for k in (1, 2, 3)]
-    first = field_rows(place(along_x, lax.rem(16 - 4 * y, 16)), message, first_blocks, 4)
+    later = after(message, second[0])
+    first = field_rows(place(along_x, lax.rem(16 - 4 * y, 16)), later, first_blocks, 4)
     first = [first[0]] + [lax.ppermute(first[k], "y", ring(4, k)) for k in (1, 2, 3)]
     field = sum_second_axis(message, first, second)
     field = lax.all_to_all(field, Z, 0, 0)

time: 129 us -> 128 us (level)
    all_to_all x1, waiting for transfers between devices: 6.32 us -> 8.74 us  [on_device(): message = lax.all_to_all(message, ('x', 'y'), 0, 0)]
    ppermute x11, waiting for transfers between devices: 4.67 us -> 2.26 us  [swap(): return lax.ppermute(a, 'core', ring(2, 1))]
  transfers between devices with their start and end apart: 27 -> 27, of which waited for: 12 -> 8; matrix products, arithmetic and copies ran while one was open for 4% -> 4% of each run, Pallas kernels for 20% -> 18%
where the time goes in v8:
time: 128 us
  starting transfers between devices  46.2 us (36%)
  Pallas kernels  27.6 us (22%)
  waiting for transfers between devices  25.1 us (20%)
  blocking collectives  18.5 us (14%)
  local copies, waits for them, and re-layouts  8.66 us (7%)
    all_to_all x1, blocking collectives, on_device(): field = lax.all_to_all(field, Z, 0, 0)  18.5 us
    pallas_call x2, Pallas kernels, pair_sums(): pl.pallas_call(functools.partial(pair_kernel, vectors, first, 1 + len(gre...  15.6 us
    all_to_all x1, waiting for transfers between devices, on_device(): field = lax.all_to_all(field, ('x', 'y'), 0, 0)  8.77 us
    all_to_all x1, waiting for transfers between devices, on_device(): message = lax.all_to_all(message, ('x', 'y'), 0, 0)  8.74 us
    all_to_all x1, starting transfers between devices, on_device(): message = lax.all_to_all(message, ('x', 'y'), 0, 0)  6.51 us
    pallas_call x2, Pallas kernels, field_rows(): pl.pallas_call(functools.partial(field_kernel, vectors), out_shape=[jax.S...  6.44 us
    all_to_all x1, starting transfers between devices, on_device(): field = lax.all_to_all(field, ('x', 'y'), 0, 0)  6.36 us
    ppermute x3, starting transfers between devices, on_device(): lax.ppermute(after(first_pieces[k], beside), 'x', ring(4, k))  5.66 us
  transfers between devices with their start and end apart: 27, of which 8 were waited for; matrix products, arithmetic and copies ran while one was open for 4% of the time, Pallas kernels for 18%

profile of v8, /device:TPU:8, one launch (start us, length us, event | category | flops | bytes accessed | tf_op | source)
XLA Modules:
  0.0 127.6 jit_solution(12686841935887965518)
XLA Ops:
  0.7 2.0 %collective-permute-start.1 = (bf16[4,320,120]{2,1,0:T(8,128)(2,1)}, bf16[4,320,120]{2,1,0:T(8,128)(2,1)}, u32[]{:S(2)}, u32[]{:S(2)}) collective-permute-start(bf16[4,320,120]{2,1,0:T(8,128)(2,1)} %bitcast.36), channel_id=1, source_target_pairs={{0,2},{2,4},{4,6},{6,32},{32,34},{34,36},{36,38},{38,0},{1,3},{3,5... | collective-permute-start | bytes 921608 | tf_op jit(solution)/shard_map/ppermute | solution.py:363
  2.7 3.3 %collective-permute-start.2 = (bf16[4,320,120]{2,1,0:T(8,128)(2,1)}, bf16[4,320,120]{2,1,0:T(8,128)(2,1)}, u32[]{:S(2)}, u32[]{:S(2)}) collective-permute-start(bf16[4,320,120]{2,1,0:T(8,128)(2,1)} %bitcast.37), channel_id=1, source_target_pairs={{0,4},{1,37},{2,6},{3,39},{4,32},{5,1},{6,34},{7,3},{32,36},{33,5}... | collective-permute-start | bytes 921608 | tf_op jit(solution)/shard_map/ppermute | solution.py:366
  7.3 1.6 %slice-done = bf16[15,192,320]{2,1,0:T(8,128)(2,1)S(1)} async-done(((bf16[15,320,320]{2,1,0:T(8,128)(2,1)}), bf16[15,192,320]{2,1,0:T(8,128)(2,1)S(1)}, s32[]{:S(2)}) %slice-start) | async-done | bytes 1843224 | tf_op jit(solution)/shard_map/slice | solution.py:374
  8.9 1.6 %copy.15 = bf16[15,4,48,320]{3,2,0,1:T(8,128)(2,1)} copy(bf16[15,4,48,320]{3,2,1,0:T(8,128)(2,1)S(1)} %bitcast.33) | data formatting | bytes 3686400 | tf_op jit(solution)/shard_map/reshape | solution.py:374
  10.5 2.4 %constant_dynamic-slice_fusion.1 = (bf16[15,32,320]{2,1,0:T(8,128)(2,1)}, bf16[15,32,320]{2,1,0:T(8,128)(2,1)}, bf16[15,32,320]{2,1,0:T(8,128)(2,1)}, bf16[15,32,320]{2,1,0:T(8,128)(2,1)S(1)}) fusion(bf16[15,320,320]{2,1,0:T(8,128)(2,1)} %param.9, s32[]{:T(128)S(6)} %select_n.18, s32[]{:T(128)S(6)} %select_n.17, s32[]{:T(128)S(6)} %select_n.16, s32[]{:T(128)S(6)} %select_n.15), kind=kLoop, calls=%fused_computation.2 | loop fusion | bytes 2457616 | tf_op jit(solution)/shard_map/dynamic_slice | solution.py:371
  13.7 5.8 %pairs.2 = (f32[8,15,128]{2,1,0:T(8,128)}, f32[8,8,128]{2,1,0:T(8,128)}, bf16[15,128,320]{2,1,0:T(8,128)(2,1)}) custom-call(bf16[15,320,120]{2,1,0:T(8,128)(2,1)} %bitcast.43, bf16[4,320,120]{2,1,0:T(8,128)(2,1)} %bitcast.39, bf16[4,320,120]{2,1,0:T(8,128)(2,1)} %copy-done.3), custom_call_target="tpu_custom_call" | custom-call | flops 1 | bytes 1 | tf_op jit(solution)/shard_map/pairs/pallas_call | solution.py:97
  20.5 5.0 %all-to-all-start = ((bf16[4,15,48,320]{3,2,1,0:T(8,128)(2,1)}), bf16[4,15,48,320]{3,2,1,0:T(8,128)(2,1)S(1)}, u32[]{:S(2)}, u32[]{:S(2)}) async-start(bf16[4,15,48,320]{3,2,1,0:T(8,128)(2,1)} %bitcast.32), calls=%async_computation | async-start | bytes 4423680 | tf_op jit(solution)/shard_map/all_to_all | solution.py:383
  25.6 1.8 %collective-permute-start.4 = (bf16[4,320,120]{2,1,0:T(8,128)(2,1)}, bf16[4,320,120]{2,1,0:T(8,128)(2,1)}, u32[]{:S(2)}, u32[]{:S(2)}) collective-permute-start(bf16[4,320,120]{2,1,0:T(8,128)(2,1)} %collective-permute-done.1.refs_1_), channel_id=1, source_target_pairs={{0,1},{1,0},{2,3},{3,2},{4,5},{5,4},{6,7},{7,6},{8,9},{9,8},{10,11... | collective-permute-start | bytes 921608 | tf_op jit(solution)/shard_map/ppermute | solution.py:360
  27.8 1.5 %collective-permute-start.8 = (bf16[15,32,320]{2,1,0:T(8,128)(2,1)}, bf16[15,32,320]{2,1,0:T(8,128)(2,1)S(1)}, u32[]{:S(2)}, u32[]{:S(2)}) collective-permute-start(bf16[15,32,320]{2,1,0:T(8,128)(2,1)} %get-tuple-element.47), channel_id=1, source_target_pairs={{0,64},{64,128},{128,192},{192,0},{1,65},{65,129},{129,193},{193,1... | collective-permute-start | bytes 921608 | tf_op jit(solution)/shard_map/ppermute | solution.py:381
  29.3 2.7 %collective-permute-start.9 = (bf16[15,32,320]{2,1,0:T(8,128)(2,1)}, bf16[15,32,320]{2,1,0:T(8,128)(2,1)S(1)}, u32[]{:S(2)}, u32[]{:S(2)}) collective-permute-start(bf16[15,32,320]{2,1,0:T(8,128)(2,1)} %get-tuple-element.48), channel_id=1, source_target_pairs={{0,128},{64,192},{128,0},{192,64},{1,129},{65,193},{129,1},{193,65... | collective-permute-start | bytes 921608 | tf_op jit(solution)/shard_map/ppermute | solution.py:381
  33.5 4.5 %collective-permute-start.7 = (bf16[48,128]{1,0:T(8,128)(2,1)S(1)}, bf16[48,128]{1,0:T(8,128)(2,1)S(1)}, u32[]{:S(2)}, u32[]{:S(2)}) collective-permute-start(bf16[48,128]{1,0:T(8,128)(2,1)S(1)} %pad.4.near_ref), channel_id=1, source_target_pairs={{0,32},{32,0},{1,33},{33,1},{2,34},{34,2},{3,35},{35,3},{4,36},{36... | collective-permute-start | bytes 36872 | tf_op jit(solution)/shard_map/ppermute | solution.py:393
  38.6 9.8 %pairs.3 = (f32[24,15,128]{2,1,0:T(8,128)}, f32[24,8,128]{2,1,0:T(8,128)}) custom-call(bf16[15,128,320]{2,1,0:T(8,128)(2,1)} %get-tuple-element.39.refs_0_, bf16[4,320,120]{2,1,0:T(8,128)(2,1)} %collective-permute-done.1.refs_1_, bf16[4,320,120]{2,1,0:T(8,128)(2,1)} %collective-permute-done.4.refs_2_, bf16[4,320,120]{2,1,0:T(8,128)(2,1)} %collective-permute-done.2.refs_3_, ...), custom_call_target="tpu_custom_call" | custom-call | flops 1 | bytes 1 | tf_op jit(solution)/shard_map/pairs/pallas_call | solution.py:97
  48.6 2.3 %message.1 = (bf16[16,128]{1,0:T(8,128)(2,1)}, bf16[16,128]{1,0:T(8,128)(2,1)}) custom-call(s32[2]{0:T(128)} %pad_add_fusion.place_ref, f32[8,15,128]{2,1,0:T(8,128)} %get-tuple-element.38.refs_0_, f32[24,15,128]{2,1,0:T(8,128)} %get-tuple-element.43.refs_1_, f32[8,8,128]{2,1,0:T(8,128)} %get-tuple-element.44.refs_2_, ...), custom_call_target="tpu_custom_call" | custom-call | tf_op jit(solution)/shard_map/message/pallas_call | solution.py:153
  54.5 6.5 %all-to-all-start.1 = ((bf16[16,112,128]{2,1,0:T(8,128)(2,1)}), bf16[16,112,128]{2,1,0:T(8,128)(2,1)S(1)}, u32[]{:S(2)}, u32[]{:S(2)}) async-start(bf16[16,112,128]{2,1,0:T(8,128)(2,1)} %copies.1), calls=%async_computation.1 | async-start | bytes 917504 | tf_op jit(solution)/shard_map/all_to_all | solution.py:400
  62.2 8.7 %all-to-all-done.1.message_ref = bf16[16,112,128]{2,1,0:T(8,128)(2,1)S(1)} async-done(((bf16[16,112,128]{2,1,0:T(8,128)(2,1)}), bf16[16,112,128]{2,1,0:T(8,128)(2,1)S(1)}, u32[]{:S(2)}, u32[]{:S(2)}) %all-to-all-start.1) | async-done | bytes 458784 | tf_op jit(solution)/shard_map/all_to_all | solution.py:400
  71.0 3.6 %field_rows.2 = (bf16[1,4,128,128]{3,2,1,0:T(8,128)(2,1)S(1)}, bf16[1,4,128,128]{3,2,1,0:T(8,128)(2,1)S(1)}, bf16[1,4,128,128]{3,2,1,0:T(8,128)(2,1)S(1)}, bf16[1,4,128,128]{3,2,1,0:T(8,128)(2,1)S(1)}) custom-call(s32[5]{0:T(128)S(1)} %stack.63.place_ref, bf16[16,112,128]{2,1,0:T(8,128)(2,1)S(1)} %all-to-all-done.1.message_ref, ...), custom_call_target="tpu_custom_call" | custom-call | flops 1207959552 | bytes 1920000 | tf_op jit(solution)/shard_map/field_rows/pallas_call | solution.py:241
  74.6 2.9 %field_rows.3 = (bf16[1,4,80,128]{3,2,1,0:T(8,128)(2,1)S(1)}, bf16[1,4,80,128]{3,2,1,0:T(8,128)(2,1)S(1)}, bf16[1,4,80,128]{3,2,1,0:T(8,128)(2,1)S(1)}, bf16[1,4,80,128]{3,2,1,0:T(8,128)(2,1)S(1)}) custom-call(s32[5]{0:T(128)S(1)} %stack.57.place_ref, bf16[16,112,128]{2,1,0:T(8,128)(2,1)S(1)} %all-to-all-done.1.message_ref, ...), custom_call_target="tpu_custom_call" | custom-call | flops 805306368 | bytes 1280000 | tf_op jit(solution)/shard_map/field_rows/pallas_call | solution.py:241
  78.3 2.4 %collective-permute-start.21 = (bf16[1,4,128,128]{3,2,1,0:T(8,128)(2,1)S(1)}, bf16[1,4,128,128]{3,2,1,0:T(8,128)(2,1)S(1)}, u32[]{:S(2)}, u32[]{:S(2)}) collective-permute-start(bf16[1,4,128,128]{3,2,1,0:T(8,128)(2,1)S(1)} %get-tuple-element.67), channel_id=1, source_target_pairs={{0,128},{64,192},{128,0},{192,64},{1,129},{65,193},{129,1},{193,65... | collective-permute-start | bytes 393224 | tf_op jit(solution)/shard_map/ppermute | solution.py:411
  80.7 1.5 %collective-permute-start.22 = (bf16[1,4,128,128]{3,2,1,0:T(8,128)(2,1)S(1)}, bf16[1,4,128,128]{3,2,1,0:T(8,128)(2,1)S(1)}, u32[]{:S(2)}, u32[]{:S(2)}) collective-permute-start(bf16[1,4,128,128]{3,2,1,0:T(8,128)(2,1)S(1)} %get-tuple-element.68), channel_id=1, source_target_pairs={{0,192},{64,0},{128,64},{192,128},{1,193},{65,1},{129,65},{193,129... | collective-permute-start | bytes 393224 | tf_op jit(solution)/shard_map/ppermute | solution.py:411
  82.2 2.6 %collective-permute-start.18 = (bf16[1,4,80,128]{3,2,1,0:T(8,128)(2,1)S(1)}, bf16[1,4,80,128]{3,2,1,0:T(8,128)(2,1)S(1)}, u32[]{:S(2)}, u32[]{:S(2)}) collective-permute-start(bf16[1,4,80,128]{3,2,1,0:T(8,128)(2,1)S(1)} %get-tuple-element.64), channel_id=1, source_target_pairs={{0,16},{8,24},{16,0},{24,8},{1,17},{9,25},{17,1},{25,9},{2,18},{10... | collective-permute-start | bytes 245768 | tf_op jit(solution)/shard_map/ppermute | solution.py:414
  85.1 3.0 %collective-permute-done.18.refs_2_ = bf16[1,4,80,128]{3,2,1,0:T(8,128)(2,1)S(1)} collective-permute-done((bf16[1,4,80,128]{3,2,1,0:T(8,128)(2,1)S(1)}, bf16[1,4,80,128]{3,2,1,0:T(8,128)(2,1)S(1)}, u32[]{:S(2)}, u32[]{:S(2)}) %collective-permute-start.18) | collective-permute-done | bytes 81952 | tf_op jit(solution)/shard_map/ppermute | solution.py:414
  89.4 18.5 %all_to_all.20.in_ref = bf16[8,208,128]{2,1,0:T(8,128)(2,1)S(1)} all-to-all(bf16[8,208,128]{2,1,0:T(8,128)(2,1)S(1)} %sum_plane.1), channel_id=1, replica_groups=mesh['x'=4,'zh'=2,'y'=4,'zl'=4,'core'=2] {'zh','zl'}, dimensions={0} | all-to-all | bytes 851968 | tf_op jit(solution)/shard_map/all_to_all | solution.py:416
  108.9 6.4 %all-to-all-start.3 = ((bf16[16,208,128]{2,1,0:T(8,128)(2,1)}), bf16[16,208,128]{2,1,0:T(8,128)(2,1)S(1)}, u32[]{:S(2)}, u32[]{:S(2)}) async-start(bf16[16,208,128]{2,1,0:T(8,128)(2,1)} %get-tuple-element.69), calls=%async_computation.3 | async-start | bytes 1703936 | tf_op jit(solution)/shard_map/all_to_all | solution.py:422
  116.9 8.8 %all-to-all-done.3.in_ref = bf16[16,208,128]{2,1,0:T(8,128)(2,1)S(1)} async-done(((bf16[16,208,128]{2,1,0:T(8,128)(2,1)}), bf16[16,208,128]{2,1,0:T(8,128)(2,1)S(1)}, u32[]{:S(2)}, u32[]{:S(2)}) %all-to-all-start.3) | async-done | bytes 852000 | tf_op jit(solution)/shard_map/all_to_all | solution.py:422
  (66 shorter events, 17.7 us)
Async XLA Ops:
  0.6 12.3 %collective-permute-start = (bf16[4,320,120]{2,1,0:T(8,128)(2,1)}, bf16[4,320,120]{2,1,0:T(8,128)(2,1)S(1)}, u32[]{:S(2)}, u32[]{:S(2)}) collective-permute-start(bf16[4,320,120]{2,1,0:T(8,128)(2,1)} %bitcast.35), channel_id=1, source_target_pairs={{0,1},{1,0},{2,3},{3,2},{4,5},{5,4},{6,7},{7,6},{8,9},{9,8},{10,11... | collective-permute-start | bytes 921608 | tf_op jit(solution)/shard_map/ppermute | solution.py:360
  0.7 18.8 %collective-permute-start.1 = (bf16[4,320,120]{2,1,0:T(8,128)(2,1)}, bf16[4,320,120]{2,1,0:T(8,128)(2,1)}, u32[]{:S(2)}, u32[]{:S(2)}) collective-permute-start(bf16[4,320,120]{2,1,0:T(8,128)(2,1)} %bitcast.36), channel_id=1, source_target_pairs={{0,2},{2,4},{4,6},{6,32},{32,34},{34,36},{36,38},{38,0},{1,3},{3,5... | collective-permute-start | bytes 921608 | tf_op jit(solution)/shard_map/ppermute | solution.py:363
  2.7 17.8 %collective-permute-start.2 = (bf16[4,320,120]{2,1,0:T(8,128)(2,1)}, bf16[4,320,120]{2,1,0:T(8,128)(2,1)}, u32[]{:S(2)}, u32[]{:S(2)}) collective-permute-start(bf16[4,320,120]{2,1,0:T(8,128)(2,1)} %bitcast.37), channel_id=1, source_target_pairs={{0,4},{1,37},{2,6},{3,39},{4,32},{5,1},{6,34},{7,3},{32,36},{33,5}... | collective-permute-start | bytes 921608 | tf_op jit(solution)/shard_map/ppermute | solution.py:366
  6.0 14.5 %collective-permute-start.3 = (bf16[4,320,120]{2,1,0:T(8,128)(2,1)}, bf16[4,320,120]{2,1,0:T(8,128)(2,1)}, u32[]{:S(2)}, u32[]{:S(2)}) collective-permute-start(bf16[4,320,120]{2,1,0:T(8,128)(2,1)} %bitcast.38), channel_id=1, source_target_pairs={{0,38},{2,0},{4,2},{6,4},{32,6},{34,32},{36,34},{38,36},{1,39},{3,... | collective-permute-start | bytes 921608 | tf_op jit(solution)/shard_map/ppermute | solution.py:364
  20.5 31.8 %all-to-all-start = ((bf16[4,15,48,320]{3,2,1,0:T(8,128)(2,1)}), bf16[4,15,48,320]{3,2,1,0:T(8,128)(2,1)S(1)}, u32[]{:S(2)}, u32[]{:S(2)}) async-start(bf16[4,15,48,320]{3,2,1,0:T(8,128)(2,1)} %bitcast.32), calls=%async_computation | async-start | bytes 4423680 | tf_op jit(solution)/shard_map/all_to_all | solution.py:383
  25.6 6.5 %collective-permute-start.4 = (bf16[4,320,120]{2,1,0:T(8,128)(2,1)}, bf16[4,320,120]{2,1,0:T(8,128)(2,1)}, u32[]{:S(2)}, u32[]{:S(2)}) collective-permute-start(bf16[4,320,120]{2,1,0:T(8,128)(2,1)} %collective-permute-done.1.refs_1_), channel_id=1, source_target_pairs={{0,1},{1,0},{2,3},{3,2},{4,5},{5,4},{6,7},{7,6},{8,9},{9,8},{10,11... | collective-permute-start | bytes 921608 | tf_op jit(solution)/shard_map/ppermute | solution.py:360
  27.3 6.2 %collective-permute-start.5 = (bf16[4,320,120]{2,1,0:T(8,128)(2,1)}, bf16[4,320,120]{2,1,0:T(8,128)(2,1)}, u32[]{:S(2)}, u32[]{:S(2)}) collective-permute-start(bf16[4,320,120]{2,1,0:T(8,128)(2,1)} %collective-permute-done.2.refs_3_), channel_id=1, source_target_pairs={{0,1},{1,0},{2,3},{3,2},{4,5},{5,4},{6,7},{7,6},{8,9},{9,8},{10,11... | collective-permute-start | bytes 921608 | tf_op jit(solution)/shard_map/ppermute | solution.py:360
  27.3 11.3 %collective-permute-start.6 = (bf16[4,320,120]{2,1,0:T(8,128)(2,1)}, bf16[4,320,120]{2,1,0:T(8,128)(2,1)}, u32[]{:S(2)}, u32[]{:S(2)}) collective-permute-start(bf16[4,320,120]{2,1,0:T(8,128)(2,1)} %collective-permute-done.3.refs_5_), channel_id=1, source_target_pairs={{0,1},{1,0},{2,3},{3,2},{4,5},{5,4},{6,7},{7,6},{8,9},{9,8},{10,11... | collective-permute-start | bytes 921608 | tf_op jit(solution)/shard_map/ppermute | solution.py:360
  27.8 20.6 %collective-permute-start.8 = (bf16[15,32,320]{2,1,0:T(8,128)(2,1)}, bf16[15,32,320]{2,1,0:T(8,128)(2,1)S(1)}, u32[]{:S(2)}, u32[]{:S(2)}) collective-permute-start(bf16[15,32,320]{2,1,0:T(8,128)(2,1)} %get-tuple-element.47), channel_id=1, source_target_pairs={{0,64},{64,128},{128,192},{192,0},{1,65},{65,129},{129,193},{193,1... | collective-permute-start | bytes 921608 | tf_op jit(solution)/shard_map/ppermute | solution.py:381
  29.3 19.3 %collective-permute-start.9 = (bf16[15,32,320]{2,1,0:T(8,128)(2,1)}, bf16[15,32,320]{2,1,0:T(8,128)(2,1)S(1)}, u32[]{:S(2)}, u32[]{:S(2)}) collective-permute-start(bf16[15,32,320]{2,1,0:T(8,128)(2,1)} %get-tuple-element.48), channel_id=1, source_target_pairs={{0,128},{64,192},{128,0},{192,64},{1,129},{65,193},{129,1},{193,65... | collective-permute-start | bytes 921608 | tf_op jit(solution)/shard_map/ppermute | solution.py:381
  32.1 16.6 %collective-permute-start.10 = (bf16[15,32,320]{2,1,0:T(8,128)(2,1)}, bf16[15,32,320]{2,1,0:T(8,128)(2,1)}, u32[]{:S(2)}, u32[]{:S(2)}) collective-permute-start(bf16[15,32,320]{2,1,0:T(8,128)(2,1)} %get-tuple-element.49), channel_id=1, source_target_pairs={{0,192},{64,0},{128,64},{192,128},{1,193},{65,1},{129,65},{193,129... | collective-permute-start | bytes 921608 | tf_op jit(solution)/shard_map/ppermute | solution.py:381
  33.5 14.9 %collective-permute-start.7 = (bf16[48,128]{1,0:T(8,128)(2,1)S(1)}, bf16[48,128]{1,0:T(8,128)(2,1)S(1)}, u32[]{:S(2)}, u32[]{:S(2)}) collective-permute-start(bf16[48,128]{1,0:T(8,128)(2,1)S(1)} %pad.4.near_ref), channel_id=1, source_target_pairs={{0,32},{32,0},{1,33},{33,1},{2,34},{34,2},{3,35},{35,3},{4,36},{36... | collective-permute-start | bytes 36872 | tf_op jit(solution)/shard_map/ppermute | solution.py:393
  52.4 18.6 %collective-permute-start.12 = (bf16[4,15,48,320]{3,2,1,0:T(8,128)(2,1)S(1)}, bf16[4,15,48,320]{3,2,1,0:T(8,128)(2,1)}, u32[]{:S(2)}, u32[]{:S(2)}) collective-permute-start(bf16[4,15,48,320]{3,2,1,0:T(8,128)(2,1)S(1)} %all-to-all-done.refs_0_), channel_id=1, source_target_pairs={{0,1},{1,0},{2,3},{3,2},{4,5},{5,4},{6,7},{7,6},{8,9},{9,8},{10,11... | collective-permute-start | bytes 5529608 | tf_op jit(solution)/shard_map/ppermute | solution.py:360
  54.5 16.4 %all-to-all-start.1 = ((bf16[16,112,128]{2,1,0:T(8,128)(2,1)}), bf16[16,112,128]{2,1,0:T(8,128)(2,1)S(1)}, u32[]{:S(2)}, u32[]{:S(2)}) async-start(bf16[16,112,128]{2,1,0:T(8,128)(2,1)} %copies.1), calls=%async_computation.1 | async-start | bytes 917504 | tf_op jit(solution)/shard_map/all_to_all | solution.py:400
  61.0 13.5 %collective-permute-start.13 = (bf16[15,32,320]{2,1,0:T(8,128)(2,1)S(1)}, bf16[15,32,320]{2,1,0:T(8,128)(2,1)}, u32[]{:S(2)}, u32[]{:S(2)}) collective-permute-start(bf16[15,32,320]{2,1,0:T(8,128)(2,1)S(1)} %get-tuple-element.58.refs_0_), channel_id=1, source_target_pairs={{0,1},{1,0},{2,3},{3,2},{4,5},{5,4},{6,7},{7,6},{8,9},{9,8},{10,11... | collective-permute-start | bytes 921608 | tf_op jit(solution)/shard_map/ppermute | solution.py:360
  61.0 13.5 %collective-permute-start.14 = (bf16[15,32,320]{2,1,0:T(8,128)(2,1)S(1)}, bf16[15,32,320]{2,1,0:T(8,128)(2,1)}, u32[]{:S(2)}, u32[]{:S(2)}) collective-permute-start(bf16[15,32,320]{2,1,0:T(8,128)(2,1)S(1)} %collective-permute-done.8.refs_1_), channel_id=1, source_target_pairs={{0,1},{1,0},{2,3},{3,2},{4,5},{5,4},{6,7},{7,6},{8,9},{9,8},{10,11... | collective-permute-start | bytes 921608 | tf_op jit(solution)/shard_map/ppermute | solution.py:360
  61.5 13.0 %collective-permute-start.15 = (bf16[15,32,320]{2,1,0:T(8,128)(2,1)}, bf16[15,32,320]{2,1,0:T(8,128)(2,1)}, u32[]{:S(2)}, u32[]{:S(2)}) collective-permute-start(bf16[15,32,320]{2,1,0:T(8,128)(2,1)} %copy-done), channel_id=1, source_target_pairs={{0,1},{1,0},{2,3},{3,2},{4,5},{5,4},{6,7},{7,6},{8,9},{9,8},{10,11... | collective-permute-start | bytes 921608 | tf_op jit(solution)/shard_map/ppermute | solution.py:360
  61.6 12.9 %collective-permute-start.16 = (bf16[15,32,320]{2,1,0:T(8,128)(2,1)}, bf16[15,32,320]{2,1,0:T(8,128)(2,1)}, u32[]{:S(2)}, u32[]{:S(2)}) collective-permute-start(bf16[15,32,320]{2,1,0:T(8,128)(2,1)} %collective-permute-done.10.refs_3_), channel_id=1, source_target_pairs={{0,1},{1,0},{2,3},{3,2},{4,5},{5,4},{6,7},{7,6},{8,9},{9,8},{10,11... | collective-permute-start | bytes 921608 | tf_op jit(solution)/shard_map/ppermute | solution.py:360
  77.5 7.3 %collective-permute-start.17 = (bf16[1,4,80,128]{3,2,1,0:T(8,128)(2,1)S(1)}, bf16[1,4,80,128]{3,2,1,0:T(8,128)(2,1)S(1)}, u32[]{:S(2)}, u32[]{:S(2)}) collective-permute-start(bf16[1,4,80,128]{3,2,1,0:T(8,128)(2,1)S(1)} %get-tuple-element.63), channel_id=1, source_target_pairs={{0,8},{8,16},{16,24},{24,0},{1,9},{9,17},{17,25},{25,1},{2,10},{10... | collective-permute-start | bytes 245768 | tf_op jit(solution)/shard_map/ppermute | solution.py:414
  78.1 11.1 %collective-permute-start.20 = (bf16[1,4,128,128]{3,2,1,0:T(8,128)(2,1)S(1)}, bf16[1,4,128,128]{3,2,1,0:T(8,128)(2,1)S(1)}, u32[]{:S(2)}, u32[]{:S(2)}) collective-permute-start(bf16[1,4,128,128]{3,2,1,0:T(8,128)(2,1)S(1)} %get-tuple-element.66), channel_id=1, source_target_pairs={{0,64},{64,128},{128,192},{192,0},{1,65},{65,129},{129,193},{193,1... | collective-permute-start | bytes 393224 | tf_op jit(solution)/shard_map/ppermute | solution.py:411
  78.3 10.9 %collective-permute-start.21 = (bf16[1,4,128,128]{3,2,1,0:T(8,128)(2,1)S(1)}, bf16[1,4,128,128]{3,2,1,0:T(8,128)(2,1)S(1)}, u32[]{:S(2)}, u32[]{:S(2)}) collective-permute-start(bf16[1,4,128,128]{3,2,1,0:T(8,128)(2,1)S(1)} %get-tuple-element.67), channel_id=1, source_target_pairs={{0,128},{64,192},{128,0},{192,64},{1,129},{65,193},{129,1},{193,65... | collective-permute-start | bytes 393224 | tf_op jit(solution)/shard_map/ppermute | solution.py:411
  80.7 8.5 %collective-permute-start.22 = (bf16[1,4,128,128]{3,2,1,0:T(8,128)(2,1)S(1)}, bf16[1,4,128,128]{3,2,1,0:T(8,128)(2,1)S(1)}, u32[]{:S(2)}, u32[]{:S(2)}) collective-permute-start(bf16[1,4,128,128]{3,2,1,0:T(8,128)(2,1)S(1)} %get-tuple-element.68), channel_id=1, source_target_pairs={{0,192},{64,0},{128,64},{192,128},{1,193},{65,1},{129,65},{193,129... | collective-permute-start | bytes 393224 | tf_op jit(solution)/shard_map/ppermute | solution.py:411
  82.2 5.9 %collective-permute-start.18 = (bf16[1,4,80,128]{3,2,1,0:T(8,128)(2,1)S(1)}, bf16[1,4,80,128]{3,2,1,0:T(8,128)(2,1)S(1)}, u32[]{:S(2)}, u32[]{:S(2)}) collective-permute-start(bf16[1,4,80,128]{3,2,1,0:T(8,128)(2,1)S(1)} %get-tuple-element.64), channel_id=1, source_target_pairs={{0,16},{8,24},{16,0},{24,8},{1,17},{9,25},{17,1},{25,9},{2,18},{10... | collective-permute-start | bytes 245768 | tf_op jit(solution)/shard_map/ppermute | solution.py:414
  108.9 16.8 %all-to-all-start.3 = ((bf16[16,208,128]{2,1,0:T(8,128)(2,1)}), bf16[16,208,128]{2,1,0:T(8,128)(2,1)S(1)}, u32[]{:S(2)}, u32[]{:S(2)}) async-start(bf16[16,208,128]{2,1,0:T(8,128)(2,1)} %get-tuple-element.69), calls=%async_computation.3 | async-start | bytes 1703936 | tf_op jit(solution)/shard_map/all_to_all | solution.py:422
  (9 other events, 32.4 us)
